TPU v7x, 32 devices: a whole 2x2x4 slice. The times are simulated.
32 devices in a mesh: dp: 4 (over y, core), expert: 8 (over z, x).
Axes of the slice: x: 2, y: 2, z: 4, core: 2. Of those that a mesh axis runs over, the one named last changes fastest.
Arguments:
- tokens: bfloat16 [4096, 3584], P(('dp', 'expert')), may hold values from -6 to 6
- cotangent: bfloat16 [4096, 3584], P(('dp', 'expert')), may hold values from -1.5 to 1.5
- gates: bfloat16 [4096, 2], P(('dp', 'expert')), may hold values from 0.19921875 to 1
- expert_ids: int32 [4096, 2], P(('dp', 'expert')), may hold values from 0 to 7, all different within a row; in each aligned block of 128 rows (0 to 127, 128 to 255, ...) at most 48 rows name the same one
- gate_w: bfloat16 [8, 3584, 1024], P('expert'), may hold values from -0.09375 to 0.09375
- up_w: bfloat16 [8, 3584, 1024], P('expert'), may hold values from -0.09375 to 0.09375
- down_w: bfloat16 [8, 1024, 3584], P('expert'), may hold values from -0.1875 to 0.1875
Outputs:
- grad_tokens: bfloat16 [4096, 3584], P('dp', 'expert')
- grad_gate_w: bfloat16 [8, 3584, 1024], P('expert', 'dp')
- grad_up_w: bfloat16 [8, 3584, 1024], P('expert', 'dp')
- grad_gates: bfloat16 [4096, 2], P(('dp', 'expert'))
Inputs may be any that keep to these rules, and one draw needn't show every extreme that they name: `expert_ids`: each token names 2 different experts; among the 128 tokens of one device no expert is named more than 48 times, and in every draw some expert is named exactly 48 times by some device's tokens.
All inputs are finite; a program needn't handle non-finite values.
Results may differ from a plain program's by a relative error of at most 0.014.
Values may be sent and summed in bfloat16 or wider, within the bound.
No kernel may reach another device: no remote copies, remote signals or barrier semaphores. Data moves between devices by JAX's collectives and lax.ppermute only.
A program may use at most 192 MiB of HBM per device.

v0:
```python
import jax
import jax.numpy as jnp
from jax import lax
from jax.sharding import PartitionSpec as P


def local(tokens, cotangent, gates, expert_ids, gate_w, up_w, down_w):
    tok_rows, model_width = tokens.shape
    per_token = expert_ids.shape[1]
    groups = lax.axis_size("expert")
    capacity = 3 * tok_rows * per_token // (2 * groups)
    flat_ids = expert_ids.reshape(-1)
    onehot = (flat_ids[:, None] == jnp.arange(groups, dtype=jnp.int32)[None, :]).astype(jnp.int32)
    position = jnp.sum(jnp.cumsum(onehot, axis=0) * onehot, axis=1) - 1
    target = flat_ids * capacity + position
    send_x = (
        jnp.zeros((groups * capacity, model_width), jnp.bfloat16)
        .at[target]
        .set(jnp.repeat(tokens, per_token, axis=0))
    )
    send_dy = (
        jnp.zeros((groups * capacity, model_width), jnp.bfloat16)
        .at[target]
        .set(jnp.repeat(cotangent, per_token, axis=0))
    )
    send_gate = jnp.zeros((groups * capacity,), jnp.bfloat16).at[target].set(gates.reshape(-1))
    recv_x, recv_dy, recv_gate = (
        lax.all_to_all(
            send_x.reshape(groups, capacity, model_width),
            "expert",
            split_axis=0,
            concat_axis=0,
            tiled=True,
        ),
        lax.all_to_all(
            send_dy.reshape(groups, capacity, model_width),
            "expert",
            split_axis=0,
            concat_axis=0,
            tiled=True,
        ),
        lax.all_to_all(
            send_gate.reshape(groups, capacity), "expert", split_axis=0, concat_axis=0, tiled=True
        ),
    )
    token_rows = recv_x.reshape(-1, model_width)
    grad_rows = recv_dy.reshape(-1, model_width)
    row_gates = recv_gate.reshape(-1).astype(jnp.float32)
    gate_mat = gate_w[0]
    up_mat = up_w[0]
    down_mat = down_w[0]
    gate_pre = jnp.dot(token_rows, gate_mat, preferred_element_type=jnp.float32)
    up_pre = jnp.dot(token_rows, up_mat, preferred_element_type=jnp.float32)
    sigmoid_a = jax.nn.sigmoid(gate_pre)
    silu_a = gate_pre * sigmoid_a
    hidden = (silu_a * up_pre).astype(jnp.bfloat16)
    back = lax.dot_general(
        grad_rows, down_mat, (((1,), (1,)), ((), ())), preferred_element_type=jnp.float32
    )
    gate_score = jnp.sum(back * hidden.astype(jnp.float32), axis=1).astype(jnp.bfloat16)
    hidden_grad = back * row_gates[:, None]
    gate_grad = (hidden_grad * up_pre * sigmoid_a * (1.0 + gate_pre * (1.0 - sigmoid_a))).astype(
        jnp.bfloat16
    )
    up_grad = (hidden_grad * silu_a).astype(jnp.bfloat16)
    row_grad = (
        lax.dot_general(
            gate_grad, gate_mat, (((1,), (1,)), ((), ())), preferred_element_type=jnp.float32
        )
        + lax.dot_general(
            up_grad, up_mat, (((1,), (1,)), ((), ())), preferred_element_type=jnp.float32
        )
    ).astype(jnp.bfloat16)
    inverse_dp = 1.0 / lax.axis_size("dp")
    term_gate = lax.dot_general(
        token_rows, gate_grad, (((0,), (0,)), ((), ())), preferred_element_type=jnp.float32
    )
    term_up = lax.dot_general(
        token_rows, up_grad, (((0,), (0,)), ((), ())), preferred_element_type=jnp.float32
    )
    sum_gate, sum_up = (
        lax.psum_scatter(
            term_gate.astype(jnp.bfloat16), "dp", scatter_dimension=0, tiled=True
        ).astype(jnp.float32),
        lax.psum_scatter(
            term_up.astype(jnp.bfloat16), "dp", scatter_dimension=0, tiled=True
        ).astype(jnp.float32),
    )
    grad_gate_w = (sum_gate * inverse_dp).astype(jnp.bfloat16)[None]
    grad_up_w = (sum_up * inverse_dp).astype(jnp.bfloat16)[None]
    grad_buffer = row_grad.reshape(groups, capacity, model_width)
    score_buffer = gate_score.reshape(groups, capacity)
    back_grad, back_score = (
        lax.all_to_all(grad_buffer, "expert", split_axis=0, concat_axis=0, tiled=True),
        lax.all_to_all(score_buffer, "expert", split_axis=0, concat_axis=0, tiled=True),
    )
    picked = back_grad.reshape(-1, model_width)[target]
    summed = jnp.sum(
        picked.reshape(tok_rows, per_token, model_width), axis=1, dtype=jnp.float32
    ).astype(jnp.bfloat16)
    grad_tokens = lax.all_to_all(summed, "expert", split_axis=1, concat_axis=0, tiled=True)
    grad_gates = back_score.reshape(-1)[target].reshape(tok_rows, per_token)
    return (grad_tokens, grad_gate_w, grad_up_w, grad_gates)


def solution(mesh):
    placed = (
        P(("dp", "expert"), None),
        P(("dp", "expert"), None),
        P(("dp", "expert"), None),
        P(("dp", "expert"), None),
        P("expert", None, None),
        P("expert", None, None),
        P("expert", None, None),
    )
    return jax.shard_map(
        local,
        mesh=mesh,
        in_specs=placed,
        out_specs=(
            P("dp", "expert"),
            P("expert", "dp", None),
            P("expert", "dp", None),
            P(("dp", "expert"), None),
        ),
        check_vma=False,
    )
```

profile of v0, /device:TPU:0, one launch (start us, length us, event | category | flops | bytes accessed | tf_op | source)
XLA Modules:
  0.0 333.5 jit_solution(94020843561319607)
XLA Ops:
  7.2 0.7 broadcast_multiply_fusion
  7.8 0.8 copy.23
  8.6 0.1 eq.29
  8.8 0.1 eq.25
  8.9 0.8 copy.25
  9.7 0.1 reshape.169
  10.0 0.1 mul.59
  10.1 0.6 reduce-window.6
  10.7 0.2 slice_reduce_fusion
  11.1 2.2 scatter_custom_fusion.1
  13.2 0.7 all_to_all.43
  13.9 7.3 %all-to-all-start.1 = ((bf16[8,1,48]{2,1,0:T(2,128)(2,1)}), bf16[8,1,48]{2,1,0:T(2,128)(2,1)S(1)}, u32[]{:S(2)}, u32[]{:S(2)}) async-start(bf16[8,1,48]{2,1,0:T(2,128)(2,1)} %all_to_all.43), calls=%async_computation.1 | async-start | bytes 8192 | tf_op jit(solution)/shard_map/all_to_all | solution.py:42
  21.2 2.1 broadcast_in_dim.24
  23.3 1.6 reshape.177
  25.0 6.0 %scatter_custom_fusion.2 = bf16[384,3584]{1,0:T(8,128)(2,1)} fusion(s32[256]{0:T(256)S(1)} %bitcast.60, bf16[256,3584]{1,0:T(8,128)(2,1)} %reshape.177, bf16[]{:T(256)} %constant.8.clone.1), kind=kCustom, calls=%fused_computation.29 | custom fusion | bytes 2753024 | tf_op jit(solution)/shard_map/scatter | solution.py:19
  30.9 6.7 %all-to-all-start.2 = ((bf16[8,48,3584]{2,1,0:T(8,128)(2,1)}), bf16[8,48,3584]{2,1,0:T(8,128)(2,1)}, u32[]{:S(2)}, u32[]{:S(2)}) async-start(bf16[8,48,3584]{2,1,0:T(8,128)(2,1)} %bitcast.7), calls=%async_computation.2 | async-start | bytes 5505024 | tf_op jit(solution)/shard_map/all_to_all | solution.py:28
  37.6 0.9 broadcast_in_dim.10
  38.6 1.6 reshape.161
  40.2 6.0 %scatter_custom_fusion = bf16[384,3584]{1,0:T(8,128)(2,1)} fusion(s32[256]{0:T(256)S(1)} %bitcast.61, bf16[256,3584]{1,0:T(8,128)(2,1)} %reshape.161, bf16[]{:T(256)} %constant.8.clone.1), kind=kCustom, calls=%fused_computation.31 | custom fusion | bytes 2753024 | tf_op jit(solution)/shard_map/scatter | solution.py:24
  46.2 53.2 %all-to-all-done.2 = bf16[8,48,3584]{2,1,0:T(8,128)(2,1)} async-done(((bf16[8,48,3584]{2,1,0:T(8,128)(2,1)}), bf16[8,48,3584]{2,1,0:T(8,128)(2,1)}, u32[]{:S(2)}, u32[]{:S(2)}) %all-to-all-start.2) | async-done | bytes 2752544 | tf_op jit(solution)/shard_map/all_to_all | solution.py:28
  99.4 3.6 %all-to-all-start = ((bf16[8,48,3584]{2,1,0:T(8,128)(2,1)}), bf16[8,48,3584]{2,1,0:T(8,128)(2,1)S(1)}, u32[]{:S(2)}, u32[]{:S(2)}) async-start(bf16[8,48,3584]{2,1,0:T(8,128)(2,1)} %bitcast.4), calls=%async_computation | async-start | bytes 5505024 | tf_op jit(solution)/shard_map/all_to_all | solution.py:35
  103.0 0.2 reduce-scatter.5.cloned.1.call-start
  103.3 8.1 %fusion.2 = f32[384,1024]{1,0:T(8,128)} fusion(bf16[384,3584]{1,0:T(8,128)(2,1)} %bitcast.8, bf16[1,3584,1024]{2,1,0:T(8,128)(2,1)} %param.11), kind=kOutput, calls=%fused_computation.9 | convolution fusion | flops 2818572288 | bytes 11665408 | tf_op jit(solution)/shard_map/dot_general | solution.py:52
  111.4 8.1 %fusion.6 = f32[384,1024]{1,0:T(8,128)} fusion(bf16[384,3584]{1,0:T(8,128)(2,1)} %bitcast.8, bf16[1,3584,1024]{2,1,0:T(8,128)(2,1)} %param.12), kind=kOutput, calls=%fused_computation.13 | convolution fusion | flops 2818572288 | bytes 11665408 | tf_op jit(solution)/shard_map/dot_general | solution.py:53
  119.5 46.0 %all-to-all-done = bf16[8,48,3584]{2,1,0:T(8,128)(2,1)S(1)} async-done(((bf16[8,48,3584]{2,1,0:T(8,128)(2,1)}), bf16[8,48,3584]{2,1,0:T(8,128)(2,1)S(1)}, u32[]{:S(2)}, u32[]{:S(2)}) %all-to-all-start) | async-done | bytes 2752544 | tf_op jit(solution)/shard_map/all_to_all | solution.py:35
  165.5 8.4 %multiply_reduce_fusion = (bf16[384]{0:T(512)(128)(2,1)S(1)}, bf16[384,1024]{1,0:T(8,128)(2,1)}, bf16[384,1024]{1,0:T(8,128)(2,1)S(1)}) fusion(f32[384,1024]{1,0:T(8,128)} %fusion.6, f32[384,1024]{1,0:T(8,128)} %fusion.2, f32[384]{0:T(512)S(1)} %reshape.140, bf16[384,3584]{1,0:T(8,128)(2,1)S(1)} %bitcast.57, bf16[1,1024,3584]{2,1,0:T(8,128)(2,1)} %param.13), kind=kOutput, calls=%fused_computation.23 | convolution fusion | flops 2826042880 | bytes 14813440 | tf_op jit(solution)/shard_map/dot_general | solution.py:57
  173.9 7.9 %convolution_convert_fusion = bf16[3584,1024]{1,0:T(8,128)(2,1)} fusion(bf16[384,3584]{1,0:T(8,128)(2,1)} %bitcast.8, bf16[384,1024]{1,0:T(8,128)(2,1)S(1)} %get-tuple-element.18), kind=kOutput, calls=%fused_computation.5 | convolution fusion | flops 2822242304 | bytes 10878976 | tf_op jit(solution)/shard_map/dot_general | solution.py:78
  181.8 0.3 reduce-scatter.3.cloned.1.call-start
  182.1 0.8 copy-done.1
  182.9 8.2 %convolution_convert_fusion.1 = bf16[3584,1024]{1,0:T(8,128)(2,1)} fusion(bf16[384,3584]{1,0:T(8,128)(2,1)} %bitcast.8, bf16[384,1024]{1,0:T(8,128)(2,1)S(1)} %copy-done.1), kind=kOutput, calls=%fused_computation.6 | convolution fusion | flops 2822242304 | bytes 10878976 | tf_op jit(solution)/shard_map/dot_general | solution.py:75
  191.2 6.0 %fusion = f32[384,3584]{1,0:T(8,128)S(1)} fusion(bf16[384,1024]{1,0:T(8,128)(2,1)S(1)} %copy-done.1, bf16[1,3584,1024]{2,1,0:T(8,128)(2,1)} %param.11), kind=kOutput, calls=%fused_computation.7 | convolution fusion | flops 2818572288 | bytes 13631488 | tf_op jit(solution)/shard_map/dot_general | solution.py:67
  197.2 9.4 %fusion.13 = bf16[384,3584]{1,0:T(8,128)(2,1)} fusion(f32[384,3584]{1,0:T(8,128)S(1)} %fusion, bf16[384,1024]{1,0:T(8,128)(2,1)S(1)} %get-tuple-element.18, bf16[1,3584,1024]{2,1,0:T(8,128)(2,1)} %param.12), kind=kOutput, calls=%fused_computation.18 | convolution fusion | flops 2821324800 | bytes 16384000 | tf_op jit(solution)/shard_map/dot_general | solution.py:70
  206.6 4.0 %all-to-all-start.3 = ((bf16[8,48,3584]{2,1,0:T(8,128)(2,1)}), bf16[8,48,3584]{2,1,0:T(8,128)(2,1)S(1)}, u32[]{:S(2)}, u32[]{:S(2)}) async-start(bf16[8,48,3584]{2,1,0:T(8,128)(2,1)} %bitcast.58), calls=%async_computation.3 | async-start | bytes 5505024 | tf_op jit(solution)/shard_map/all_to_all | solution.py:94
  210.6 0.7 convert_element_type.81
  211.3 61.9 %all-to-all-done.3 = bf16[8,48,3584]{2,1,0:T(8,128)(2,1)S(1)} async-done(((bf16[8,48,3584]{2,1,0:T(8,128)(2,1)}), bf16[8,48,3584]{2,1,0:T(8,128)(2,1)S(1)}, u32[]{:S(2)}, u32[]{:S(2)}) %all-to-all-start.3) | async-done | bytes 2752544 | tf_op jit(solution)/shard_map/all_to_all | solution.py:94
  273.2 3.9 %all-to-all-start.5 = ((bf16[8,1,48]{2,1,0:T(2,128)(2,1)}), bf16[8,1,48]{2,1,0:T(2,128)(2,1)S(1)}, u32[]{:S(2)}, u32[]{:S(2)}) async-start(bf16[8,1,48]{2,1,0:T(2,128)(2,1)} %convert_element_type.81), calls=%async_computation.7 | async-start | bytes 8192 | tf_op jit(solution)/shard_map/all_to_all | solution.py:95
  277.1 3.0 gather_fusion
  280.1 3.9 %reshape.137 = bf16[128,2,3584]{2,1,0:T(2,128)(2,1)S(1)} reshape(bf16[256,3584]{1,0:T(8,128)(2,1)} %gather_fusion) | data formatting | bytes 3670016 | tf_op jit(solution)/shard_map/reshape | solution.py:99
  284.0 4.9 %reduce_sum.31 = bf16[128,3584]{1,0:T(8,128)(2,1)S(1)} reduce(bf16[128,2,3584]{2,1,0:T(2,128)(2,1)S(1)} %reshape.137, bf16[]{:T(256)} %constant.8.clone.1), dimensions={1}, to_apply=%region_6.7 | reduce | flops 458752 | bytes 2752514 | tf_op jit(solution)/shard_map/reduce_sum | solution.py:98
  288.9 1.3 copy.27
  290.2 6.0 %all-to-all-start.4 = ((bf16[128,8,448]{0,2,1:T(8,128)(2,1)}), bf16[128,8,448]{0,2,1:T(8,128)(2,1)S(1)}, u32[]{:S(2)}, u32[]{:S(2)}) async-start(bf16[128,8,448]{0,2,1:T(8,128)(2,1)} %bitcast.13), calls=%async_computation.4 | async-start | bytes 1835008 | tf_op jit(solution)/shard_map/all_to_all | solution.py:101
  296.3 1.9 gather_fusion.1
  298.3 0.2 reshape.139
  298.4 0.6 copy.30
  299.0 20.0 %all-to-all-done.4 = bf16[128,8,448]{0,2,1:T(8,128)(2,1)S(1)} async-done(((bf16[128,8,448]{0,2,1:T(8,128)(2,1)}), bf16[128,8,448]{0,2,1:T(8,128)(2,1)S(1)}, u32[]{:S(2)}, u32[]{:S(2)}) %all-to-all-start.4) | async-done | bytes 917536 | tf_op jit(solution)/shard_map/all_to_all | solution.py:101
  319.0 1.1 copy_bitcast_fusion
  320.1 3.2 fusion.17
  323.2 3.2 fusion.16
  (21 shorter events, 0.5 us)
Async XLA Ops:
  13.9 17.0 %all-to-all-start.1 = ((bf16[8,1,48]{2,1,0:T(2,128)(2,1)}), bf16[8,1,48]{2,1,0:T(2,128)(2,1)S(1)}, u32[]{:S(2)}, u32[]{:S(2)}) async-start(bf16[8,1,48]{2,1,0:T(2,128)(2,1)} %all_to_all.43), calls=%async_computation.1 | async-start | bytes 8192 | tf_op jit(solution)/shard_map/all_to_all | solution.py:42
  30.9 6.7 %copy-start = (bf16[128,3584]{1,0:T(8,128)(2,1)S(1)}, bf16[128,3584]{1,0:T(8,128)(2,1)}, u32[]{:S(2)}) copy-start(bf16[128,3584]{1,0:T(8,128)(2,1)} %param.8) | copy-start | bytes 2752516
  30.9 68.5 %all-to-all-start.2 = ((bf16[8,48,3584]{2,1,0:T(8,128)(2,1)}), bf16[8,48,3584]{2,1,0:T(8,128)(2,1)}, u32[]{:S(2)}, u32[]{:S(2)}) async-start(bf16[8,48,3584]{2,1,0:T(8,128)(2,1)} %bitcast.7), calls=%async_computation.2 | async-start | bytes 5505024 | tf_op jit(solution)/shard_map/all_to_all | solution.py:28
  99.4 66.1 %all-to-all-start = ((bf16[8,48,3584]{2,1,0:T(8,128)(2,1)}), bf16[8,48,3584]{2,1,0:T(8,128)(2,1)S(1)}, u32[]{:S(2)}, u32[]{:S(2)}) async-start(bf16[8,48,3584]{2,1,0:T(8,128)(2,1)} %bitcast.4), calls=%async_computation | async-start | bytes 5505024 | tf_op jit(solution)/shard_map/all_to_all | solution.py:35
  103.0 217.0 %reduce-scatter.5.cloned.1.call-start = ((), (), s32[]{:S(2)}) async-start(), calls=%async_computation.9 | async-start | bytes 9175040 | tf_op jit(solution)/shard_map/reduce_scatter | solution.py:85
  181.8 1.1 copy-start.1
  181.8 141.4 %reduce-scatter.3.cloned.1.call-start = ((), (), s32[]{:S(2)}) async-start(), calls=%async_computation.8 | async-start | bytes 9175040 | tf_op jit(solution)/shard_map/reduce_scatter | solution.py:82
  206.6 66.6 %all-to-all-start.3 = ((bf16[8,48,3584]{2,1,0:T(8,128)(2,1)}), bf16[8,48,3584]{2,1,0:T(8,128)(2,1)S(1)}, u32[]{:S(2)}, u32[]{:S(2)}) async-start(bf16[8,48,3584]{2,1,0:T(8,128)(2,1)} %bitcast.58), calls=%async_computation.3 | async-start | bytes 5505024 | tf_op jit(solution)/shard_map/all_to_all | solution.py:94
  273.2 17.0 %all-to-all-start.5 = ((bf16[8,1,48]{2,1,0:T(2,128)(2,1)}), bf16[8,1,48]{2,1,0:T(2,128)(2,1)S(1)}, u32[]{:S(2)}, u32[]{:S(2)}) async-start(bf16[8,1,48]{2,1,0:T(2,128)(2,1)} %convert_element_type.81), calls=%async_computation.7 | async-start | bytes 8192 | tf_op jit(solution)/shard_map/all_to_all | solution.py:95
  290.2 28.8 %all-to-all-start.4 = ((bf16[128,8,448]{0,2,1:T(8,128)(2,1)}), bf16[128,8,448]{0,2,1:T(8,128)(2,1)S(1)}, u32[]{:S(2)}, u32[]{:S(2)}) async-start(bf16[128,8,448]{0,2,1:T(8,128)(2,1)} %bitcast.13), calls=%async_computation.4 | async-start | bytes 1835008 | tf_op jit(solution)/shard_map/all_to_all | solution.py:101
Sparse Core Ops, SparseCore 0:
  182.0 64.5 reduce-scatter.4
  249.3 65.3 reduce-scatter.2
where the time goes:
time: 340 us; the launch traced here: 333 us
  waiting for transfers between devices  181 us (53%)
  matrix products  56.1 us (16%)
  local copies, waits for them, and re-layouts  37.1 us (11%)
  starting transfers between devices  32 us (9%)
  between operations  14.4 us (4%)
  other arithmetic  12.7 us (4%)
    all_to_all x1, waiting for transfers between devices, local(): lax.all_to_all(grad_buffer, 'expert', split_axis=0, concat_axis=0, tiled=...  61.9 us
    all_to_all x1, waiting for transfers between devices, local(): lax.all_to_all(send_x.reshape(groups, capacity, model_width), 'expert', s...  53.2 us
    all_to_all x1, waiting for transfers between devices, local(): lax.all_to_all(send_dy.reshape(groups, capacity, model_width), 'expert',...  46 us
    all_to_all x1, waiting for transfers between devices, local(): lax.all_to_all(summed, 'expert', split_axis=1, concat_axis=0, tiled=True)  20 us
    dot_general x1, matrix products, local(): lax.dot_general(up_grad, up_mat, (((1,), (1,)), ((), ())), preferred_elem...  9.39 us
    dot_general x1, matrix products, local(): lax.dot_general(grad_rows, down_mat, (((1,), (1,)), ((), ())), preferred_...  8.43 us
    dot_general x1, matrix products, local(): lax.dot_general(token_rows, gate_grad, (((0,), (0,)), ((), ())), preferre...  8.22 us
    dot_general x1, matrix products, local(): gate_pre = jnp.dot(token_rows, gate_mat, preferred_element_type=jnp.float32)  8.07 us
  transfers between devices with their start and end apart: 8, of which 4 were waited for; matrix products, arithmetic and copies ran while one was open for 24% of the time, Pallas kernels for 0%

commit v1 on v0

v1 whole, which is shorter than its diff:
```python
import functools

import jax
import jax.numpy as jnp
from jax import lax
from jax.experimental import pallas as pl
from jax.experimental.pallas import tpu as pltpu
from jax.sharding import PartitionSpec as P

F32 = jnp.float32
BF16 = jnp.bfloat16
NT = (((1,), (1,)), ((), ()))
TN = (((0,), (0,)), ((), ()))


def params(mib=48):
    return pltpu.CompilerParams(vmem_limit_bytes=mib << 20)


def cost(flops, nbytes):
    return pl.CostEstimate(flops=int(flops), bytes_accessed=int(nbytes), transcendentals=0)


def vmem(count):
    return [pl.BlockSpec(memory_space=pltpu.VMEM)] * count


def smem():
    return pl.BlockSpec(memory_space=pltpu.SMEM)


def prep_kernel(n, cap, me_ref, ids_ref, gates_ref, tok_ref, meta_ref, *out_refs):
    toks = tok_ref.shape[0]
    expert = lax.broadcasted_iota(jnp.int32, (n, toks), 0) ^ me_ref[0]
    first = ids_ref[0:1, :] == expert
    second = ids_ref[1:2, :] == expert
    count = (first | second).astype(F32)
    before = (
        lax.broadcasted_iota(jnp.int32, (toks, toks), 0)
        < lax.broadcasted_iota(jnp.int32, (toks, toks), 1)
    ).astype(F32)
    position = jnp.dot(count.astype(BF16), before.astype(BF16), preferred_element_type=F32)
    code = jnp.where(first | second, position, -1.0)
    gates = gates_ref[...].astype(F32)
    weight = jnp.where(first, gates[0:1, :], 0.0) + jnp.where(second, gates[1:2, :], 0.0)
    meta_ref[...] = jnp.concatenate([code, weight], axis=0).astype(BF16)
    select_rows(n, cap, code, tok_ref, out_refs)


def select_rows(n, cap, code, tok_ref, out_refs):
    toks = tok_ref.shape[0]
    slot = lax.broadcasted_iota(jnp.int32, (cap, toks), 0).astype(F32)
    for j in range(n):
        pick = (slot == code[j : j + 1, :]).astype(F32).astype(BF16)
        out_refs[j][...] = jnp.dot(pick, tok_ref[...], preferred_element_type=F32).astype(BF16)


def select_kernel(n, cap, meta_ref, tok_ref, *out_refs):
    code = meta_ref[...].astype(F32)[0:n, :]
    select_rows(n, cap, code, tok_ref, out_refs)


def forward_kernel(n, cap, *refs):
    x_refs, meta_refs = refs[:n], refs[n : 2 * n]
    gate_ref, up_ref, rows_ref, hidden_ref, pa_ref, pb_ref, w_ref = refs[2 * n :]
    toks = meta_refs[0].shape[1]

    @pl.when(pl.program_id(0) == 0)
    def _():
        slot = lax.broadcasted_iota(jnp.int32, (cap, toks), 0).astype(F32)
        for j in range(n):
            rows_ref[j * cap : (j + 1) * cap, :] = x_refs[j][...]
            meta = meta_refs[j][...].astype(F32)
            picked = jnp.where(slot == meta[j : j + 1, :], meta[n + j : n + j + 1, :], 0.0)
            total = jnp.sum(picked, axis=1, keepdims=True)
            w_ref[j * cap : (j + 1) * cap, :] = jnp.broadcast_to(total, (cap, w_ref.shape[1]))

    a = jnp.dot(rows_ref[...], gate_ref[0], preferred_element_type=F32)
    b = jnp.dot(rows_ref[...], up_ref[0], preferred_element_type=F32)
    w = w_ref[:, 0:1]
    sig = jax.nn.sigmoid(a)
    silu = a * sig
    hidden_ref[...] = (silu * b).astype(BF16)
    pa_ref[...] = w * b * sig * (1.0 + a * (1.0 - sig))
    pb_ref[...] = w * silu


def back_kernel(n, cap, *refs):
    y_refs = refs[:n]
    hidden_ref, pa_ref, pb_ref, down_ref, grads_ref, score_ref, rows_ref, part_ref = refs[n:]
    step = pl.program_id(0)

    @pl.when(step == 0)
    def _():
        for j in range(n):
            rows_ref[j * cap : (j + 1) * cap, :] = y_refs[j][...]
        part_ref[...] = jnp.zeros_like(part_ref)

    back = lax.dot_general(rows_ref[...], down_ref[0], NT, preferred_element_type=F32)
    grads_ref[0] = (back * pa_ref[...]).astype(BF16)
    grads_ref[1] = (back * pb_ref[...]).astype(BF16)
    prod = back * hidden_ref[...].astype(F32)
    part = part_ref[...]
    for c in range(prod.shape[1] // 128):
        part = part + prod[:, c * 128 : (c + 1) * 128]
    part_ref[...] = part

    @pl.when(step == pl.num_programs(0) - 1)
    def _():
        total = jnp.sum(jnp.transpose(part_ref[...]), axis=0, keepdims=True)
        shape = score_ref.shape
        top = lax.broadcasted_iota(jnp.int32, shape, 0) == 0
        score_ref[...] = jnp.where(top, jnp.broadcast_to(total, shape), 0.0).astype(BF16)


def rowgrad_kernel(count, feats, me_ref, grads_ref, score_ref, gate_ref, up_ref, *out_refs):
    del me_ref
    val = lax.dot_general(gate_ref[0], grads_ref[0], NT, preferred_element_type=F32)
    val = val + lax.dot_general(up_ref[0], grads_ref[1], NT, preferred_element_type=F32)
    val = val.astype(BF16)
    for i in range(count):

        @pl.when(pl.program_id(0) == i)
        def _():
            out_refs[i][0:feats, :] = val
            out_refs[i][feats:, :] = score_ref[...]


def combine_kernel(n, cap, feats, me_ref, ids_ref, *refs):
    meta_refs, got_refs = refs[:n], refs[n : 2 * n]
    out_ref, gates_ref = refs[2 * n :]
    me = me_ref[0]
    rows = n * cap
    toks = meta_refs[0].shape[1]
    metas = [meta_refs[j][...].astype(F32) for j in range(n)]
    total = jnp.zeros((feats, n * toks), F32)
    gg0 = jnp.zeros((16, toks), F32)
    gg1 = jnp.zeros((16, toks), F32)
    row = lax.broadcasted_iota(jnp.int32, (rows, n * toks), 0).astype(F32)
    for k in range(n):
        wanted = []
        for j in range(n):
            code = metas[j][j ^ k : (j ^ k) + 1, :]
            wanted.append(jnp.where(code >= 0.0, code + float((j ^ k) * cap), -1.0))
        wanted = jnp.concatenate(wanted, axis=1)
        pick = (row == wanted).astype(F32).astype(BF16)
        total = total + jnp.dot(got_refs[k][0:feats, :], pick, preferred_element_type=F32)
        score = jnp.dot(got_refs[k][feats:, :], pick[:, 0:toks], preferred_element_type=F32)
        gg0 = gg0 + jnp.where(ids_ref[0:1, :] == (me ^ k), score, 0.0)
        gg1 = gg1 + jnp.where(ids_ref[1:2, :] == (me ^ k), score, 0.0)
    for j in range(n):
        place = pl.multiple_of((me ^ j) * toks, toks)
        out_ref[:, pl.ds(place, toks)] = total[:, j * toks : (j + 1) * toks].astype(BF16)
    gates_ref[...] = jnp.concatenate([gg0[0:1], gg1[0:1]], axis=0).astype(BF16)


def weights_kernel(ndp, *refs):
    x_refs, g_refs = refs[:ndp], refs[ndp : 2 * ndp]
    gate_ref, up_ref = refs[2 * ndp :]
    for half, out in ((0, gate_ref), (1, up_ref)):
        total = None
        for q in range(ndp):
            term = lax.dot_general(x_refs[q][...], g_refs[q][half], TN, preferred_element_type=F32)
            total = term if total is None else total + term
        out[0] = (total * (1.0 / ndp)).astype(BF16)


def local(tokens, cotangent, gates, expert_ids, gate_w, up_w, down_w):
    toks, d = tokens.shape
    top = expert_ids.shape[1]
    h = gate_w.shape[2]
    n = lax.axis_size("expert")
    ndp = lax.axis_size("dp")
    cap = -(-(3 * toks * top // (2 * n)) // 16) * 16
    rows = n * cap
    feats = d // n
    block = d // ndp
    me = lax.axis_index("expert").astype(jnp.int32)
    my_dp = lax.axis_index("dp")
    me_arr = me.reshape(1)
    ids_t = expert_ids.T
    gates_t = gates.T

    def swap(v, k):
        return lax.ppermute(v, "expert", [(i, i ^ k) for i in range(n)])

    def swap_dp(v, q):
        return lax.ppermute(v, "dp", [(i, i ^ q) for i in range(ndp)])

    block_shape = jax.ShapeDtypeStruct((cap, d), BF16)
    meta, *send_x = pl.pallas_call(
        functools.partial(prep_kernel, n, cap),
        out_shape=[jax.ShapeDtypeStruct((2 * n, toks), BF16)] + [block_shape] * n,
        in_specs=[smem()] + vmem(3),
        out_specs=vmem(n + 1),
        compiler_params=params(),
        cost_estimate=cost(2 * rows * toks * d, 2 * (rows + toks) * d),
        name="prep",
    )(me_arr, ids_t, gates_t, tokens)
    metas = [meta] + [swap(meta, k) for k in range(1, n)]
    got_x = [send_x[0]] + [swap(send_x[k], k) for k in range(1, n)]

    send_y = pl.pallas_call(
        functools.partial(select_kernel, n, cap),
        out_shape=[block_shape] * n,
        in_specs=vmem(2),
        out_specs=vmem(n),
        compiler_params=params(),
        cost_estimate=cost(2 * rows * toks * d, 2 * (rows + toks) * d),
        name="select",
    )(meta, cotangent)
    got_y = [send_y[0]] + [swap(send_y[k], k) for k in range(1, n)]

    tile = 256
    steps = h // tile
    whole = lambda shape: pl.BlockSpec(shape, lambda i: (0,) * len(shape))
    x_rows, hidden, pa, pb = pl.pallas_call(
        functools.partial(forward_kernel, n, cap),
        grid=(steps,),
        out_shape=[
            jax.ShapeDtypeStruct((rows, d), BF16),
            jax.ShapeDtypeStruct((rows, h), BF16),
            jax.ShapeDtypeStruct((rows, h), F32),
            jax.ShapeDtypeStruct((rows, h), F32),
        ],
        in_specs=[whole((cap, d))] * n
        + [whole((2 * n, toks))] * n
        + [pl.BlockSpec((1, d, tile), lambda i: (0, 0, i))] * 2,
        out_specs=[whole((rows, d))] + [pl.BlockSpec((rows, tile), lambda i: (0, i))] * 3,
        scratch_shapes=[pltpu.VMEM((rows, 128), F32)],
        compiler_params=params(),
        cost_estimate=cost(4 * rows * d * h, 4 * d * h + 4 * rows * d + 10 * rows * h),
        name="forward",
    )(*got_x, *metas, gate_w, up_w)

    def block_of(q):
        return lax.dynamic_slice_in_dim(x_rows, (my_dp ^ q) * block, block, axis=1)

    x_parts = [block_of(0)] + [swap_dp(block_of(q), q) for q in range(1, ndp)]

    grads, score = pl.pallas_call(
        functools.partial(back_kernel, n, cap),
        grid=(steps,),
        out_shape=[
            jax.ShapeDtypeStruct((2, rows, h), BF16),
            jax.ShapeDtypeStruct((16, rows), BF16),
        ],
        in_specs=[whole((cap, d))] * n
        + [pl.BlockSpec((rows, tile), lambda i: (0, i))] * 3
        + [pl.BlockSpec((1, tile, d), lambda i: (0, i, 0))],
        out_specs=[pl.BlockSpec((2, rows, tile), lambda i: (0, 0, i)), whole((16, rows))],
        scratch_shapes=[pltpu.VMEM((rows, d), BF16), pltpu.VMEM((rows, 128), F32)],
        compiler_params=params(),
        cost_estimate=cost(2 * rows * d * h, 2 * d * h + 2 * rows * d + 14 * rows * h),
        name="back",
    )(*got_y, hidden, pa, pb, down_w)

    def rowgrads(parts):
        first, count = parts[0], len(parts)
        spec = pl.BlockSpec((1, feats, h), lambda i, me_ref: (0, me_ref[0] ^ (first - i), 0))
        fixed = lambda shape: pl.BlockSpec(shape, lambda i, me_ref: (0,) * len(shape))
        return pl.pallas_call(
            functools.partial(rowgrad_kernel, count, feats),
            grid_spec=pltpu.PrefetchScalarGridSpec(
                num_scalar_prefetch=1,
                grid=(count,),
                in_specs=[fixed((2, rows, h)), fixed((16, rows)), spec, spec],
                out_specs=[fixed((feats + 16, rows))] * count,
            ),
            out_shape=[jax.ShapeDtypeStruct((feats + 16, rows), BF16)] * count,
            compiler_params=params(),
            cost_estimate=cost(4 * count * feats * rows * h, 4 * count * feats * h + 4 * rows * h),
            name="rowgrad",
        )(me_arr, grads, score, gate_w, up_w)

    order = list(range(n - 1, -1, -1))
    half = n // 2
    back_rows = [None] * n
    for parts in (order[: half // 2], order[half // 2 : half], order[half:]):
        for k, sent in zip(parts, rowgrads(parts)):
            back_rows[k] = swap(sent, k) if k else sent

    g_parts = [grads] + [None] * (ndp - 1)
    for q in range(0, ndp, 2):
        if q:
            g_parts[q] = swap_dp(grads, q)
        g_parts[q + 1] = swap_dp(g_parts[q], 1)

    tile_w = 256
    out_spec = pl.BlockSpec((1, block, tile_w), lambda i: (0, 0, i))
    grad_gate_w, grad_up_w = pl.pallas_call(
        functools.partial(weights_kernel, ndp),
        grid=(h // tile_w,),
        out_shape=[jax.ShapeDtypeStruct((1, block, h), BF16)] * 2,
        in_specs=[whole((rows, block))] * ndp
        + [pl.BlockSpec((2, rows, tile_w), lambda i: (0, 0, i))] * ndp,
        out_specs=[out_spec, out_spec],
        compiler_params=params(),
        cost_estimate=cost(
            4 * ndp * rows * block * h, 2 * ndp * rows * (block + 2 * h) + 4 * block * h
        ),
        name="weights",
    )(*x_parts, *g_parts)

    summed, gg = pl.pallas_call(
        functools.partial(combine_kernel, n, cap, feats),
        out_shape=[
            jax.ShapeDtypeStruct((feats, n * toks), BF16),
            jax.ShapeDtypeStruct((2, toks), BF16),
        ],
        in_specs=[smem()] + vmem(1 + 2 * n),
        out_specs=vmem(2),
        compiler_params=params(),
        cost_estimate=cost(2 * n * feats * rows * n * toks, 2 * feats * n * (rows + toks)),
        name="combine",
    )(me_arr, ids_t, *metas, *back_rows)
    return summed.T, grad_gate_w, grad_up_w, gg.T


def solution(mesh):
    placed = (
        P(("dp", "expert"), None),
        P(("dp", "expert"), None),
        P(("dp", "expert"), None),
        P(("dp", "expert"), None),
        P("expert", None, None),
        P("expert", None, None),
        P("expert", None, None),
    )
    return jax.shard_map(
        local,
        mesh=mesh,
        in_specs=placed,
        out_specs=(
            P("dp", "expert"),
            P("expert", "dp", None),
            P("expert", "dp", None),
            P(("dp", "expert"), None),
        ),
        check_vma=False,
    )
```

time: 340 us -> 304 us (0.89); the launches traced: 333 us -> 303 us
  matrix products: 56.1 us -> 0 us
  Pallas kernels: 0 us -> 53 us
  local copies, waits for them, and re-layouts: 37.1 us -> 9.95 us
  starting transfers between devices: 32 us -> 51 us
  between operations: 14.4 us -> 0.79 us
  other arithmetic: 12.7 us -> 0 us
  waiting for transfers between devices: 181 us -> 189 us
    ppermute x0 -> x34, waiting for transfers between devices: none -> 189 us  [the longest x28 144 us: swap(): return lax.ppermute(v, 'expert', [(i, i ^ k) for i in range(n)])]
    all_to_all x6 -> x0, waiting for transfers between devices: 181 us -> none  [the longest x1 61.9 us: local(): lax.all_to_all(grad_buffer, 'expert', split_axis=0, concat_axis=0, tiled=...]
    dot_general x7 -> x0, matrix products: 56.1 us -> none  [the longest x1 9.39 us: local(): lax.dot_general(up_grad, up_mat, (((1,), (1,)), ((), ())), preferred_elem...]
    pallas_call x0 -> x9, Pallas kernels: none -> 53 us  [the longest x3 15.2 us: rowgrads(): pl.pallas_call(functools.partial(rowgrad_kernel, count, feats), grid_spec...]
    ppermute x0 -> x34, starting transfers between devices: none -> 51 us  [the longest x28 46.7 us: swap(): return lax.ppermute(v, 'expert', [(i, i ^ k) for i in range(n)])]
    all_to_all x6 -> x0, starting transfers between devices: 31.6 us -> none  [the longest x1 7.25 us: local(): lax.all_to_all(send_gate.reshape(groups, capacity), 'expert', split_axis=...]
    scatter x3 -> x0, local copies, waits for them, and re-layouts: 14.1 us -> none  [the longest x1 5.96 us: local(): send_dy = jnp.zeros((groups * capacity, model_width), jnp.bfloat16).at[ta...]
    reshape x6 -> x0, local copies, waits for them, and re-layouts: 7.56 us -> none  [the longest x1 3.88 us: local(): picked.reshape(tok_rows, per_token, model_width)]
  transfers between devices with their start and end apart: 8 -> 34, of which waited for: 4 -> 18; matrix products, arithmetic and copies ran while one was open for 24% -> 1% of each run, Pallas kernels for 0% -> 11%
where the time goes in v1:
time: 304 us; the launch traced here: 303 us
  waiting for transfers between devices  189 us (62%)
  Pallas kernels  53 us (17%)
  starting transfers between devices  51 us (17%)
  local copies, waits for them, and re-layouts  9.95 us (3%)
    ppermute x28, waiting for transfers between devices, swap(): return lax.ppermute(v, 'expert', [(i, i ^ k) for i in range(n)])  144 us
    ppermute x28, starting transfers between devices, swap(): return lax.ppermute(v, 'expert', [(i, i ^ k) for i in range(n)])  46.7 us
    ppermute x6, waiting for transfers between devices, swap_dp(): return lax.ppermute(v, 'dp', [(i, i ^ q) for i in range(ndp)])  45.1 us
    pallas_call x3, Pallas kernels, rowgrads(): pl.pallas_call(functools.partial(rowgrad_kernel, count, feats), grid_spec...  15.2 us
    pallas_call x1, Pallas kernels, local(): pl.pallas_call(functools.partial(forward_kernel, n, cap), grid=(steps,),...  11 us
    pallas_call x1, Pallas kernels, local(): pl.pallas_call(functools.partial(weights_kernel, ndp), grid=(h // tile_w,...  10.9 us
    unnamed x28, local copies, waits for them, and re-layouts  7.89 us
    pallas_call x1, Pallas kernels, local(): pl.pallas_call(functools.partial(back_kernel, n, cap), grid=(steps,), out...  7 us
  transfers between devices with their start and end apart: 34, of which 18 were waited for; matrix products, arithmetic and copies ran while one was open for 1% of the time, Pallas kernels for 11%

profile of v1, /device:TPU:0, one launch (start us, length us, event | category | flops | bytes accessed | tf_op | source)
XLA Modules:
  0.0 303.4 jit_solution(4912258082980965698)
XLA Ops:
  0.6 1.2 copy-done.1
  3.2 1.2 prep.1
  4.4 3.0 collective-permute-start.14
  7.4 1.6 collective-permute-start.15
  9.0 3.0 collective-permute-start.17
  12.0 1.5 collective-permute-start
  13.5 2.1 collective-permute-done.refs_9_.refs_1_
  15.6 2.1 collective-permute-start.1
  17.7 14.0 %collective-permute-done.1.refs_10_.refs_2_ = bf16[16,128]{1,0:T(8,128)(2,1)S(1)} collective-permute-done((bf16[16,128]{1,0:T(8,128)(2,1)S(1)}, bf16[16,128]{1,0:T(8,128)(2,1)S(1)}, u32[]{:S(2)}, u32[]{:S(2)}) %collective-permute-start.1) | collective-permute-done | bytes 4128 | tf_op jit(solution)/shard_map/ppermute | solution.py:185
  31.7 1.5 collective-permute-start.2
  33.3 3.0 collective-permute-done.2.refs_11_.refs_3_
  36.2 2.6 collective-permute-start.3
  38.9 1.9 collective-permute-done.3.refs_12_.refs_4_
  40.8 2.5 collective-permute-start.4
  43.3 2.9 collective-permute-done.4.refs_13_.refs_5_
  46.2 3.6 %collective-permute-start.5 = (bf16[16,128]{1,0:T(8,128)(2,1)S(1)}, bf16[16,128]{1,0:T(8,128)(2,1)S(1)}, u32[]{:S(2)}, u32[]{:S(2)}) collective-permute-start(bf16[16,128]{1,0:T(8,128)(2,1)S(1)} %get-tuple-element.39.meta_ref.refs_8_.refs_0_), channel_id=1, source_target_pairs={{0,6},{1,7},{2,4},{3,5},{4,2},{5,3},{6,0},{7,1},{8,14},{9,15},{10,... | collective-permute-start | bytes 12296 | tf_op jit(solution)/shard_map/ppermute | solution.py:185
  49.8 1.8 collective-permute-done.5.refs_14_.refs_6_
  51.6 3.5 %collective-permute-start.6 = (bf16[16,128]{1,0:T(8,128)(2,1)S(1)}, bf16[16,128]{1,0:T(8,128)(2,1)S(1)}, u32[]{:S(2)}, u32[]{:S(2)}) collective-permute-start(bf16[16,128]{1,0:T(8,128)(2,1)S(1)} %get-tuple-element.39.meta_ref.refs_8_.refs_0_), channel_id=1, source_target_pairs={{0,7},{1,6},{2,5},{3,4},{4,3},{5,2},{6,1},{7,0},{8,15},{9,14},{10,... | collective-permute-start | bytes 12296 | tf_op jit(solution)/shard_map/ppermute | solution.py:185
  55.1 1.2 copy-done.2
  58.1 3.6 %collective-permute-start.19 = (bf16[48,3584]{1,0:T(8,128)(2,1)S(1)}, bf16[48,3584]{1,0:T(8,128)(2,1)S(1)}, u32[]{:S(2)}, u32[]{:S(2)}) collective-permute-start(bf16[48,3584]{1,0:T(8,128)(2,1)S(1)} %get-tuple-element.54), channel_id=1, source_target_pairs={{0,6},{1,7},{2,4},{3,5},{4,2},{5,3},{6,0},{7,1},{8,14},{9,15},{10,... | collective-permute-start | bytes 1032200 | tf_op jit(solution)/shard_map/ppermute | solution.py:185
  62.3 2.3 collective-permute-start.10
  65.7 33.8 %collective-permute-done.18.refs_5_ = bf16[48,3584]{1,0:T(8,128)(2,1)S(1)} collective-permute-done((bf16[48,3584]{1,0:T(8,128)(2,1)S(1)}, bf16[48,3584]{1,0:T(8,128)(2,1)S(1)}, u32[]{:S(2)}, u32[]{:S(2)}) %collective-permute-start.18) | collective-permute-done | bytes 344096 | tf_op jit(solution)/shard_map/ppermute | solution.py:185
  99.6 1.7 collective-permute-start.12
  101.2 3.1 %collective-permute-start.13 = (bf16[48,3584]{1,0:T(8,128)(2,1)S(1)}, bf16[48,3584]{1,0:T(8,128)(2,1)S(1)}, u32[]{:S(2)}, u32[]{:S(2)}) collective-permute-start(bf16[48,3584]{1,0:T(8,128)(2,1)S(1)} %get-tuple-element.47), channel_id=1, source_target_pairs={{0,7},{1,6},{2,5},{3,4},{4,3},{5,2},{6,1},{7,0},{8,15},{9,14},{10,... | collective-permute-start | bytes 1032200 | tf_op jit(solution)/shard_map/ppermute | solution.py:185
  104.9 31.6 %collective-permute-done.10.refs_4_ = bf16[48,3584]{1,0:T(8,128)(2,1)S(1)} collective-permute-done((bf16[48,3584]{1,0:T(8,128)(2,1)S(1)}, bf16[48,3584]{1,0:T(8,128)(2,1)S(1)}, u32[]{:S(2)}, u32[]{:S(2)}) %collective-permute-start.10) | collective-permute-done | bytes 344096 | tf_op jit(solution)/shard_map/ppermute | solution.py:185
  136.5 7.4 %collective-permute-done.11.refs_5_ = bf16[48,3584]{1,0:T(8,128)(2,1)S(1)} collective-permute-done((bf16[48,3584]{1,0:T(8,128)(2,1)S(1)}, bf16[48,3584]{1,0:T(8,128)(2,1)S(1)}, u32[]{:S(2)}, u32[]{:S(2)}) %collective-permute-start.11) | collective-permute-done | bytes 344096 | tf_op jit(solution)/shard_map/ppermute | solution.py:185
  143.9 11.0 %forward.1 = (bf16[384,3584]{1,0:T(8,128)(2,1)}, bf16[384,1024]{1,0:T(8,128)(2,1)S(1)}, f32[384,1024]{1,0:T(8,128)S(1)}, f32[384,1024]{1,0:T(8,128)}) custom-call(bf16[48,3584]{1,0:T(8,128)(2,1)S(1)} %get-tuple-element.48.refs_0_, bf16[48,3584]{1,0:T(8,128)(2,1)S(1)} %collective-permute-done.14.refs_1_, ...), custom_call_target="tpu_custom_call" | custom-call | flops 5637144576 | bytes 24117248 | tf_op jit(solution)/shard_map/forward/pallas_call | solution.py:217
  154.9 1.1 copy-done
  156.0 2.5 collective-permute-done.9.refs_3_
  158.5 7.0 %back.1 = (bf16[2,384,1024]{2,1,0:T(8,128)(2,1)S(1)}, bf16[16,384]{1,0:T(8,128)(2,1)S(1)}) custom-call(bf16[48,3584]{1,0:T(8,128)(2,1)S(1)} %get-tuple-element.40.refs_0_, bf16[48,3584]{1,0:T(8,128)(2,1)S(1)} %collective-permute-done.7.refs_1_, bf16[48,3584]{1,0:T(8,128)(2,1)S(1)} %collective-permute-done.8.refs_2_, ...), custom_call_target="tpu_custom_call" | custom-call | flops 2818572288 | bytes 15597568 | tf_op jit(solution)/shard_map/back/pallas_call | solution.py:241
  165.5 1.6 collective-permute-start.32
  167.1 3.8 %rowgrad.5 = (bf16[464,384]{1,0:T(8,128)(2,1)S(1)}, bf16[464,384]{1,0:T(8,128)(2,1)S(1)}) custom-call(s32[1]{0:T(128)} %bitcast.me_ref, bf16[2,384,1024]{2,1,0:T(8,128)(2,1)S(1)} %get-tuple-element.59.grads_ref.refs_4_, bf16[16,384]{1,0:T(8,128)(2,1)S(1)} %get-tuple-element.60.score_ref, bf16[1,3584,1024]{2,1,0:T(8,128)(2,1)} %gate_ref.5, ...), custom_call_target="tpu_custom_call" | custom-call | flops 1409286144 | bytes 5242880 | tf_op jit(solution)/shard_map/rowgrad/pallas_call | solution.py:262
  170.9 1.8 collective-permute-start.26
  172.7 29.3 %collective-permute-done.32.refs_6_ = bf16[2,384,1024]{2,1,0:T(8,128)(2,1)} collective-permute-done((bf16[2,384,1024]{2,1,0:T(8,128)(2,1)S(1)}, bf16[2,384,1024]{2,1,0:T(8,128)(2,1)}, u32[]{:S(2)}, u32[]{:S(2)}) %collective-permute-start.32) | collective-permute-done | bytes 1572896 | tf_op jit(solution)/shard_map/ppermute | solution.py:188
  202.0 1.7 collective-permute-start.27
  203.7 3.8 %rowgrad.4 = (bf16[464,384]{1,0:T(8,128)(2,1)S(1)}, bf16[464,384]{1,0:T(8,128)(2,1)S(1)}) custom-call(s32[1]{0:T(128)} %bitcast.me_ref, bf16[2,384,1024]{2,1,0:T(8,128)(2,1)S(1)} %get-tuple-element.59.grads_ref.refs_4_, bf16[16,384]{1,0:T(8,128)(2,1)S(1)} %get-tuple-element.60.score_ref, bf16[1,3584,1024]{2,1,0:T(8,128)(2,1)} %gate_ref.5, ...), custom_call_target="tpu_custom_call" | custom-call | flops 1409286144 | bytes 5242880 | tf_op jit(solution)/shard_map/rowgrad/pallas_call | solution.py:262
  207.5 3.7 %collective-permute-start.24 = (bf16[464,384]{1,0:T(8,128)(2,1)S(1)}, bf16[464,384]{1,0:T(8,128)(2,1)S(1)}, u32[]{:S(2)}, u32[]{:S(2)}) collective-permute-start(bf16[464,384]{1,0:T(8,128)(2,1)S(1)} %get-tuple-element.65), channel_id=1, source_target_pairs={{0,4},{1,5},{2,6},{3,7},{4,0},{5,1},{6,2},{7,3},{8,12},{9,13},{10,... | collective-permute-start | bytes 1069064 | tf_op jit(solution)/shard_map/ppermute | solution.py:185
  212.2 7.5 %rowgrad.3 = (bf16[464,384]{1,0:T(8,128)(2,1)}, bf16[464,384]{1,0:T(8,128)(2,1)}, bf16[464,384]{1,0:T(8,128)(2,1)}, bf16[464,384]{1,0:T(8,128)(2,1)S(1)}) custom-call(s32[1]{0:T(128)} %bitcast.me_ref, bf16[2,384,1024]{2,1,0:T(8,128)(2,1)S(1)} %get-tuple-element.59.grads_ref.refs_4_, bf16[16,384]{1,0:T(8,128)(2,1)S(1)} %get-tuple-element.60.score_ref, ...), custom_call_target="tpu_custom_call" | custom-call | flops 2818572288 | bytes 8912896 | tf_op jit(solution)/shard_map/rowgrad/pallas_call | solution.py:262
  221.8 24.2 %collective-permute-done.24.refs_12_ = bf16[464,384]{1,0:T(8,128)(2,1)S(1)} collective-permute-done((bf16[464,384]{1,0:T(8,128)(2,1)S(1)}, bf16[464,384]{1,0:T(8,128)(2,1)S(1)}, u32[]{:S(2)}, u32[]{:S(2)}) %collective-permute-start.24) | collective-permute-done | bytes 356384 | tf_op jit(solution)/shard_map/ppermute | solution.py:185
  246.8 7.0 %collective-permute-done.25.refs_13_ = bf16[464,384]{1,0:T(8,128)(2,1)S(1)} collective-permute-done((bf16[464,384]{1,0:T(8,128)(2,1)S(1)}, bf16[464,384]{1,0:T(8,128)(2,1)S(1)}, u32[]{:S(2)}, u32[]{:S(2)}) %collective-permute-start.25) | collective-permute-done | bytes 356384 | tf_op jit(solution)/shard_map/ppermute | solution.py:185
  254.6 2.1 constant_dynamic-slice_fusion
  256.7 4.7 %collective-permute-done.22.refs_10_ = bf16[464,384]{1,0:T(8,128)(2,1)} collective-permute-done((bf16[464,384]{1,0:T(8,128)(2,1)}, bf16[464,384]{1,0:T(8,128)(2,1)}, u32[]{:S(2)}, u32[]{:S(2)}) %collective-permute-start.22) | collective-permute-done | bytes 356384 | tf_op jit(solution)/shard_map/ppermute | solution.py:185
  261.5 1.5 collective-permute-start.29
  263.0 6.0 %collective-permute-done.23.refs_11_ = bf16[464,384]{1,0:T(8,128)(2,1)} collective-permute-done((bf16[464,384]{1,0:T(8,128)(2,1)}, bf16[464,384]{1,0:T(8,128)(2,1)}, u32[]{:S(2)}, u32[]{:S(2)}) %collective-permute-start.23) | collective-permute-done | bytes 356384 | tf_op jit(solution)/shard_map/ppermute | solution.py:185
  270.2 6.6 %combine.1 = (bf16[448,1024]{1,0:T(8,128)(2,1)}, bf16[2,128]{1,0:T(2,128)(2,1)}) custom-call(s32[1]{0:T(128)} %bitcast.me_ref, s32[2,128]{1,0:T(2,128)S(1)} %bitcast.6, bf16[16,128]{1,0:T(8,128)(2,1)S(1)} %get-tuple-element.39.meta_ref.refs_8_.refs_0_, bf16[16,128]{1,0:T(8,128)(2,1)S(1)} %collective-permute-done.refs_9_.refs_1_, ...), custom_call_target="tpu_custom_call" | custom-call | flops 2818572288 | bytes 3670016 | tf_op jit(solution)/shard_map/combine/pallas_call | solution.py:305
  276.8 3.0 collective-permute-done.29.refs_2_
  279.8 12.8 %collective-permute-done.30.refs_3_ = bf16[384,896]{1,0:T(8,128)(2,1)S(1)} collective-permute-done((bf16[384,896]{1,0:T(8,128)(2,1)S(1)}, bf16[384,896]{1,0:T(8,128)(2,1)S(1)}, u32[]{:S(2)}, u32[]{:S(2)}) %collective-permute-start.30) | collective-permute-done | bytes 688160 | tf_op jit(solution)/shard_map/ppermute | solution.py:188
  292.5 10.9 %weights.1 = (bf16[1,896,1024]{2,1,0:T(8,128)(2,1)}, bf16[1,896,1024]{2,1,0:T(8,128)(2,1)}) custom-call(bf16[384,896]{1,0:T(8,128)(2,1)S(1)} %get-tuple-element.77.refs_0_, bf16[384,896]{1,0:T(8,128)(2,1)S(1)} %collective-permute-done.28.refs_1_, bf16[384,896]{1,0:T(8,128)(2,1)S(1)} %collective-permute-done.29.refs_2_, ...), custom_call_target="tpu_custom_call" | custom-call | flops 5637144576 | bytes 12713984 | tf_op jit(solution)/shard_map/weights/pallas_call | solution.py:291
  (58 shorter events, 11.3 us)
Async XLA Ops:
  0.6 1.2 copy-start.1
  1.8 0.7 copy-start.11
  2.5 0.7 copy-start.13
  4.4 53.7 %collective-permute-start.14 = (bf16[48,3584]{1,0:T(8,128)(2,1)S(1)}, bf16[48,3584]{1,0:T(8,128)(2,1)S(1)}, u32[]{:S(2)}, u32[]{:S(2)}) collective-permute-start(bf16[48,3584]{1,0:T(8,128)(2,1)S(1)} %get-tuple-element.49), channel_id=1, source_target_pairs={{0,1},{1,0},{2,3},{3,2},{4,5},{5,4},{6,7},{7,6},{8,9},{9,8},{10,11... | collective-permute-start | bytes 1032200 | tf_op jit(solution)/shard_map/ppermute | solution.py:185
  7.4 54.3 %collective-permute-start.15 = (bf16[48,3584]{1,0:T(8,128)(2,1)S(1)}, bf16[48,3584]{1,0:T(8,128)(2,1)S(1)}, u32[]{:S(2)}, u32[]{:S(2)}) collective-permute-start(bf16[48,3584]{1,0:T(8,128)(2,1)S(1)} %get-tuple-element.50), channel_id=1, source_target_pairs={{0,2},{1,3},{2,0},{3,1},{4,6},{5,7},{6,4},{7,5},{8,10},{9,11},{10,... | collective-permute-start | bytes 1032200 | tf_op jit(solution)/shard_map/ppermute | solution.py:185
  9.0 53.4 %collective-permute-start.16 = (bf16[48,3584]{1,0:T(8,128)(2,1)S(1)}, bf16[48,3584]{1,0:T(8,128)(2,1)S(1)}, u32[]{:S(2)}, u32[]{:S(2)}) collective-permute-start(bf16[48,3584]{1,0:T(8,128)(2,1)S(1)} %get-tuple-element.51), channel_id=1, source_target_pairs={{0,3},{1,2},{2,1},{3,0},{4,7},{5,6},{6,5},{7,4},{8,11},{9,10},{10,... | collective-permute-start | bytes 1032200 | tf_op jit(solution)/shard_map/ppermute | solution.py:185
  9.0 55.7 %collective-permute-start.17 = (bf16[48,3584]{1,0:T(8,128)(2,1)S(1)}, bf16[48,3584]{1,0:T(8,128)(2,1)S(1)}, u32[]{:S(2)}, u32[]{:S(2)}) collective-permute-start(bf16[48,3584]{1,0:T(8,128)(2,1)S(1)} %get-tuple-element.52), channel_id=1, source_target_pairs={{0,4},{1,5},{2,6},{3,7},{4,0},{5,1},{6,2},{7,3},{8,12},{9,13},{10,... | collective-permute-start | bytes 1032200 | tf_op jit(solution)/shard_map/ppermute | solution.py:185
  12.0 3.6 %collective-permute-start = (bf16[16,128]{1,0:T(8,128)(2,1)S(1)}, bf16[16,128]{1,0:T(8,128)(2,1)S(1)}, u32[]{:S(2)}, u32[]{:S(2)}) collective-permute-start(bf16[16,128]{1,0:T(8,128)(2,1)S(1)} %get-tuple-element.39.meta_ref.refs_8_.refs_0_), channel_id=1, source_target_pairs={{0,1},{1,0},{2,3},{3,2},{4,5},{5,4},{6,7},{7,6},{8,9},{9,8},{10,11... | collective-permute-start | bytes 12296 | tf_op jit(solution)/shard_map/ppermute | solution.py:185
  15.6 16.2 %collective-permute-start.1 = (bf16[16,128]{1,0:T(8,128)(2,1)S(1)}, bf16[16,128]{1,0:T(8,128)(2,1)S(1)}, u32[]{:S(2)}, u32[]{:S(2)}) collective-permute-start(bf16[16,128]{1,0:T(8,128)(2,1)S(1)} %get-tuple-element.39.meta_ref.refs_8_.refs_0_), channel_id=1, source_target_pairs={{0,2},{1,3},{2,0},{3,1},{4,6},{5,7},{6,4},{7,5},{8,10},{9,11},{10,... | collective-permute-start | bytes 12296 | tf_op jit(solution)/shard_map/ppermute | solution.py:185
  31.7 4.5 %collective-permute-start.2 = (bf16[16,128]{1,0:T(8,128)(2,1)S(1)}, bf16[16,128]{1,0:T(8,128)(2,1)S(1)}, u32[]{:S(2)}, u32[]{:S(2)}) collective-permute-start(bf16[16,128]{1,0:T(8,128)(2,1)S(1)} %get-tuple-element.39.meta_ref.refs_8_.refs_0_), channel_id=1, source_target_pairs={{0,3},{1,2},{2,1},{3,0},{4,7},{5,6},{6,5},{7,4},{8,11},{9,10},{10,... | collective-permute-start | bytes 12296 | tf_op jit(solution)/shard_map/ppermute | solution.py:185
  36.2 4.5 %collective-permute-start.3 = (bf16[16,128]{1,0:T(8,128)(2,1)S(1)}, bf16[16,128]{1,0:T(8,128)(2,1)S(1)}, u32[]{:S(2)}, u32[]{:S(2)}) collective-permute-start(bf16[16,128]{1,0:T(8,128)(2,1)S(1)} %get-tuple-element.39.meta_ref.refs_8_.refs_0_), channel_id=1, source_target_pairs={{0,4},{1,5},{2,6},{3,7},{4,0},{5,1},{6,2},{7,3},{8,12},{9,13},{10,... | collective-permute-start | bytes 12296 | tf_op jit(solution)/shard_map/ppermute | solution.py:185
  40.8 5.4 %collective-permute-start.4 = (bf16[16,128]{1,0:T(8,128)(2,1)S(1)}, bf16[16,128]{1,0:T(8,128)(2,1)S(1)}, u32[]{:S(2)}, u32[]{:S(2)}) collective-permute-start(bf16[16,128]{1,0:T(8,128)(2,1)S(1)} %get-tuple-element.39.meta_ref.refs_8_.refs_0_), channel_id=1, source_target_pairs={{0,5},{1,4},{2,7},{3,6},{4,1},{5,0},{6,3},{7,2},{8,13},{9,12},{10,... | collective-permute-start | bytes 12296 | tf_op jit(solution)/shard_map/ppermute | solution.py:185
  46.2 5.4 %collective-permute-start.5 = (bf16[16,128]{1,0:T(8,128)(2,1)S(1)}, bf16[16,128]{1,0:T(8,128)(2,1)S(1)}, u32[]{:S(2)}, u32[]{:S(2)}) collective-permute-start(bf16[16,128]{1,0:T(8,128)(2,1)S(1)} %get-tuple-element.39.meta_ref.refs_8_.refs_0_), channel_id=1, source_target_pairs={{0,6},{1,7},{2,4},{3,5},{4,2},{5,3},{6,0},{7,1},{8,14},{9,15},{10,... | collective-permute-start | bytes 12296 | tf_op jit(solution)/shard_map/ppermute | solution.py:185
  51.6 6.5 %collective-permute-start.6 = (bf16[16,128]{1,0:T(8,128)(2,1)S(1)}, bf16[16,128]{1,0:T(8,128)(2,1)S(1)}, u32[]{:S(2)}, u32[]{:S(2)}) collective-permute-start(bf16[16,128]{1,0:T(8,128)(2,1)S(1)} %get-tuple-element.39.meta_ref.refs_8_.refs_0_), channel_id=1, source_target_pairs={{0,7},{1,6},{2,5},{3,4},{4,3},{5,2},{6,1},{7,0},{8,15},{9,14},{10,... | collective-permute-start | bytes 12296 | tf_op jit(solution)/shard_map/ppermute | solution.py:185
  55.1 1.2 copy-start.2
  58.1 41.5 %collective-permute-start.18 = (bf16[48,3584]{1,0:T(8,128)(2,1)S(1)}, bf16[48,3584]{1,0:T(8,128)(2,1)S(1)}, u32[]{:S(2)}, u32[]{:S(2)}) collective-permute-start(bf16[48,3584]{1,0:T(8,128)(2,1)S(1)} %get-tuple-element.53), channel_id=1, source_target_pairs={{0,5},{1,4},{2,7},{3,6},{4,1},{5,0},{6,3},{7,2},{8,13},{9,12},{10,... | collective-permute-start | bytes 1032200 | tf_op jit(solution)/shard_map/ppermute | solution.py:185
  58.1 43.2 %collective-permute-start.19 = (bf16[48,3584]{1,0:T(8,128)(2,1)S(1)}, bf16[48,3584]{1,0:T(8,128)(2,1)S(1)}, u32[]{:S(2)}, u32[]{:S(2)}) collective-permute-start(bf16[48,3584]{1,0:T(8,128)(2,1)S(1)} %get-tuple-element.54), channel_id=1, source_target_pairs={{0,6},{1,7},{2,4},{3,5},{4,2},{5,3},{6,0},{7,1},{8,14},{9,15},{10,... | collective-permute-start | bytes 1032200 | tf_op jit(solution)/shard_map/ppermute | solution.py:185
  61.6 42.7 %collective-permute-start.20 = (bf16[48,3584]{1,0:T(8,128)(2,1)S(1)}, bf16[48,3584]{1,0:T(8,128)(2,1)S(1)}, u32[]{:S(2)}, u32[]{:S(2)}) collective-permute-start(bf16[48,3584]{1,0:T(8,128)(2,1)S(1)} %get-tuple-element.55), channel_id=1, source_target_pairs={{0,7},{1,6},{2,5},{3,4},{4,3},{5,2},{6,1},{7,0},{8,15},{9,14},{10,... | collective-permute-start | bytes 1032200 | tf_op jit(solution)/shard_map/ppermute | solution.py:185
  62.3 74.1 %collective-permute-start.10 = (bf16[48,3584]{1,0:T(8,128)(2,1)S(1)}, bf16[48,3584]{1,0:T(8,128)(2,1)S(1)}, u32[]{:S(2)}, u32[]{:S(2)}) collective-permute-start(bf16[48,3584]{1,0:T(8,128)(2,1)S(1)} %get-tuple-element.44), channel_id=1, source_target_pairs={{0,4},{1,5},{2,6},{3,7},{4,0},{5,1},{6,2},{7,3},{8,12},{9,13},{10,... | collective-permute-start | bytes 1032200 | tf_op jit(solution)/shard_map/ppermute | solution.py:185
  64.6 79.2 %collective-permute-start.11 = (bf16[48,3584]{1,0:T(8,128)(2,1)S(1)}, bf16[48,3584]{1,0:T(8,128)(2,1)S(1)}, u32[]{:S(2)}, u32[]{:S(2)}) collective-permute-start(bf16[48,3584]{1,0:T(8,128)(2,1)S(1)} %get-tuple-element.45), channel_id=1, source_target_pairs={{0,5},{1,4},{2,7},{3,6},{4,1},{5,0},{6,3},{7,2},{8,13},{9,12},{10,... | collective-permute-start | bytes 1032200 | tf_op jit(solution)/shard_map/ppermute | solution.py:185
  99.6 56.4 %collective-permute-start.12 = (bf16[48,3584]{1,0:T(8,128)(2,1)S(1)}, bf16[48,3584]{1,0:T(8,128)(2,1)S(1)}, u32[]{:S(2)}, u32[]{:S(2)}) collective-permute-start(bf16[48,3584]{1,0:T(8,128)(2,1)S(1)} %get-tuple-element.46), channel_id=1, source_target_pairs={{0,6},{1,7},{2,4},{3,5},{4,2},{5,3},{6,0},{7,1},{8,14},{9,15},{10,... | collective-permute-start | bytes 1032200 | tf_op jit(solution)/shard_map/ppermute | solution.py:185
  101.2 54.8 %collective-permute-start.13 = (bf16[48,3584]{1,0:T(8,128)(2,1)S(1)}, bf16[48,3584]{1,0:T(8,128)(2,1)S(1)}, u32[]{:S(2)}, u32[]{:S(2)}) collective-permute-start(bf16[48,3584]{1,0:T(8,128)(2,1)S(1)} %get-tuple-element.47), channel_id=1, source_target_pairs={{0,7},{1,6},{2,5},{3,4},{4,3},{5,2},{6,1},{7,0},{8,15},{9,14},{10,... | collective-permute-start | bytes 1032200 | tf_op jit(solution)/shard_map/ppermute | solution.py:185
  104.3 51.7 %collective-permute-start.7 = (bf16[48,3584]{1,0:T(8,128)(2,1)S(1)}, bf16[48,3584]{1,0:T(8,128)(2,1)S(1)}, u32[]{:S(2)}, u32[]{:S(2)}) collective-permute-start(bf16[48,3584]{1,0:T(8,128)(2,1)S(1)} %get-tuple-element.41), channel_id=1, source_target_pairs={{0,1},{1,0},{2,3},{3,2},{4,5},{5,4},{6,7},{7,6},{8,9},{9,8},{10,11... | collective-permute-start | bytes 1032200 | tf_op jit(solution)/shard_map/ppermute | solution.py:185
  136.5 19.5 %collective-permute-start.8 = (bf16[48,3584]{1,0:T(8,128)(2,1)S(1)}, bf16[48,3584]{1,0:T(8,128)(2,1)S(1)}, u32[]{:S(2)}, u32[]{:S(2)}) collective-permute-start(bf16[48,3584]{1,0:T(8,128)(2,1)S(1)} %get-tuple-element.42), channel_id=1, source_target_pairs={{0,2},{1,3},{2,0},{3,1},{4,6},{5,7},{6,4},{7,5},{8,10},{9,11},{10,... | collective-permute-start | bytes 1032200 | tf_op jit(solution)/shard_map/ppermute | solution.py:185
  143.9 14.6 %collective-permute-start.9 = (bf16[48,3584]{1,0:T(8,128)(2,1)S(1)}, bf16[48,3584]{1,0:T(8,128)(2,1)S(1)}, u32[]{:S(2)}, u32[]{:S(2)}) collective-permute-start(bf16[48,3584]{1,0:T(8,128)(2,1)S(1)} %get-tuple-element.43), channel_id=1, source_target_pairs={{0,3},{1,2},{2,1},{3,0},{4,7},{5,6},{6,5},{7,4},{8,11},{9,10},{10,... | collective-permute-start | bytes 1032200 | tf_op jit(solution)/shard_map/ppermute | solution.py:185
  154.8 1.1 copy-start
  165.5 36.5 %collective-permute-start.32 = (bf16[2,384,1024]{2,1,0:T(8,128)(2,1)S(1)}, bf16[2,384,1024]{2,1,0:T(8,128)(2,1)}, u32[]{:S(2)}, u32[]{:S(2)}) collective-permute-start(bf16[2,384,1024]{2,1,0:T(8,128)(2,1)S(1)} %get-tuple-element.59.grads_ref.refs_4_), channel_id=1, source_target_pairs={{0,16},{8,24},{16,0},{24,8},{1,17},{9,25},{17,1},{25,9},{2,18},{10... | collective-permute-start | bytes 4718600 | tf_op jit(solution)/shard_map/ppermute | solution.py:188
  170.9 40.3 %collective-permute-start.26 = (bf16[464,384]{1,0:T(8,128)(2,1)S(1)}, bf16[464,384]{1,0:T(8,128)(2,1)S(1)}, u32[]{:S(2)}, u32[]{:S(2)}) collective-permute-start(bf16[464,384]{1,0:T(8,128)(2,1)S(1)} %get-tuple-element.67), channel_id=1, source_target_pairs={{0,6},{1,7},{2,4},{3,5},{4,2},{5,3},{6,0},{7,1},{8,14},{9,15},{10,... | collective-permute-start | bytes 1069064 | tf_op jit(solution)/shard_map/ppermute | solution.py:185
  172.7 119.8 %collective-permute-start.31 = (bf16[2,384,1024]{2,1,0:T(8,128)(2,1)S(1)}, bf16[2,384,1024]{2,1,0:T(8,128)(2,1)S(1)}, u32[]{:S(2)}, u32[]{:S(2)}) collective-permute-start(bf16[2,384,1024]{2,1,0:T(8,128)(2,1)S(1)} %get-tuple-element.59.grads_ref.refs_4_), channel_id=1, source_target_pairs={{0,8},{8,0},{16,24},{24,16},{1,9},{9,1},{17,25},{25,17},{2,10},{10... | collective-permute-start | bytes 4718600 | tf_op jit(solution)/shard_map/ppermute | solution.py:188
  202.0 90.5 %collective-permute-start.33 = (bf16[2,384,1024]{2,1,0:T(8,128)(2,1)}, bf16[2,384,1024]{2,1,0:T(8,128)(2,1)}, u32[]{:S(2)}, u32[]{:S(2)}) collective-permute-start(bf16[2,384,1024]{2,1,0:T(8,128)(2,1)} %collective-permute-done.32.refs_6_), channel_id=1, source_target_pairs={{0,8},{8,0},{16,24},{24,16},{1,9},{9,1},{17,25},{25,17},{2,10},{10... | collective-permute-start | bytes 4718600 | tf_op jit(solution)/shard_map/ppermute | solution.py:188
  202.0 18.5 %collective-permute-start.27 = (bf16[464,384]{1,0:T(8,128)(2,1)S(1)}, bf16[464,384]{1,0:T(8,128)(2,1)S(1)}, u32[]{:S(2)}, u32[]{:S(2)}) collective-permute-start(bf16[464,384]{1,0:T(8,128)(2,1)S(1)} %get-tuple-element.68), channel_id=1, source_target_pairs={{0,7},{1,6},{2,5},{3,4},{4,3},{5,2},{6,1},{7,0},{8,15},{9,14},{10,... | collective-permute-start | bytes 1069064 | tf_op jit(solution)/shard_map/ppermute | solution.py:185
  207.5 38.5 %collective-permute-start.24 = (bf16[464,384]{1,0:T(8,128)(2,1)S(1)}, bf16[464,384]{1,0:T(8,128)(2,1)S(1)}, u32[]{:S(2)}, u32[]{:S(2)}) collective-permute-start(bf16[464,384]{1,0:T(8,128)(2,1)S(1)} %get-tuple-element.65), channel_id=1, source_target_pairs={{0,4},{1,5},{2,6},{3,7},{4,0},{5,1},{6,2},{7,3},{8,12},{9,13},{10,... | collective-permute-start | bytes 1069064 | tf_op jit(solution)/shard_map/ppermute | solution.py:185
  211.3 42.5 %collective-permute-start.25 = (bf16[464,384]{1,0:T(8,128)(2,1)S(1)}, bf16[464,384]{1,0:T(8,128)(2,1)S(1)}, u32[]{:S(2)}, u32[]{:S(2)}) collective-permute-start(bf16[464,384]{1,0:T(8,128)(2,1)S(1)} %get-tuple-element.66), channel_id=1, source_target_pairs={{0,5},{1,4},{2,7},{3,6},{4,1},{5,0},{6,3},{7,2},{8,13},{9,12},{10,... | collective-permute-start | bytes 1069064 | tf_op jit(solution)/shard_map/ppermute | solution.py:185
  219.7 0.7 copy-start.9
  220.5 0.8 copy-start.3
  221.3 35.4 %collective-permute-start.21 = (bf16[464,384]{1,0:T(8,128)(2,1)}, bf16[464,384]{1,0:T(8,128)(2,1)}, u32[]{:S(2)}, u32[]{:S(2)}) collective-permute-start(bf16[464,384]{1,0:T(8,128)(2,1)} %get-tuple-element.62), channel_id=1, source_target_pairs={{0,1},{1,0},{2,3},{3,2},{4,5},{5,4},{6,7},{7,6},{8,9},{9,8},{10,11... | collective-permute-start | bytes 1069064 | tf_op jit(solution)/shard_map/ppermute | solution.py:185
  246.0 0.7 copy-start.5
  246.8 14.7 %collective-permute-start.22 = (bf16[464,384]{1,0:T(8,128)(2,1)}, bf16[464,384]{1,0:T(8,128)(2,1)}, u32[]{:S(2)}, u32[]{:S(2)}) collective-permute-start(bf16[464,384]{1,0:T(8,128)(2,1)} %get-tuple-element.63), channel_id=1, source_target_pairs={{0,2},{1,3},{2,0},{3,1},{4,6},{5,7},{6,4},{7,5},{8,10},{9,11},{10,... | collective-permute-start | bytes 1069064 | tf_op jit(solution)/shard_map/ppermute | solution.py:185
  253.7 0.8 copy-start.7
  254.5 14.5 %collective-permute-start.23 = (bf16[464,384]{1,0:T(8,128)(2,1)}, bf16[464,384]{1,0:T(8,128)(2,1)}, u32[]{:S(2)}, u32[]{:S(2)}) collective-permute-start(bf16[464,384]{1,0:T(8,128)(2,1)} %get-tuple-element.64), channel_id=1, source_target_pairs={{0,3},{1,2},{2,1},{3,0},{4,7},{5,6},{6,5},{7,4},{8,11},{9,10},{10,... | collective-permute-start | bytes 1069064 | tf_op jit(solution)/shard_map/ppermute | solution.py:185
  254.5 15.6 %copy-start.4 = (bf16[464,384]{1,0:T(8,128)(2,1)S(1)}, bf16[464,384]{1,0:T(8,128)(2,1)}, u32[]{:S(2)}) copy-start(bf16[464,384]{1,0:T(8,128)(2,1)} %copy-done.3) | copy-start | bytes 1069060
  254.5 15.6 %copy-start.6 = (bf16[464,384]{1,0:T(8,128)(2,1)S(1)}, bf16[464,384]{1,0:T(8,128)(2,1)}, u32[]{:S(2)}) copy-start(bf16[464,384]{1,0:T(8,128)(2,1)} %copy-done.5) | copy-start | bytes 1069060
  254.5 15.6 %copy-start.8 = (bf16[464,384]{1,0:T(8,128)(2,1)S(1)}, bf16[464,384]{1,0:T(8,128)(2,1)}, u32[]{:S(2)}) copy-start(bf16[464,384]{1,0:T(8,128)(2,1)} %copy-done.7) | copy-start | bytes 1069060
  254.5 15.6 %copy-start.10 = (bf16[464,384]{1,0:T(8,128)(2,1)S(1)}, bf16[464,384]{1,0:T(8,128)(2,1)}, u32[]{:S(2)}) copy-start(bf16[464,384]{1,0:T(8,128)(2,1)} %copy-done.9) | copy-start | bytes 1069060
  254.5 15.6 %copy-start.12 = (s32[128,2]{0,1:T(2,128)S(1)}, s32[128,2]{0,1:T(2,128)}, u32[]{:S(2)}) copy-start(s32[128,2]{0,1:T(2,128)} %param.10) | copy-start | bytes 3076
  256.6 20.1 %collective-permute-start.28 = (bf16[384,896]{1,0:T(8,128)(2,1)S(1)}, bf16[384,896]{1,0:T(8,128)(2,1)S(1)}, u32[]{:S(2)}, u32[]{:S(2)}) collective-permute-start(bf16[384,896]{1,0:T(8,128)(2,1)S(1)} %get-tuple-element.76), channel_id=1, source_target_pairs={{0,8},{8,0},{16,24},{24,16},{1,9},{9,1},{17,25},{25,17},{2,10},{10... | collective-permute-start | bytes 2064392 | tf_op jit(solution)/shard_map/ppermute | solution.py:188
  261.5 18.3 %collective-permute-start.29 = (bf16[384,896]{1,0:T(8,128)(2,1)S(1)}, bf16[384,896]{1,0:T(8,128)(2,1)S(1)}, u32[]{:S(2)}, u32[]{:S(2)}) collective-permute-start(bf16[384,896]{1,0:T(8,128)(2,1)S(1)} %get-tuple-element.75), channel_id=1, source_target_pairs={{0,16},{8,24},{16,0},{24,8},{1,17},{9,25},{17,1},{25,9},{2,18},{10... | collective-permute-start | bytes 2064392 | tf_op jit(solution)/shard_map/ppermute | solution.py:188
  269.0 23.5 %collective-permute-start.30 = (bf16[384,896]{1,0:T(8,128)(2,1)S(1)}, bf16[384,896]{1,0:T(8,128)(2,1)S(1)}, u32[]{:S(2)}, u32[]{:S(2)}) collective-permute-start(bf16[384,896]{1,0:T(8,128)(2,1)S(1)} %get-tuple-element.74), channel_id=1, source_target_pairs={{0,24},{8,16},{16,8},{24,0},{1,25},{9,17},{17,9},{25,1},{2,26},{10... | collective-permute-start | bytes 2064392 | tf_op jit(solution)/shard_map/ppermute | solution.py:188

commit v2 on v1

v2 whole, which is shorter than its diff:
```python
import functools

import jax
import jax.numpy as jnp
from jax import lax
from jax.experimental import pallas as pl
from jax.experimental.pallas import tpu as pltpu
from jax.sharding import PartitionSpec as P

F32 = jnp.float32
BF16 = jnp.bfloat16
NT = (((1,), (1,)), ((), ()))
TN = (((0,), (0,)), ((), ()))


def params(mib=48):
    return pltpu.CompilerParams(vmem_limit_bytes=mib << 20)


def vmem(count):
    return [pl.BlockSpec(memory_space=pltpu.VMEM)] * count


def smem():
    return pl.BlockSpec(memory_space=pltpu.SMEM)


LONG = 1 << 40


def pick_rows(cap, code, meta, tok_ref, dest):
    toks, d = tok_ref.shape
    slot = lax.broadcasted_iota(jnp.int32, (cap, toks), 0).astype(F32)
    for j, ref, at in dest:
        pick = (slot == code[j : j + 1, :]).astype(F32).astype(BF16)
        chosen = jnp.dot(pick, tok_ref[...], preferred_element_type=F32).astype(BF16)
        ref[at : at + cap, 0:d] = chosen
        if ref.shape[1] > d:
            ref[at : at + cap, d:] = jnp.zeros((cap, toks), BF16)
            ref[at : at + meta.shape[0], d:] = meta


def prep_kernel(n, nx, cap, me_ref, ids_ref, gates_ref, tok_ref, cot_ref, meta_ref, *out_refs):
    toks = tok_ref.shape[0]
    nz = n // nx
    expert = lax.broadcasted_iota(jnp.int32, (n, toks), 0) ^ me_ref[0]
    first = ids_ref[0:1, :] == expert
    second = ids_ref[1:2, :] == expert
    count = (first | second).astype(F32)
    before = (
        lax.broadcasted_iota(jnp.int32, (toks, toks), 0)
        < lax.broadcasted_iota(jnp.int32, (toks, toks), 1)
    ).astype(F32)
    position = jnp.dot(count.astype(BF16), before.astype(BF16), preferred_element_type=F32)
    code = jnp.where(first | second, position, -1.0)
    gates = gates_ref[...].astype(F32)
    weight = jnp.where(first, gates[0:1, :], 0.0) + jnp.where(second, gates[1:2, :], 0.0)
    meta = jnp.concatenate([code, weight], axis=0).astype(BF16)
    meta_ref[...] = meta
    near_refs, rest, y_refs = out_refs[: nz - 2], out_refs[nz - 2 : 1 - nx], out_refs[1 - nx :]
    near = [(zk * nx + xo, near_refs[zk - 1], xo * cap) for zk in range(1, nz - 1) for xo in range(nx)]
    spots = list(range(n - nx, n)) + list(range(nx))
    pick_rows(cap, code, meta, tok_ref, near + [(j, ref, 0) for j, ref in zip(spots, rest)])
    by_column = [(zk * nx + xo, y_refs[xo - 1], zk * cap) for zk in range(nz) for xo in range(1, nx)]
    pick_rows(cap, code, meta, cot_ref, by_column)


def second_kernel(n, nx, cap, meta_ref, cot_ref, *refs):
    nz = n // nx
    y_came, x_own, x_came = refs[: nx - 1], refs[nx - 1 : 2 * nx - 2], refs[2 * nx - 2 : 2 * nx + nz - 4]
    y_refs, x_refs = refs[1 - nx - nz : 1 - nx], refs[1 - nx :]
    meta = meta_ref[...]
    own = [(zk * nx, y_refs[zk], 0) for zk in range(nz)]
    pick_rows(cap, meta.astype(F32)[0:n, :], meta, cot_ref, own)
    for xo in range(1, nx):
        for zk in range(1, nz):
            y_refs[zk][xo * cap : (xo + 1) * cap, :] = y_came[xo - 1][zk * cap : (zk + 1) * cap, :]
        x_refs[xo - 1][0:cap, :] = x_own[xo - 1][...]
        for i, ref in enumerate(x_came, 1):
            x_refs[xo - 1][i * cap : (i + 1) * cap, :] = ref[xo * cap : (xo + 1) * cap, :]


def found_x(n, nx, cap, refs):
    nz = n // nx
    z_refs, side_refs, far_refs = refs[: nz - 1], refs[nz - 1 : nz + nx - 2], refs[nz + nx - 2 :]
    found = []
    for zk in range(nz - 1):
        found += [(z_refs[zk], 0)] + [(side_refs[xo], zk * cap) for xo in range(nx - 1)]
    return found + [(ref, 0) for ref in far_refs]


def found_y(n, nx, cap, refs):
    nz = n // nx
    z_refs, y_refs = refs[:nz], refs[nz:]
    return [
        (z_refs[zk], xo * cap) if zk or not xo else (y_refs[xo - 1], 0)
        for zk in range(nz)
        for xo in range(nx)
    ]


def fence_kernel(out_ref):
    out_ref[...] = jnp.zeros_like(out_ref)


def forward_kernel(n, nx, cap, count, ny, place_ref, *refs):
    found = found_x(n, nx, cap, refs[:count])
    meta_ref, gate_ref, up_ref, pass_ref, *out_refs = refs[count:]
    part_refs, out_refs = out_refs[:ny], out_refs[ny:]
    hidden_ref, pa_ref, pb_ref, passed_ref, metas_ref, w_ref, rows_ref = out_refs
    toks = meta_ref.shape[1]
    d = rows_ref.shape[1]
    width = part_refs[0].shape[1]

    @pl.when(pl.program_id(0) == 0)
    def _():
        slot = lax.broadcasted_iota(jnp.int32, (cap, toks), 0).astype(F32)
        for j, (ref, at) in enumerate(found):
            rows_ref[j * cap : (j + 1) * cap, :] = ref[at : at + cap, 0:d]
            if j:
                metas_ref[j] = ref[at : at + 2 * n, d:]
            else:
                metas_ref[j] = meta_ref[...]
            meta = metas_ref[j].astype(F32)
            picked = jnp.where(slot == meta[j : j + 1, :], meta[n + j : n + j + 1, :], 0.0)
            total = jnp.sum(picked, axis=1, keepdims=True)
            w_ref[j * cap : (j + 1) * cap, :] = jnp.broadcast_to(total, (cap, w_ref.shape[1]))
        for yo, ref in enumerate(part_refs):
            at = pl.multiple_of((place_ref[0] ^ yo) * width, 128)
            ref[...] = rows_ref[:, pl.ds(at, width)]
        passed_ref[...] = pass_ref[...]

    a = jnp.dot(rows_ref[...], gate_ref[0], preferred_element_type=F32)
    b = jnp.dot(rows_ref[...], up_ref[0], preferred_element_type=F32)
    w = w_ref[:, 0:1]
    sig = jax.nn.sigmoid(a)
    silu = a * sig
    hidden_ref[...] = (silu * b).astype(BF16)
    pa_ref[...] = w * b * sig * (1.0 + a * (1.0 - sig))
    pb_ref[...] = w * silu


def back_kernel(n, nx, cap, count, *refs):
    found = found_y(n, nx, cap, refs[:count])
    hidden_ref, pa_ref, pb_ref, down_ref, grads_ref, score_ref, rows_ref, part_ref = refs[count:]
    step = pl.program_id(0)

    @pl.when(step == 0)
    def _():
        for j, (ref, at) in enumerate(found):
            rows_ref[j * cap : (j + 1) * cap, :] = ref[at : at + cap, :]
        part_ref[...] = jnp.zeros_like(part_ref)

    back = lax.dot_general(rows_ref[...], down_ref[0], NT, preferred_element_type=F32)
    grads_ref[0] = (back * pa_ref[...]).astype(BF16)
    grads_ref[1] = (back * pb_ref[...]).astype(BF16)
    prod = back * hidden_ref[...].astype(F32)
    part = part_ref[...]
    for c in range(prod.shape[1] // 128):
        part = part + prod[:, c * 128 : (c + 1) * 128]
    part_ref[...] = part

    @pl.when(step == pl.num_programs(0) - 1)
    def _():
        total = jnp.sum(jnp.transpose(part_ref[...]), axis=0, keepdims=True)
        shape = score_ref.shape
        top = lax.broadcasted_iota(jnp.int32, shape, 0) == 0
        score_ref[...] = jnp.where(top, jnp.broadcast_to(total, shape), 0.0).astype(BF16)


def rowgrad_kernel(places, dest_ref, grads_ref, score_ref, gate_ref, up_ref, *out_refs):
    del dest_ref
    size = gate_ref.shape[1]
    val = lax.dot_general(gate_ref[0], grads_ref[0], NT, preferred_element_type=F32)
    val = val + lax.dot_general(up_ref[0], grads_ref[1], NT, preferred_element_type=F32)
    val = val.astype(BF16)
    for i, (out, at) in enumerate(places):

        @pl.when(pl.program_id(0) == i)
        def _():
            out_refs[out][at : at + size, :] = val
            out_refs[out][at + size : at + size + 16, :] = score_ref[...]


def second_back_kernel(nx, size, came_ref, *refs):
    for i in range(nx - 1):
        out = refs[nx - 1 + i]
        out[0:size, :] = refs[i][...]
        out[size:, :] = came_ref[(i + 1) * size : (i + 2) * size, :]


def combine_kernel(n, cap, feats, parts, last, me_ref, ids_ref, metas_ref, *refs):
    me = me_ref[0]
    rows = n * cap
    toks = metas_ref.shape[2]
    metas = [metas_ref[j].astype(F32) for j in range(n)]
    if last:
        total_ref, part_ref, out_ref, gates_ref = refs[-4:]
        total = total_ref[...]
        gg = [part_ref[0], part_ref[1]]
    else:
        total_ref, part_ref = refs[-2:]
        total = jnp.zeros((feats, n * toks), F32)
        gg = [jnp.zeros((16, toks), F32)] * 2
    row = lax.broadcasted_iota(jnp.int32, (rows, n * toks), 0).astype(F32)
    for k, which, at in parts:
        wanted = []
        for j in range(n):
            code = metas[j][j ^ k : (j ^ k) + 1, :]
            wanted.append(jnp.where(code >= 0.0, code + float((j ^ k) * cap), -1.0))
        wanted = jnp.concatenate(wanted, axis=1)
        pick = (row == wanted).astype(F32).astype(BF16)
        got = refs[which][at : at + feats, :]
        total = total + jnp.dot(got, pick, preferred_element_type=F32)
        got = refs[which][at + feats : at + feats + 16, :]
        score = jnp.dot(got, pick[:, 0:toks], preferred_element_type=F32)
        gg = [gg[c] + jnp.where(ids_ref[c : c + 1, :] == (me ^ k), score, 0.0) for c in (0, 1)]
    if not last:
        total_ref[...] = total
        part_ref[0] = gg[0]
        part_ref[1] = gg[1]
        return
    for j in range(n):
        place = pl.multiple_of((me ^ j) * toks, toks)
        out_ref[:, pl.ds(place, toks)] = total[:, j * toks : (j + 1) * toks].astype(BF16)
    gates_ref[...] = jnp.concatenate([gg[0][0:1], gg[1][0:1]], axis=0).astype(BF16)


def stack_kernel(ny, core_ref, *refs):
    g_refs, x_refs = refs[:ny], refs[ny : 2 * ny]
    stack_ref, keep_ref, send_ref = refs[2 * ny :]
    block = keep_ref.shape[2]
    for yo in range(ny):
        stack_ref[yo] = g_refs[yo][...]

        @pl.when(core_ref[0] == 0)
        def _():
            keep_ref[yo] = x_refs[yo][:, :block]
            send_ref[yo] = x_refs[yo][:, block:]

        @pl.when(core_ref[0] != 0)
        def _():
            keep_ref[yo] = x_refs[yo][:, block:]
            send_ref[yo] = x_refs[yo][:, :block]


def weights_kernel(ndp, *refs):
    ny = ndp // 2
    x_refs, g_refs, stack_ref = refs[:2], refs[2 : 2 + ny], refs[2 + ny]
    gate_ref, up_ref = refs[-2:]
    for half, out in ((0, gate_ref), (1, up_ref)):
        total = None
        for q in range(ndp):
            g = stack_ref[q // 2, half] if q % 2 else g_refs[q // 2][half]
            term = lax.dot_general(x_refs[q % 2][q // 2], g, TN, preferred_element_type=F32)
            total = term if total is None else total + term
        out[0] = (total * (1.0 / ndp)).astype(BF16)


def local(tokens, cotangent, gates, expert_ids, gate_w, up_w, down_w):
    toks, d = tokens.shape
    top = expert_ids.shape[1]
    h = gate_w.shape[2]
    n = lax.axis_size("expert")
    ndp = lax.axis_size("dp")
    nz = 4
    nx = n // nz
    ny = ndp // 2
    cap = -(-(3 * toks * top // (2 * n)) // 16) * 16
    rows = n * cap
    feats = d // n
    size = feats + 16
    block = d // ndp
    wide = d + toks
    me = lax.axis_index("expert").astype(jnp.int32)
    my_dp = lax.axis_index("dp").astype(jnp.int32)
    me_arr = me.reshape(1)
    my_y, my_core = (my_dp // 2).reshape(1), (my_dp % 2).reshape(1)
    ids_t = expert_ids.T
    gates_t = gates.T
    any_space = pl.BlockSpec(memory_space=pl.ANY)

    def swap(v, k):
        return lax.ppermute(v, "expert", [(i, i ^ k) for i in range(n)])

    def swap_dp(v, q):
        return lax.ppermute(v, "dp", [(i, i ^ q) for i in range(ndp)])

    def shape(*dims, dtype=BF16):
        return jax.ShapeDtypeStruct(dims, dtype)

    previous = []

    def run(body, name, outs, args, in_specs, out_specs, after=(), grid=(), scalars=0, scratch=(), weight=LONG):
        waits = [*after, *previous]
        first = len(args)

        def trimmed(*refs):
            body(*refs[:first], *refs[first + len(waits) :])

        made = pl.pallas_call(
            trimmed,
            grid_spec=pltpu.PrefetchScalarGridSpec(
                num_scalar_prefetch=scalars,
                grid=grid,
                in_specs=[*in_specs, *[any_space] * len(waits)],
                out_specs=out_specs,
                scratch_shapes=scratch,
            ),
            out_shape=outs,
            compiler_params=params(),
            cost_estimate=pl.CostEstimate(flops=weight, bytes_accessed=weight, transcendentals=0),
            name=name,
        )(*args, *waits)
        previous[:] = made[-1:]
        return made

    def call(body, name, outs, args, after=(), scalars=0):
        in_specs = [smem()] * scalars + vmem(len(args) - scalars)
        return run(body, name, outs, args, in_specs, vmem(len(outs)), after)

    def fence(after):
        call(fence_kernel, "fence", [shape(8, 128, dtype=F32)], [], after)

    near_z = range(1, nz - 1)
    meta, *made = call(
        functools.partial(prep_kernel, n, nx, cap),
        "prep",
        [shape(2 * n, toks)]
        + [shape(nx * cap, wide)] * (nz - 2)
        + [shape(cap, wide)] * nx
        + [shape(cap, d)]
        + [shape(cap, wide)] * (nx - 1)
        + [shape(nz * cap, d)] * (nx - 1),
        [me_arr, ids_t, gates_t, tokens, cotangent],
        scalars=1,
    )
    x_near, x_far, made = made[: nz - 2], made[nz - 2 : nz - 2 + nx], made[nz - 2 + nx :]
    x_own, x_side, y_side = made[0], made[1:nx], made[nx:]
    x_near = [swap(v, zk * nx) for zk, v in zip(near_z, x_near)]
    x_far = [swap(v, n - nx + xo) for xo, v in enumerate(x_far)]
    y_side = [swap(v, xo) for xo, v in enumerate(y_side, 1)]
    made = call(
        functools.partial(second_kernel, n, nx, cap),
        "second",
        [shape(cap, d)]
        + [shape(nx * cap, d)] * (nz - 1)
        + [shape((nz - 1) * cap, wide)] * (nx - 1),
        [meta, cotangent, *y_side, *x_side, *x_near],
    )
    y_own, y_late = made[0], made[1]
    x_side = [swap(v, xo) for xo, v in enumerate(made[nz:], 1)]
    y_z = [swap(made[zk], zk * nx) for zk in range(2, nz)]
    got_x = [x_own, *x_near, *x_side, *x_far]
    fence(x_far)

    tile = 256
    steps = h // tile
    whole = lambda shape: pl.BlockSpec(shape, lambda i: (0,) * len(shape))
    column = pl.BlockSpec((rows, tile), lambda i: (0, i))
    *x_parts, hidden, pa, pb, y_late, metas = run(
        functools.partial(forward_kernel, n, nx, cap, len(got_x), ny),
        "forward",
        [shape(rows, 2 * block)] * ny
        + [shape(rows, h), shape(rows, h, dtype=F32), shape(rows, h, dtype=F32)]
        + [shape(nx * cap, d), shape(n, 2 * n, toks)],
        [my_y, *got_x, meta, gate_w, up_w, y_late],
        [smem()]
        + [whole(v.shape) for v in got_x]
        + [whole((2 * n, toks))]
        + [pl.BlockSpec((1, d, tile), lambda i: (0, 0, i))] * 2
        + [whole((nx * cap, d))],
        [whole((rows, 2 * block))] * ny
        + [column] * 3
        + [whole((nx * cap, d)), whole((n, 2 * n, toks))],
        grid=(steps,),
        scratch=[pltpu.VMEM((rows, 128), F32), pltpu.VMEM((rows, d), BF16)],
        weight=1,
    )
    x_parts = [x_parts[0]] + [swap_dp(v, 2 * yo) for yo, v in enumerate(x_parts[1:], 1)]
    y_late = swap(y_late, nx)
    fence(y_z)
    got_y = [y_own, y_late, *y_z, *y_side]

    grads, score = run(
        functools.partial(back_kernel, n, nx, cap, len(got_y)),
        "back",
        [shape(2, rows, h), shape(16, rows)],
        [*got_y, hidden, pa, pb, down_w],
        [whole(v.shape) for v in got_y]
        + [column] * 3
        + [pl.BlockSpec((1, tile, d), lambda i: (0, i, 0))],
        [pl.BlockSpec((2, rows, tile), lambda i: (0, 0, i)), whole((16, rows))],
        grid=(steps,),
        scratch=[pltpu.VMEM((rows, d), BF16), pltpu.VMEM((rows, 128), F32)],
        weight=1,
    )
    g_parts = [grads] + [swap_dp(grads, 2 * yo) for yo in range(1, ny)]

    def rowgrads(places, outs, after=(), weight=1):
        dest = jnp.array([k for k, _, _ in places], jnp.int32) ^ me
        spec = pl.BlockSpec((1, feats, h), lambda i, dest_ref: (0, dest_ref[i], 0))
        fixed = lambda dims: pl.BlockSpec(dims, lambda i, dest_ref: (0,) * len(dims))
        return run(
            functools.partial(rowgrad_kernel, [(out, at) for _, out, at in places]),
            "rowgrad",
            [shape(size * many, rows) for many in outs],
            [dest, grads, score, gate_w, up_w],
            [fixed((2, rows, h)), fixed((16, rows)), spec, spec],
            [fixed((size * many, rows)) for many in outs],
            after,
            grid=(len(places),),
            scalars=1,
            weight=weight,
        )

    far = list(range(n - nx, n))
    mids = list(range(2 * nx, n - nx))
    now, held = mids[len(mids) // 2 :], mids[: len(mids) // 2]
    sent = rowgrads([(k, i, 0) for i, k in enumerate(far)], [1] * nx)
    early = [swap(v, k) for k, v in zip(far, sent)]
    *sent, near = rowgrads(
        [(k, i, 0) for i, k in enumerate(now)]
        + [(nx + xo, len(now), xo * size) for xo in range(nx)],
        [1] * len(now) + [nx],
        x_parts[1:],
    )
    near = swap(near, nx)
    middle = [swap(v, k) for k, v in zip(now, sent)]
    own, *sent = rowgrads(
        [(k, i, 0) for i, k in enumerate([0, *range(1, nx), *held])],
        [1] * (nx + len(held)),
        weight=LONG,
    )
    late = [swap(v, k) for k, v in zip(held, sent[nx - 1 :])]
    g_stack, x_keep, x_send = call(
        functools.partial(stack_kernel, ny),
        "stack",
        [shape(ny, 2, rows, h)] + [shape(ny, rows, block)] * 2,
        [my_core, *g_parts, *x_parts],
        early,
        scalars=1,
    )
    g_stack, x_came = swap_dp(g_stack, 1), swap_dp(x_send, 1)

    sent = call(
        functools.partial(second_back_kernel, nx, size),
        "second_back",
        [shape(2 * size, rows)] * (nx - 1),
        [near, *sent[: nx - 1]],
    )
    columns = [swap(v, xo) for xo, v in enumerate(sent, 1)]

    def combine(parts, refs, carried, outs):
        return call(
            functools.partial(combine_kernel, n, cap, feats, parts, bool(carried)),
            "combine",
            outs,
            [me_arr, ids_t, metas, *refs, *carried],
            scalars=1,
        )

    parts = [(0, 0, 0), (nx, 1, 0)] + [(k, i, 0) for i, k in enumerate(far + now, 2)]
    sums = combine(
        parts,
        [own, near, *early, *middle],
        [],
        [shape(feats, n * toks, dtype=F32), shape(2, 16, toks, dtype=F32)],
    )

    tile_w = 256
    out_spec = pl.BlockSpec((1, block, tile_w), lambda i: (0, 0, i))
    grad_gate_w, grad_up_w = run(
        functools.partial(weights_kernel, ndp),
        "weights",
        [shape(1, block, h)] * 2,
        [x_keep, x_came, *g_parts, g_stack],
        [whole((ny, rows, block))] * 2
        + [pl.BlockSpec((2, rows, tile_w), lambda i: (0, 0, i))] * ny
        + [pl.BlockSpec((ny, 2, rows, tile_w), lambda i: (0, 0, 0, i))],
        [out_spec, out_spec],
        grid=(h // tile_w,),
    )

    parts = [(k, i, 0) for i, k in enumerate(held)]
    for xo in range(1, nx):
        ref = len(parts) if xo == 1 else ref + 1
        parts = parts + [(xo, ref, 0), (nx + xo, ref, size)]
    summed, gg = combine(
        parts,
        [*late, *columns],
        sums,
        [shape(feats, n * toks), shape(2, toks)],
    )
    return summed.T, grad_gate_w, grad_up_w, gg.T


def solution(mesh):
    placed = (
        P(("dp", "expert"), None),
        P(("dp", "expert"), None),
        P(("dp", "expert"), None),
        P(("dp", "expert"), None),
        P("expert", None, None),
        P("expert", None, None),
        P("expert", None, None),
    )
    return jax.shard_map(
        local,
        mesh=mesh,
        in_specs=placed,
        out_specs=(
            P("dp", "expert"),
            P("expert", "dp", None),
            P("expert", "dp", None),
            P(("dp", "expert"), None),
        ),
        check_vma=False,
    )
```

time: 304 us -> 228 us (0.75)
  waiting for transfers between devices: 189 us -> 101 us
  Pallas kernels: 53 us -> 73.4 us
  starting transfers between devices: 51 us -> 45.6 us
    ppermute x6 -> x4, waiting for transfers between devices: 45.1 us -> 0.01 us  [swap_dp(): return lax.ppermute(v, 'dp', [(i, i ^ q) for i in range(ndp)])]
    ppermute x28 -> x15, waiting for transfers between devices: 144 us -> 101 us  [swap(): return lax.ppermute(v, 'expert', [(i, i ^ k) for i in range(n)])]
    pallas_call x9 -> x14, Pallas kernels: 53 us -> 73.4 us  [run(): pl.pallas_call(trimmed, grid_spec=pltpu.PrefetchScalarGridSpec(num_scalar...]
    ppermute x28 -> x15, starting transfers between devices: 46.7 us -> 42.6 us  [swap(): return lax.ppermute(v, 'expert', [(i, i ^ k) for i in range(n)])]
    unnamed x28 -> x34, local copies, waits for them, and re-layouts: 7.89 us -> 7.47 us
  transfers between devices with their start and end apart: 34 -> 19, of which waited for: 18 -> 7; matrix products, arithmetic and copies ran while one was open for 1% -> 0% of each run, Pallas kernels for 11% -> 29%
where the time goes in v2:
time: 228 us
  waiting for transfers between devices  101 us (44%)
  Pallas kernels  73.4 us (32%)
  starting transfers between devices  45.6 us (20%)
  local copies, waits for them, and re-layouts  7.47 us (3%)
    ppermute x15, waiting for transfers between devices, swap(): return lax.ppermute(v, 'expert', [(i, i ^ k) for i in range(n)])  101 us
    pallas_call x14, Pallas kernels, run(): pl.pallas_call(trimmed, grid_spec=pltpu.PrefetchScalarGridSpec(num_scalar...  73.4 us
    ppermute x15, starting transfers between devices, swap(): return lax.ppermute(v, 'expert', [(i, i ^ k) for i in range(n)])  42.6 us
    unnamed x34, local copies, waits for them, and re-layouts  7.47 us
  transfers between devices with their start and end apart: 19, of which 7 were waited for; matrix products, arithmetic and copies ran while one was open for 0% of the time, Pallas kernels for 29%

profile of v2, /device:TPU:0, one launch (start us, length us, event | category | flops | bytes accessed | tf_op | source)
XLA Modules:
  0.0 227.9 jit_solution(11166660264122408369)
XLA Ops:
  0.6 1.2 copy-done.3
  1.8 1.2 copy-done.4
  3.0 0.7 copy-done.9
  3.7 0.7 copy-done.12
  4.3 3.0 %prep.1 = (bf16[16,128]{1,0:T(8,128)(2,1)S(1)}, bf16[96,3712]{1,0:T(8,128)(2,1)}, bf16[96,3712]{1,0:T(8,128)(2,1)}, bf16[48,3712]{1,0:T(8,128)(2,1)}, bf16[48,37...) custom-call(s32[1]{0:T(128)} %bitcast.refs_0_, ...), custom_call_target="tpu_custom_call" | custom-call | flops 1099511627776 | bytes 1099511627776 | tf_op jit(solution)/shard_map/prep/pallas_call | solution.py:301
  7.3 2.9 %collective-permute-start.2 = (bf16[192,3584]{1,0:T(8,128)(2,1)}, bf16[192,3584]{1,0:T(8,128)(2,1)S(1)}, u32[]{:S(2)}, u32[]{:S(2)}) collective-permute-start(bf16[192,3584]{1,0:T(8,128)(2,1)} %get-tuple-element.46.refs_6_), channel_id=1, source_target_pairs={{0,1},{1,0},{2,3},{3,2},{4,5},{5,4},{6,7},{7,6},{8,9},{9,8},{10,11... | collective-permute-start | bytes 4128776 | tf_op jit(solution)/shard_map/ppermute | solution.py:284
  10.3 1.6 collective-permute-start
  11.8 2.6 %collective-permute-start.1 = (bf16[96,3712]{1,0:T(8,128)(2,1)}, bf16[96,3712]{1,0:T(8,128)(2,1)S(1)}, u32[]{:S(2)}, u32[]{:S(2)}) collective-permute-start(bf16[96,3712]{1,0:T(8,128)(2,1)} %get-tuple-element.44), channel_id=1, source_target_pairs={{0,4},{1,5},{2,6},{3,7},{4,0},{5,1},{6,2},{7,3},{8,12},{9,13},{10,... | collective-permute-start | bytes 2138120 | tf_op jit(solution)/shard_map/ppermute | solution.py:284
  14.4 0.2 collective-permute-start.4
  14.7 3.6 %collective-permute-start.5 = (bf16[48,3712]{1,0:T(8,128)(2,1)}, bf16[48,3712]{1,0:T(8,128)(2,1)}, u32[]{:S(2)}, u32[]{:S(2)}) collective-permute-start(bf16[48,3712]{1,0:T(8,128)(2,1)} %get-tuple-element.50), channel_id=1, source_target_pairs={{0,7},{1,6},{2,5},{3,4},{4,3},{5,2},{6,1},{7,0},{8,15},{9,14},{10,... | collective-permute-start | bytes 1069064 | tf_op jit(solution)/shard_map/ppermute | solution.py:284
  18.3 24.0 %collective-permute-done.refs_4_.refs_2_ = bf16[96,3712]{1,0:T(8,128)(2,1)S(1)} collective-permute-done((bf16[96,3712]{1,0:T(8,128)(2,1)}, bf16[96,3712]{1,0:T(8,128)(2,1)S(1)}, u32[]{:S(2)}, u32[]{:S(2)}) %collective-permute-start) | collective-permute-done | bytes 712736 | tf_op jit(solution)/shard_map/ppermute | solution.py:284
  42.3 34.9 %collective-permute-done.1.refs_5_.refs_3_ = bf16[96,3712]{1,0:T(8,128)(2,1)S(1)} collective-permute-done((bf16[96,3712]{1,0:T(8,128)(2,1)}, bf16[96,3712]{1,0:T(8,128)(2,1)S(1)}, u32[]{:S(2)}, u32[]{:S(2)}) %collective-permute-start.1) | collective-permute-done | bytes 712736 | tf_op jit(solution)/shard_map/ppermute | solution.py:284
  77.2 0.0 collective-permute-done.2.refs_2_.refs_4_
  77.2 1.1 copy-done
  78.2 1.2 copy-done.5
  79.4 3.4 %second.1 = (bf16[48,3584]{1,0:T(8,128)(2,1)S(1)}, bf16[96,3584]{1,0:T(8,128)(2,1)S(1)}, bf16[96,3584]{1,0:T(8,128)(2,1)}, bf16[96,3584]{1,0:T(8,128)(2,1)}, bf16[144,3712]{1,0:T(8,128)(2,1)}) custom-call(bf16[16,128]{1,0:T(8,128)(2,1)S(1)} %get-tuple-element.45.refs_0_.refs_7_, bf16[128,3584]{1,0:T(8,128)(2,1)S(1)} %copy-done.5, bf16[192,3584]{1,0:T(8,128)(2,1)} %copy-done, ...), custom_call_target="tpu_custom_call" | custom-call | flops 1099511627776 | bytes 1099511627776 | tf_op jit(solution)/shard_map/second/pallas_call | solution.py:301
  82.8 0.0 collective-permute-start.7
  82.8 2.5 %collective-permute-start.8 = (bf16[96,3584]{1,0:T(8,128)(2,1)}, bf16[96,3584]{1,0:T(8,128)(2,1)}, u32[]{:S(2)}, u32[]{:S(2)}) collective-permute-start(bf16[96,3584]{1,0:T(8,128)(2,1)} %get-tuple-element.56), channel_id=1, source_target_pairs={{0,6},{1,7},{2,4},{3,5},{4,2},{5,3},{6,0},{7,1},{8,14},{9,15},{10,... | collective-permute-start | bytes 2064392 | tf_op jit(solution)/shard_map/ppermute | solution.py:284
  85.3 0.5 collective-permute-start.3
  85.8 0.0 collective-permute-done.4.refs_0_.refs_5_
  85.8 0.0 collective-permute-done.5.refs_1_.refs_6_
  85.8 14.8 %collective-permute-done.3.refs_4_ = bf16[144,3712]{1,0:T(8,128)(2,1)} collective-permute-done((bf16[144,3712]{1,0:T(8,128)(2,1)}, bf16[144,3712]{1,0:T(8,128)(2,1)}, u32[]{:S(2)}, u32[]{:S(2)}) %collective-permute-start.3) | collective-permute-done | bytes 1069088 | tf_op jit(solution)/shard_map/ppermute | solution.py:284
  100.6 11.7 %forward.1 = (bf16[384,1792]{1,0:T(8,128)(2,1)}, bf16[384,1792]{1,0:T(8,128)(2,1)}, bf16[384,1024]{1,0:T(8,128)(2,1)S(1)}, f32[384,1024]{1,0:T(8,128)}, f32[384,...) custom-call(s32[1]{0:T(128)} %bitcast.2.refs_0_, ...), custom_call_target="tpu_custom_call" | custom-call | flops 1 | bytes 1 | tf_op jit(solution)/shard_map/forward/pallas_call | solution.py:301
  112.3 7.3 %collective-permute-start.6 = (bf16[96,3584]{1,0:T(8,128)(2,1)}, bf16[96,3584]{1,0:T(8,128)(2,1)}, u32[]{:S(2)}, u32[]{:S(2)}) collective-permute-start(bf16[96,3584]{1,0:T(8,128)(2,1)} %get-tuple-element.54), channel_id=1, source_target_pairs={{0,2},{1,3},{2,0},{3,1},{4,6},{5,7},{6,4},{7,5},{8,10},{9,11},{10,... | collective-permute-start | bytes 2064392 | tf_op jit(solution)/shard_map/ppermute | solution.py:284
  119.6 1.5 collective-permute-start.9
  121.1 0.9 collective-permute-done.7.refs_0_.refs_2_
  122.0 13.0 %collective-permute-done.6.refs_1_ = bf16[96,3584]{1,0:T(8,128)(2,1)} collective-permute-done((bf16[96,3584]{1,0:T(8,128)(2,1)}, bf16[96,3584]{1,0:T(8,128)(2,1)}, u32[]{:S(2)}, u32[]{:S(2)}) %collective-permute-start.6) | collective-permute-done | bytes 688160 | tf_op jit(solution)/shard_map/ppermute | solution.py:284
  135.1 8.4 %back.1 = (bf16[2,384,1024]{2,1,0:T(8,128)(2,1)}, bf16[16,384]{1,0:T(8,128)(2,1)S(1)}) custom-call(bf16[48,3584]{1,0:T(8,128)(2,1)S(1)} %get-tuple-element.53.refs_0_, bf16[96,3584]{1,0:T(8,128)(2,1)} %collective-permute-done.6.refs_1_, bf16[96,3584]{1,0:T(8,128)(2,1)} %collective-permute-done.7.refs_0_.refs_2_, ...), custom_call_target="tpu_custom_call" | custom-call | flops 1 | bytes 1 | tf_op jit(solution)/shard_map/back/pallas_call | solution.py:301
  143.4 1.5 collective-permute-start.12
  145.0 5.8 %rowgrad.3 = (bf16[464,384]{1,0:T(8,128)(2,1)}, bf16[464,384]{1,0:T(8,128)(2,1)}) custom-call(s32[2]{0:T(128)S(1)} %broadcast_xor_fusion.refs_0_, bf16[2,384,1024]{2,1,0:T(8,128)(2,1)} %get-tuple-element.60.refs_1_.refs_2_, bf16[16,384]{1,0:T(8,128)(2,1)S(1)} %get-tuple-element.61.refs_2_.refs_5_, bf16[1,3584,1024]{2,1,0:T(8,128)(2,1)} %refs_3_.7, ...), custom_call_target="tpu_custom_call" | custom-call | flops 1 | bytes 1 | tf_op jit(solution)/shard_map/rowgrad/pallas_call | solution.py:301
  150.7 2.5 %collective-permute-start.13 = (bf16[464,384]{1,0:T(8,128)(2,1)}, bf16[464,384]{1,0:T(8,128)(2,1)}, u32[]{:S(2)}, u32[]{:S(2)}) collective-permute-start(bf16[464,384]{1,0:T(8,128)(2,1)} %get-tuple-element.68), channel_id=1, source_target_pairs={{0,6},{1,7},{2,4},{3,5},{4,2},{5,3},{6,0},{7,1},{8,14},{9,15},{10,... | collective-permute-start | bytes 1069064 | tf_op jit(solution)/shard_map/ppermute | solution.py:284
  153.2 1.3 collective-permute-start.14
  154.5 7.3 %rowgrad.4 = (bf16[464,384]{1,0:T(8,128)(2,1)}, bf16[928,384]{1,0:T(8,128)(2,1)}) custom-call(s32[3]{0:T(128)S(1)} %get-tuple-element.80.refs_0_, bf16[2,384,1024]{2,1,0:T(8,128)(2,1)} %get-tuple-element.60.refs_1_.refs_2_, bf16[16,384]{1,0:T(8,128)(2,1)S(1)} %get-tuple-element.61.refs_2_.refs_5_, bf16[1,3584,1024]{2,1,0:T(8,128)(2,1)} %refs_3_.7, ...), custom_call_target="tpu_custom_call" | custom-call | flops 1 | bytes 1 | tf_op jit(solution)/shard_map/rowgrad/pallas_call | solution.py:301
  161.9 2.0 collective-permute-start.16
  163.9 1.9 collective-permute-start.11
  165.8 7.1 %rowgrad.5 = (bf16[464,384]{1,0:T(8,128)(2,1)S(1)}, bf16[464,384]{1,0:T(8,128)(2,1)S(1)}, bf16[464,384]{1,0:T(8,128)(2,1)}) custom-call(s32[3]{0:T(128)S(1)} %get-tuple-element.81.refs_0_, bf16[2,384,1024]{2,1,0:T(8,128)(2,1)} %get-tuple-element.60.refs_1_.refs_2_, bf16[16,384]{1,0:T(8,128)(2,1)S(1)} %get-tuple-element.61.refs_2_.refs_5_, ...), custom_call_target="tpu_custom_call" | custom-call | flops 1099511627776 | bytes 1099511627776 | tf_op jit(solution)/shard_map/rowgrad/pallas_call | solution.py:301
  172.9 13.1 %collective-permute-start.10 = (bf16[464,384]{1,0:T(8,128)(2,1)}, bf16[464,384]{1,0:T(8,128)(2,1)}, u32[]{:S(2)}, u32[]{:S(2)}) collective-permute-start(bf16[464,384]{1,0:T(8,128)(2,1)} %get-tuple-element.65.refs_7_), channel_id=1, source_target_pairs={{0,4},{1,5},{2,6},{3,7},{4,0},{5,1},{6,2},{7,3},{8,12},{9,13},{10,... | collective-permute-start | bytes 1069064 | tf_op jit(solution)/shard_map/ppermute | solution.py:284
  186.0 5.0 %stack.1 = (bf16[2,2,384,1024]{3,2,1,0:T(8,128)(2,1)}, bf16[2,384,896]{2,1,0:T(8,128)(2,1)S(1)}, bf16[2,384,896]{2,1,0:T(8,128)(2,1)}) custom-call(s32[1]{0:T(128)} %bitcast.4.refs_0_, bf16[2,384,1024]{2,1,0:T(8,128)(2,1)} %get-tuple-element.60.refs_1_.refs_2_, bf16[2,384,1024]{2,1,0:T(8,128)(2,1)} %collective-permute-done.12.refs_2_.refs_3_, ...), custom_call_target="tpu_custom_call" | custom-call | flops 1099511627776 | bytes 1099511627776 | tf_op jit(solution)/shard_map/stack/pallas_call | solution.py:301
  191.0 1.9 collective-permute-done.11.refs_0_.refs_4_
  192.9 2.0 second_back.1.refs_8_
  194.9 0.6 collective-permute-start.15
  195.5 11.1 %collective-permute-done.16.refs_7_ = bf16[464,384]{1,0:T(8,128)(2,1)} collective-permute-done((bf16[464,384]{1,0:T(8,128)(2,1)}, bf16[464,384]{1,0:T(8,128)(2,1)}, u32[]{:S(2)}, u32[]{:S(2)}) %collective-permute-start.16) | collective-permute-done | bytes 356384 | tf_op jit(solution)/shard_map/ppermute | solution.py:284
  206.6 4.1 %combine.2 = (f32[448,1024]{1,0:T(8,128)S(1)}, f32[2,16,128]{2,1,0:T(8,128)S(1)}) custom-call(s32[1]{0:T(128)} %bitcast.refs_0_, s32[2,128]{1,0:T(2,128)S(1)} %bitcast.8, bf16[8,16,128]{2,1,0:T(8,128)(2,1)S(1)} %copy-done.7, bf16[464,384]{1,0:T(8,128)(2,1)S(1)} %get-tuple-element.70.refs_3_, bf16[928,384]{1,0:T(8,128)(2,1)} %collective-permute-done.11.refs_0_.refs_4_, ...), custom_call_target="tpu_custom_call" | custom-call | flops 1099511627776 | bytes 1099511627776 | tf_op jit(solution)/shard_map/combine/pallas_call | solution.py:301
  210.8 0.0 copy-start.11
  210.8 11.5 %weights.1 = (bf16[1,896,1024]{2,1,0:T(8,128)(2,1)}, bf16[1,896,1024]{2,1,0:T(8,128)(2,1)}) custom-call(bf16[2,384,896]{2,1,0:T(8,128)(2,1)S(1)} %get-tuple-element.74.refs_0_, bf16[2,384,896]{2,1,0:T(8,128)(2,1)} %collective-permute-done.17.refs_1_, bf16[2,384,1024]{2,1,0:T(8,128)(2,1)} %get-tuple-element.60.refs_1_.refs_2_, ...), custom_call_target="tpu_custom_call" | custom-call | flops 1099511627776 | bytes 1099511627776 | tf_op jit(solution)/shard_map/weights/pallas_call | solution.py:301
  222.3 0.0 copy-start.13
  222.3 1.5 copy-done.13
  223.8 4.1 %combine.3 = (bf16[448,1024]{1,0:T(8,128)(2,1)}, bf16[2,128]{1,0:T(2,128)(2,1)}) custom-call(s32[1]{0:T(128)} %bitcast.refs_0_, s32[2,128]{1,0:T(2,128)S(1)} %bitcast.9, bf16[8,16,128]{2,1,0:T(8,128)(2,1)S(1)} %copy-done.8, bf16[464,384]{1,0:T(8,128)(2,1)} %collective-permute-done.10.refs_3_, bf16[928,384]{1,0:T(8,128)(2,1)} %collective-permute-done.15.refs_4_, ...), custom_call_target="tpu_custom_call" | custom-call | flops 1099511627776 | bytes 1099511627776 | tf_op jit(solution)/shard_map/combine/pallas_call | solution.py:301
  (40 shorter events, 0.1 us)
Async XLA Ops:
  0.6 1.2 copy-start.3
  1.8 1.2 copy-start.4
  3.0 0.7 copy-start.9
  3.7 0.7 copy-start.12
  4.3 13.9 %copy-start.16 = (s32[2]{0:T(128)S(1)}, s32[2]{0:T(128)}, u32[]{:S(2)}) copy-start(s32[2]{0:T(128)} %constant.38.clone) | copy-start | bytes 28
  4.3 13.9 %copy-start.14 = (s32[3]{0:T(128)S(1)}, s32[3]{0:T(128)}, u32[]{:S(2)}) copy-start(s32[3]{0:T(128)} %constant.40.clone) | copy-start | bytes 40
  4.3 13.9 %copy-start.15 = (s32[3]{0:T(128)S(1)}, s32[3]{0:T(128)}, u32[]{:S(2)}) copy-start(s32[3]{0:T(128)} %constant.39.clone) | copy-start | bytes 40
  7.3 69.8 %collective-permute-start.2 = (bf16[192,3584]{1,0:T(8,128)(2,1)}, bf16[192,3584]{1,0:T(8,128)(2,1)S(1)}, u32[]{:S(2)}, u32[]{:S(2)}) collective-permute-start(bf16[192,3584]{1,0:T(8,128)(2,1)} %get-tuple-element.46.refs_6_), channel_id=1, source_target_pairs={{0,1},{1,0},{2,3},{3,2},{4,5},{5,4},{6,7},{7,6},{8,9},{9,8},{10,11... | collective-permute-start | bytes 4128776 | tf_op jit(solution)/shard_map/ppermute | solution.py:284
  10.3 32.0 %collective-permute-start = (bf16[96,3712]{1,0:T(8,128)(2,1)}, bf16[96,3712]{1,0:T(8,128)(2,1)S(1)}, u32[]{:S(2)}, u32[]{:S(2)}) collective-permute-start(bf16[96,3712]{1,0:T(8,128)(2,1)} %get-tuple-element.43), channel_id=1, source_target_pairs={{0,2},{1,3},{2,0},{3,1},{4,6},{5,7},{6,4},{7,5},{8,10},{9,11},{10,... | collective-permute-start | bytes 2138120 | tf_op jit(solution)/shard_map/ppermute | solution.py:284
  11.8 65.3 %collective-permute-start.1 = (bf16[96,3712]{1,0:T(8,128)(2,1)}, bf16[96,3712]{1,0:T(8,128)(2,1)S(1)}, u32[]{:S(2)}, u32[]{:S(2)}) collective-permute-start(bf16[96,3712]{1,0:T(8,128)(2,1)} %get-tuple-element.44), channel_id=1, source_target_pairs={{0,4},{1,5},{2,6},{3,7},{4,0},{5,1},{6,2},{7,3},{8,12},{9,13},{10,... | collective-permute-start | bytes 2138120 | tf_op jit(solution)/shard_map/ppermute | solution.py:284
  14.4 71.4 %collective-permute-start.4 = (bf16[48,3712]{1,0:T(8,128)(2,1)}, bf16[48,3712]{1,0:T(8,128)(2,1)}, u32[]{:S(2)}, u32[]{:S(2)}) collective-permute-start(bf16[48,3712]{1,0:T(8,128)(2,1)} %get-tuple-element.49), channel_id=1, source_target_pairs={{0,6},{1,7},{2,4},{3,5},{4,2},{5,3},{6,0},{7,1},{8,14},{9,15},{10,... | collective-permute-start | bytes 1069064 | tf_op jit(solution)/shard_map/ppermute | solution.py:284
  14.7 71.1 %collective-permute-start.5 = (bf16[48,3712]{1,0:T(8,128)(2,1)}, bf16[48,3712]{1,0:T(8,128)(2,1)}, u32[]{:S(2)}, u32[]{:S(2)}) collective-permute-start(bf16[48,3712]{1,0:T(8,128)(2,1)} %get-tuple-element.50), channel_id=1, source_target_pairs={{0,7},{1,6},{2,5},{3,4},{4,3},{5,2},{6,1},{7,0},{8,15},{9,14},{10,... | collective-permute-start | bytes 1069064 | tf_op jit(solution)/shard_map/ppermute | solution.py:284
  77.2 1.1 copy-start
  78.2 1.2 copy-start.5
  82.8 39.2 %collective-permute-start.7 = (bf16[96,3584]{1,0:T(8,128)(2,1)}, bf16[96,3584]{1,0:T(8,128)(2,1)}, u32[]{:S(2)}, u32[]{:S(2)}) collective-permute-start(bf16[96,3584]{1,0:T(8,128)(2,1)} %get-tuple-element.55), channel_id=1, source_target_pairs={{0,4},{1,5},{2,6},{3,7},{4,0},{5,1},{6,2},{7,3},{8,12},{9,13},{10,... | collective-permute-start | bytes 2064392 | tf_op jit(solution)/shard_map/ppermute | solution.py:284
  82.8 39.2 %collective-permute-start.8 = (bf16[96,3584]{1,0:T(8,128)(2,1)}, bf16[96,3584]{1,0:T(8,128)(2,1)}, u32[]{:S(2)}, u32[]{:S(2)}) collective-permute-start(bf16[96,3584]{1,0:T(8,128)(2,1)} %get-tuple-element.56), channel_id=1, source_target_pairs={{0,6},{1,7},{2,4},{3,5},{4,2},{5,3},{6,0},{7,1},{8,14},{9,15},{10,... | collective-permute-start | bytes 2064392 | tf_op jit(solution)/shard_map/ppermute | solution.py:284
  85.3 15.3 %collective-permute-start.3 = (bf16[144,3712]{1,0:T(8,128)(2,1)}, bf16[144,3712]{1,0:T(8,128)(2,1)}, u32[]{:S(2)}, u32[]{:S(2)}) collective-permute-start(bf16[144,3712]{1,0:T(8,128)(2,1)} %get-tuple-element.48.refs_2_), channel_id=1, source_target_pairs={{0,1},{1,0},{2,3},{3,2},{4,5},{5,4},{6,7},{7,6},{8,9},{9,8},{10,11... | collective-permute-start | bytes 3207176 | tf_op jit(solution)/shard_map/ppermute | solution.py:284
  112.3 9.7 %copy-start.6 = (bf16[8,16,128]{2,1,0:T(8,128)(2,1)}, bf16[8,16,128]{2,1,0:T(8,128)(2,1)S(1)}, u32[]{:S(2)}) copy-start(bf16[8,16,128]{2,1,0:T(8,128)(2,1)S(1)} %get-tuple-element.52.refs_2_) | copy-start | bytes 98308
  112.3 22.7 %collective-permute-start.6 = (bf16[96,3584]{1,0:T(8,128)(2,1)}, bf16[96,3584]{1,0:T(8,128)(2,1)}, u32[]{:S(2)}, u32[]{:S(2)}) collective-permute-start(bf16[96,3584]{1,0:T(8,128)(2,1)} %get-tuple-element.54), channel_id=1, source_target_pairs={{0,2},{1,3},{2,0},{3,1},{4,6},{5,7},{6,4},{7,5},{8,10},{9,11},{10,... | collective-permute-start | bytes 2064392 | tf_op jit(solution)/shard_map/ppermute | solution.py:284
  119.6 34.9 %collective-permute-start.9 = (bf16[384,1792]{1,0:T(8,128)(2,1)}, bf16[384,1792]{1,0:T(8,128)(2,1)}, u32[]{:S(2)}, u32[]{:S(2)}) collective-permute-start(bf16[384,1792]{1,0:T(8,128)(2,1)} %get-tuple-element.62), channel_id=1, source_target_pairs={{0,16},{8,24},{16,0},{24,8},{1,17},{9,25},{17,1},{25,9},{2,18},{10... | collective-permute-start | bytes 4128776 | tf_op jit(solution)/shard_map/ppermute | solution.py:287
  122.0 13.0 %copy-start.1 = (bf16[192,3584]{1,0:T(8,128)(2,1)S(1)}, bf16[192,3584]{1,0:T(8,128)(2,1)}, u32[]{:S(2)}) copy-start(bf16[192,3584]{1,0:T(8,128)(2,1)} %copy-done) | copy-start | bytes 4128772
  143.4 42.6 %collective-permute-start.12 = (bf16[2,384,1024]{2,1,0:T(8,128)(2,1)}, bf16[2,384,1024]{2,1,0:T(8,128)(2,1)}, u32[]{:S(2)}, u32[]{:S(2)}) collective-permute-start(bf16[2,384,1024]{2,1,0:T(8,128)(2,1)} %get-tuple-element.60.refs_1_.refs_2_), channel_id=1, source_target_pairs={{0,16},{8,24},{16,0},{24,8},{1,17},{9,25},{17,1},{25,9},{2,18},{10... | collective-permute-start | bytes 4718600 | tf_op jit(solution)/shard_map/ppermute | solution.py:287
  150.7 22.2 %collective-permute-start.13 = (bf16[464,384]{1,0:T(8,128)(2,1)}, bf16[464,384]{1,0:T(8,128)(2,1)}, u32[]{:S(2)}, u32[]{:S(2)}) collective-permute-start(bf16[464,384]{1,0:T(8,128)(2,1)} %get-tuple-element.68), channel_id=1, source_target_pairs={{0,6},{1,7},{2,4},{3,5},{4,2},{5,3},{6,0},{7,1},{8,14},{9,15},{10,... | collective-permute-start | bytes 1069064 | tf_op jit(solution)/shard_map/ppermute | solution.py:284
  153.2 32.8 %collective-permute-start.14 = (bf16[464,384]{1,0:T(8,128)(2,1)}, bf16[464,384]{1,0:T(8,128)(2,1)}, u32[]{:S(2)}, u32[]{:S(2)}) collective-permute-start(bf16[464,384]{1,0:T(8,128)(2,1)} %get-tuple-element.63.refs_6_), channel_id=1, source_target_pairs={{0,7},{1,6},{2,5},{3,4},{4,3},{5,2},{6,1},{7,0},{8,15},{9,14},{10,... | collective-permute-start | bytes 1069064 | tf_op jit(solution)/shard_map/ppermute | solution.py:284
  161.9 44.8 %collective-permute-start.16 = (bf16[464,384]{1,0:T(8,128)(2,1)}, bf16[464,384]{1,0:T(8,128)(2,1)}, u32[]{:S(2)}, u32[]{:S(2)}) collective-permute-start(bf16[464,384]{1,0:T(8,128)(2,1)} %get-tuple-element.71), channel_id=1, source_target_pairs={{0,5},{1,4},{2,7},{3,6},{4,1},{5,0},{6,3},{7,2},{8,13},{9,12},{10,... | collective-permute-start | bytes 1069064 | tf_op jit(solution)/shard_map/ppermute | solution.py:284
  163.9 29.0 %collective-permute-start.11 = (bf16[928,384]{1,0:T(8,128)(2,1)}, bf16[928,384]{1,0:T(8,128)(2,1)}, u32[]{:S(2)}, u32[]{:S(2)}) collective-permute-start(bf16[928,384]{1,0:T(8,128)(2,1)} %get-tuple-element.64.refs_5_), channel_id=1, source_target_pairs={{0,2},{1,3},{2,0},{3,1},{4,6},{5,7},{6,4},{7,5},{8,10},{9,11},{10,... | collective-permute-start | bytes 2138120 | tf_op jit(solution)/shard_map/ppermute | solution.py:284
  165.8 20.2 %copy-start.2 = (bf16[384,1792]{1,0:T(8,128)(2,1)S(1)}, bf16[384,1792]{1,0:T(8,128)(2,1)}, u32[]{:S(2)}) copy-start(bf16[384,1792]{1,0:T(8,128)(2,1)} %get-tuple-element.67.refs_3_) | copy-start | bytes 4128772
  172.9 49.3 %collective-permute-start.10 = (bf16[464,384]{1,0:T(8,128)(2,1)}, bf16[464,384]{1,0:T(8,128)(2,1)}, u32[]{:S(2)}, u32[]{:S(2)}) collective-permute-start(bf16[464,384]{1,0:T(8,128)(2,1)} %get-tuple-element.65.refs_7_), channel_id=1, source_target_pairs={{0,4},{1,5},{2,6},{3,7},{4,0},{5,1},{6,2},{7,3},{8,12},{9,13},{10,... | collective-permute-start | bytes 1069064 | tf_op jit(solution)/shard_map/ppermute | solution.py:284
  191.0 19.7 %collective-permute-start.17 = (bf16[2,384,896]{2,1,0:T(8,128)(2,1)}, bf16[2,384,896]{2,1,0:T(8,128)(2,1)}, u32[]{:S(2)}, u32[]{:S(2)}) collective-permute-start(bf16[2,384,896]{2,1,0:T(8,128)(2,1)} %get-tuple-element.69.refs_2_), channel_id=1, source_target_pairs={{0,8},{8,0},{16,24},{24,16},{1,9},{9,1},{17,25},{25,17},{2,10},{10... | collective-permute-start | bytes 4128776 | tf_op jit(solution)/shard_map/ppermute | solution.py:287
  192.9 13.7 %copy-start.7 = (bf16[8,16,128]{2,1,0:T(8,128)(2,1)S(1)}, bf16[8,16,128]{2,1,0:T(8,128)(2,1)}, u32[]{:S(2)}) copy-start(bf16[8,16,128]{2,1,0:T(8,128)(2,1)} %copy-done.6) | copy-start | bytes 98308
  192.9 13.7 %copy-start.10 = (s32[128,2]{0,1:T(2,128)S(1)}, s32[128,2]{0,1:T(2,128)}, u32[]{:S(2)}) copy-start(s32[128,2]{0,1:T(2,128)} %param.13) | copy-start | bytes 3076
  194.9 27.4 %collective-permute-start.15 = (bf16[928,384]{1,0:T(8,128)(2,1)}, bf16[928,384]{1,0:T(8,128)(2,1)}, u32[]{:S(2)}, u32[]{:S(2)}) collective-permute-start(bf16[928,384]{1,0:T(8,128)(2,1)} %second_back.1.refs_8_), channel_id=1, source_target_pairs={{0,1},{1,0},{2,3},{3,2},{4,5},{5,4},{6,7},{7,6},{8,9},{9,8},{10,11... | collective-permute-start | bytes 2138120 | tf_op jit(solution)/shard_map/ppermute | solution.py:284
  195.5 15.3 %collective-permute-start.18 = (bf16[2,2,384,1024]{3,2,1,0:T(8,128)(2,1)}, bf16[2,2,384,1024]{3,2,1,0:T(8,128)(2,1)}, u32[]{:S(2)}, u32[]{:S(2)}) collective-permute-start(bf16[2,2,384,1024]{3,2,1,0:T(8,128)(2,1)} %get-tuple-element.75), channel_id=1, source_target_pairs={{0,8},{8,0},{16,24},{24,16},{1,9},{9,1},{17,25},{25,17},{2,10},{10... | collective-permute-start | bytes 9437192 | tf_op jit(solution)/shard_map/ppermute | solution.py:287
  210.8 11.5 %copy-start.8 = (bf16[8,16,128]{2,1,0:T(8,128)(2,1)S(1)}, bf16[8,16,128]{2,1,0:T(8,128)(2,1)}, u32[]{:S(2)}) copy-start(bf16[8,16,128]{2,1,0:T(8,128)(2,1)} %copy-done.6) | copy-start | bytes 98308
  210.8 11.5 %copy-start.11 = (s32[128,2]{0,1:T(2,128)S(1)}, s32[128,2]{0,1:T(2,128)}, u32[]{:S(2)}) copy-start(s32[128,2]{0,1:T(2,128)} %param.13) | copy-start | bytes 3076
  222.3 1.5 copy-start.13

commit v3 on v2

v3 whole, which is shorter than its diff:
```python
import functools

import jax
import jax.numpy as jnp
from jax import lax
from jax.experimental import pallas as pl
from jax.experimental.pallas import tpu as pltpu
from jax.sharding import PartitionSpec as P

F32 = jnp.float32
BF16 = jnp.bfloat16
NT = (((1,), (1,)), ((), ()))
TN = (((0,), (0,)), ((), ()))


def params(mib=48):
    return pltpu.CompilerParams(vmem_limit_bytes=mib << 20)


def vmem(count):
    return [pl.BlockSpec(memory_space=pltpu.VMEM)] * count


def smem():
    return pl.BlockSpec(memory_space=pltpu.SMEM)


LONG = 1 << 40


def pick_rows(cap, code, meta, tokens, dest):
    toks, d = tokens.shape
    slot = lax.broadcasted_iota(jnp.int32, (cap, toks), 0).astype(F32)
    for j, ref, at in dest:
        pick = (slot == code[j : j + 1, :]).astype(F32).astype(BF16)
        chosen = jnp.dot(pick, tokens, preferred_element_type=F32).astype(BF16)
        ref[at : at + cap, 0:d] = chosen
        if ref.shape[1] > d:
            add_routing(ref, at, cap, d, meta)


def add_routing(ref, at, count, d, meta):
    ref[at : at + count, d:] = jnp.zeros((count, meta.shape[1]), BF16)
    ref[at : at + meta.shape[0], d:] = meta


def prep_kernel(n, nx, cap, me_ref, *refs):
    sources, meta_ref, out_refs = refs[:4], refs[4], refs[5:-5]
    held, sems = refs[-5:-1], refs[-1]
    copies = [
        pltpu.make_async_copy(src, dst, sems.at[i])
        for i, (src, dst) in enumerate(zip(sources, held))
    ]
    for copy in copies:
        copy.start()
    ids_ref, gates_ref, tok_ref, cot_ref = held
    copies[0].wait()
    copies[1].wait()
    toks = tok_ref.shape[0]
    nz = n // nx
    expert = lax.broadcasted_iota(jnp.int32, (n, toks), 0) ^ me_ref[0]
    first = ids_ref[0:1, :] == expert
    second = ids_ref[1:2, :] == expert
    count = (first | second).astype(F32)
    before = (
        lax.broadcasted_iota(jnp.int32, (toks, toks), 0)
        < lax.broadcasted_iota(jnp.int32, (toks, toks), 1)
    ).astype(F32)
    position = jnp.dot(count.astype(BF16), before.astype(BF16), preferred_element_type=F32)
    code = jnp.where(first | second, position, -1.0)
    gates = gates_ref[...].astype(F32)
    weight = jnp.where(first, gates[0:1, :], 0.0) + jnp.where(second, gates[1:2, :], 0.0)
    meta = jnp.concatenate([code, weight], axis=0).astype(BF16)
    meta_ref[...] = meta
    near_ref, all_ref, rest, y_refs = out_refs[0], out_refs[1], out_refs[2 : 1 - nx], out_refs[1 - nx :]
    copies[2].wait()
    tokens = tok_ref[...]
    all_ref[:, 0 : tokens.shape[1]] = tokens
    add_routing(all_ref, 0, toks, tokens.shape[1], meta)
    near = [(nx + xo, near_ref, xo * cap) for xo in range(nx)]
    pick_rows(cap, code, meta, tokens, near + [(j, ref, 0) for j, ref in enumerate(rest)])
    by_column = [(zk * nx + xo, y_refs[xo - 1], zk * cap) for zk in range(nz) for xo in range(1, nx)]
    copies[3].wait()
    pick_rows(cap, code, meta, cot_ref[...], by_column)


def second_kernel(n, nx, cap, meta_ref, cot_ref, *refs):
    nz = n // nx
    came, y_refs = refs[: nx - 1], refs[nx - 1 :]
    meta = meta_ref[...]
    own = [(zk * nx, y_refs[zk], 0) for zk in range(nz)]
    pick_rows(cap, meta.astype(F32)[0:n, :], meta, cot_ref[...], own)
    for xo in range(1, nx):
        for zk in range(nz):
            y_refs[zk][xo * cap : (xo + 1) * cap, :] = came[xo - 1][zk * cap : (zk + 1) * cap, :]


def third_kernel(n, nx, cap, all_ref, near_ref, *refs):
    own, x_refs, here_ref, pass_refs = refs[: nx - 1], refs[nx - 1 : 2 * nx - 2], refs[2 * nx - 2], refs[2 * nx - 1 :]
    toks, wide = all_ref.shape
    meta = all_ref[0 : 2 * n, wide - toks :]
    dest = [(2 * nx, here_ref, 0)] + [(2 * nx + xo, x_refs[xo - 1], 2 * cap) for xo in range(1, nx)]
    dest += [(3 * nx + xo, pass_refs[xo], 0) for xo in range(nx)]
    pick_rows(cap, meta.astype(F32)[0:n, :], meta, all_ref[:, 0 : wide - toks], dest)
    for xo in range(1, nx):
        x_refs[xo - 1][0:cap, :] = own[xo - 1][...]
        x_refs[xo - 1][cap : 2 * cap, :] = near_ref[xo * cap : (xo + 1) * cap, :]


def found_x(n, nx, cap, refs):
    nz = n // nx
    z_refs, side_refs, far_refs = refs[: nz - 1], refs[nz - 1 : nz + nx - 2], refs[nz + nx - 2 :]
    found = []
    for zk in range(nz - 1):
        found += [(z_refs[zk], 0)] + [(side_refs[xo], zk * cap) for xo in range(nx - 1)]
    return found + [(ref, 0) for ref in far_refs]


def hold_kernel(in_ref, out_ref):
    out_ref[...] = in_ref[...]


def fence_kernel(out_ref):
    out_ref[...] = jnp.zeros_like(out_ref)


def forward_kernel(n, nx, cap, count, ny, place_ref, *refs):
    found = found_x(n, nx, cap, refs[:count])
    meta_ref, gate_ref, up_ref, *out_refs = refs[count:]
    part_refs, out_refs = out_refs[:ny], out_refs[ny:]
    hidden_ref, pa_ref, pb_ref, metas_ref, w_ref, rows_ref = out_refs
    toks = meta_ref.shape[1]
    d = rows_ref.shape[1]
    width = part_refs[0].shape[1]

    @pl.when(pl.program_id(0) == 0)
    def _():
        slot = lax.broadcasted_iota(jnp.int32, (cap, toks), 0).astype(F32)
        for j, (ref, at) in enumerate(found):
            row = j * cap
            rows_ref[row : row + cap, :] = ref[at : at + cap, 0:d]
            if j:
                metas_ref[j] = ref[at : at + 2 * n, d:]
            else:
                metas_ref[j] = meta_ref[...]
            meta = metas_ref[j].astype(F32)
            picked = jnp.where(slot == meta[j : j + 1, :], meta[n + j : n + j + 1, :], 0.0)
            total = jnp.sum(picked, axis=1, keepdims=True)
            w_ref[row : row + cap, :] = jnp.broadcast_to(total, (cap, w_ref.shape[1]))
        for yo, ref in enumerate(part_refs):
            at = pl.multiple_of((place_ref[0] ^ yo) * width, 128)
            ref[...] = rows_ref[:, pl.ds(at, width)]

    a = jnp.dot(rows_ref[...], gate_ref[0], preferred_element_type=F32)
    b = jnp.dot(rows_ref[...], up_ref[0], preferred_element_type=F32)
    w = w_ref[:, 0:1]
    sig = jax.nn.sigmoid(a)
    silu = a * sig
    hidden_ref[...] = (silu * b).astype(BF16)
    pa_ref[...] = w * b * sig * (1.0 + a * (1.0 - sig))
    pb_ref[...] = w * silu


def back_kernel(count, *refs):
    y_refs = refs[:count]
    hidden_ref, pa_ref, pb_ref, down_ref, grads_ref, score_ref, rows_ref, part_ref = refs[count:]
    step = pl.program_id(0)

    @pl.when(step == 0)
    def _():
        row = 0
        for ref in y_refs:
            rows_ref[row : row + ref.shape[0], :] = ref[...]
            row += ref.shape[0]
        part_ref[...] = jnp.zeros_like(part_ref)

    back = lax.dot_general(rows_ref[...], down_ref[0], NT, preferred_element_type=F32)
    grads_ref[0] = (back * pa_ref[...]).astype(BF16)
    grads_ref[1] = (back * pb_ref[...]).astype(BF16)
    prod = back * hidden_ref[...].astype(F32)
    part = part_ref[...]
    for c in range(prod.shape[1] // 128):
        part = part + prod[:, c * 128 : (c + 1) * 128]
    part_ref[...] = part

    @pl.when(step == pl.num_programs(0) - 1)
    def _():
        total = jnp.sum(jnp.transpose(part_ref[...]), axis=0, keepdims=True)
        shape = score_ref.shape
        top = lax.broadcasted_iota(jnp.int32, shape, 0) == 0
        score_ref[...] = jnp.where(top, jnp.broadcast_to(total, shape), 0.0).astype(BF16)


def rowgrad_kernel(places, dest_ref, grads_ref, score_ref, gate_ref, up_ref, *out_refs):
    del dest_ref
    size = gate_ref.shape[1]
    val = lax.dot_general(gate_ref[0], grads_ref[0], NT, preferred_element_type=F32)
    val = val + lax.dot_general(up_ref[0], grads_ref[1], NT, preferred_element_type=F32)
    val = val.astype(BF16)
    for i, (out, at) in enumerate(places):

        @pl.when(pl.program_id(0) == i)
        def _():
            out_refs[out][at : at + size, :] = val
            out_refs[out][at + size : at + size + 16, :] = score_ref[...]


def second_back_kernel(nx, size, came_ref, *refs):
    for i in range(nx - 1):
        out = refs[nx - 1 + i]
        out[0:size, :] = refs[i][...]
        out[size:, :] = came_ref[(i + 1) * size : (i + 2) * size, :]


def combine_kernel(n, cap, feats, parts, last, me_ref, ids_ref, metas_ref, *refs):
    me = me_ref[0]
    rows = n * cap
    toks = metas_ref.shape[2]
    metas = [metas_ref[j].astype(F32) for j in range(n)]
    if last:
        total_ref, part_ref, out_ref, gates_ref = refs[-4:]
        total = total_ref[...]
        gg = [part_ref[0], part_ref[1]]
    else:
        total_ref, part_ref = refs[-2:]
        total = jnp.zeros((feats, n * toks), F32)
        gg = [jnp.zeros((16, toks), F32)] * 2
    row = lax.broadcasted_iota(jnp.int32, (rows, n * toks), 0).astype(F32)
    for k, which, at in parts:
        wanted = []
        for j in range(n):
            code = metas[j][j ^ k : (j ^ k) + 1, :]
            wanted.append(jnp.where(code >= 0.0, code + float((j ^ k) * cap), -1.0))
        wanted = jnp.concatenate(wanted, axis=1)
        pick = (row == wanted).astype(F32).astype(BF16)
        got = refs[which][at : at + feats, :]
        total = total + jnp.dot(got, pick, preferred_element_type=F32)
        got = refs[which][at + feats : at + feats + 16, :]
        score = jnp.dot(got, pick[:, 0:toks], preferred_element_type=F32)
        gg = [gg[c] + jnp.where(ids_ref[c : c + 1, :] == (me ^ k), score, 0.0) for c in (0, 1)]
    if not last:
        total_ref[...] = total
        part_ref[0] = gg[0]
        part_ref[1] = gg[1]
        return
    for j in range(n):
        place = pl.multiple_of((me ^ j) * toks, toks)
        out_ref[:, pl.ds(place, toks)] = total[:, j * toks : (j + 1) * toks].astype(BF16)
    gates_ref[...] = jnp.concatenate([gg[0][0:1], gg[1][0:1]], axis=0).astype(BF16)


def first_weights_kernel(rows, core_ref, x_ref, x_came_ref, g_ref, g_came_ref, out_ref, mark_ref, xt_ref, both_ref):
    block = xt_ref.shape[0]

    @pl.when(pl.program_id(0) == 0)
    def _():
        mark_ref[...] = jnp.zeros_like(mark_ref)
        take_halves(rows, block, core_ref, x_ref, x_came_ref, xt_ref, 0)

    for half in range(2):
        both_ref[0:rows] = g_ref[half]
        both_ref[rows:] = g_came_ref[half]
        out_ref[half] = jnp.dot(xt_ref[...], both_ref[...], preferred_element_type=F32).astype(BF16)


def take_halves(rows, block, core_ref, x_ref, x_came_ref, xt_ref, at):
    @pl.when(core_ref[0] == 0)
    def _():
        xt_ref[:, at : at + rows] = x_ref[:, :block].T
        xt_ref[:, at + rows : at + 2 * rows] = x_came_ref[:, :block].T

    @pl.when(core_ref[0] != 0)
    def _():
        xt_ref[:, at : at + rows] = x_ref[:, block:].T
        xt_ref[:, at + rows : at + 2 * rows] = x_came_ref[:, block:].T


def rest_weights_kernel(rows, others, core_ref, *refs):
    x_refs, refs = refs[: 2 * others], refs[2 * others :]
    g_refs, part_ref = refs[: 2 * others], refs[2 * others]
    gate_ref, up_ref, mark_ref, xt_ref, all_ref = refs[2 * others + 1 :]
    block = xt_ref.shape[0]

    @pl.when(pl.program_id(0) == 0)
    def _():
        mark_ref[...] = jnp.zeros_like(mark_ref)
        for i in range(others):
            take_halves(rows, block, core_ref, x_refs[2 * i], x_refs[2 * i + 1], xt_ref, 2 * i * rows)

    for half, out in ((0, gate_ref), (1, up_ref)):
        for i, ref in enumerate(g_refs):
            all_ref[i * rows : (i + 1) * rows] = ref[half]
        total = jnp.dot(xt_ref[...], all_ref[...], preferred_element_type=F32)
        total = total + part_ref[half].astype(F32)
        out[0] = (total * (1.0 / (2 * others + 2))).astype(BF16)


def local(tokens, cotangent, gates, expert_ids, gate_w, up_w, down_w):
    toks, d = tokens.shape
    top = expert_ids.shape[1]
    h = gate_w.shape[2]
    n = lax.axis_size("expert")
    ndp = lax.axis_size("dp")
    nz = 4
    nx = n // nz
    ny = ndp // 2
    cap = -(-(3 * toks * top // (2 * n)) // 16) * 16
    rows = n * cap
    feats = d // n
    size = feats + 16
    block = d // ndp
    wide = d + toks
    me = lax.axis_index("expert").astype(jnp.int32)
    my_dp = lax.axis_index("dp").astype(jnp.int32)
    me_arr = me.reshape(1)
    my_y, my_core = (my_dp // 2).reshape(1), (my_dp % 2).reshape(1)
    ids_t = expert_ids.T
    gates_t = gates.T
    any_space = pl.BlockSpec(memory_space=pl.ANY)

    def swap(v, k):
        return lax.ppermute(v, "expert", [(i, i ^ k) for i in range(n)])

    def swap_dp(v, q):
        return lax.ppermute(v, "dp", [(i, i ^ q) for i in range(ndp)])

    def shape(*dims, dtype=BF16):
        return jax.ShapeDtypeStruct(dims, dtype)

    previous = []

    def run(body, name, outs, args, in_specs, out_specs, after=(), grid=(), scalars=0, scratch=(), weight=LONG, mib=48):
        waits = [*after, *previous]
        first = len(args)

        def trimmed(*refs):
            body(*refs[:first], *refs[first + len(waits) :])

        made = pl.pallas_call(
            trimmed,
            grid_spec=pltpu.PrefetchScalarGridSpec(
                num_scalar_prefetch=scalars,
                grid=grid,
                in_specs=[*in_specs, *[any_space] * len(waits)],
                out_specs=out_specs,
                scratch_shapes=scratch,
            ),
            out_shape=outs,
            compiler_params=params(mib),
            cost_estimate=pl.CostEstimate(flops=weight, bytes_accessed=1, transcendentals=0),
            name=name,
        )(*args, *waits)
        previous[:] = [min(made, key=lambda v: v.size)]
        return made

    whole = lambda dims: pl.BlockSpec(dims, lambda *_: (0,) * len(dims))

    def call(body, name, outs, args, after=(), scalars=0, **kinds):
        in_specs = [smem()] * scalars + vmem(len(args) - scalars)
        return run(body, name, outs, args, in_specs, vmem(len(outs)), after, **kinds)

    def fence(after):
        call(fence_kernel, "fence", [shape(8, 128, dtype=F32)], [], after)

    sources = [ids_t, gates_t, tokens, cotangent]
    outs = (
        [shape(2 * n, toks), shape(nx * cap, wide), shape(toks, wide), shape(cap, d)]
        + [shape(cap, wide)] * (nx - 1)
        + [shape(nz * cap, d)] * (nx - 1)
    )
    meta, x_near, x_all, x_own, *made = run(
        functools.partial(prep_kernel, n, nx, cap),
        "prep",
        outs,
        [me_arr, *sources],
        [smem()] + [pl.BlockSpec(memory_space=pltpu.HBM)] * len(sources),
        vmem(len(outs)),
        scratch=[pltpu.VMEM(v.shape, v.dtype) for v in sources]
        + [pltpu.SemaphoreType.DMA((len(sources),))],
        mib=59,
    )
    x_side, y_side = made[: nx - 1], made[nx - 1 :]
    x_near = swap(x_near, nx)
    x_all = swap(x_all, 2 * nx)
    y_side = [swap(v, xo) for xo, v in enumerate(y_side, 1)]
    y_sent = call(
        functools.partial(second_kernel, n, nx, cap),
        "second",
        [shape(nx * cap, d)] * nz,
        [meta, cotangent, *y_side],
        mib=59,
    )
    made = call(
        functools.partial(third_kernel, n, nx, cap),
        "third",
        [shape((nz - 1) * cap, wide)] * (nx - 1) + [shape(cap, wide)] * (1 + nx),
        [x_all, x_near, *x_side],
        mib=59,
    )
    x_side = [swap(v, xo) for xo, v in enumerate(made[: nx - 1], 1)]
    x_mid, x_passed = made[nx - 1], made[nx:]
    x_far = [swap(v, nx + xo) for xo, v in enumerate(x_passed)]
    y_z = [swap(y_sent[zk], zk * nx) for zk in range(2, nz)]
    got_x = [x_own, x_near, x_mid, *x_side, *x_far]
    y_near = call(hold_kernel, "hold", [shape(nx * cap, d)], [y_sent[1]], x_far, mib=59)[0]
    y_near = swap(y_near, nx)

    tile = 256
    steps = h // tile
    column = pl.BlockSpec((rows, tile), lambda i: (0, i))
    *x_parts, hidden, pa, pb, metas = run(
        functools.partial(forward_kernel, n, nx, cap, len(got_x), ny),
        "forward",
        [shape(rows, 2 * block)] * ny
        + [shape(rows, h), shape(rows, h, dtype=F32), shape(rows, h, dtype=F32)]
        + [shape(n, 2 * n, toks)],
        [my_y, *got_x, meta, gate_w, up_w],
        [smem()]
        + [whole(v.shape) for v in got_x]
        + [whole((2 * n, toks))]
        + [pl.BlockSpec((1, d, tile), lambda i: (0, 0, i))] * 2,
        [whole((rows, 2 * block))] * ny
        + [column] * 3
        + [whole((n, 2 * n, toks))],
        grid=(steps,),
        scratch=[pltpu.VMEM((rows, 128), F32), pltpu.VMEM((rows, d), BF16)],
        weight=1,
    )
    x_own_came = swap_dp(x_parts[0], 1)
    x_parts = [x_parts[0]] + [swap_dp(v, 2 * yo) for yo, v in enumerate(x_parts[1:], 1)]
    fence(y_z)
    got_y = [y_sent[0], y_near, *y_z]
    grads, score = run(
        functools.partial(back_kernel, len(got_y)),
        "back",
        [shape(2, rows, h), shape(16, rows)],
        [*got_y, hidden, pa, pb, down_w],
        [whole(v.shape) for v in got_y]
        + [column] * 3
        + [pl.BlockSpec((1, tile, d), lambda i: (0, i, 0))],
        [pl.BlockSpec((2, rows, tile), lambda i: (0, 0, i)), whole((16, rows))],
        after=[x_own_came],
        grid=(steps,),
        scratch=[pltpu.VMEM((rows, d), BF16), pltpu.VMEM((rows, 128), F32)],
        weight=1,
        mib=59,
    )
    g_own_came = swap_dp(grads, 1)
    g_parts = [grads] + [swap_dp(grads, 2 * yo) for yo in range(1, ny)]

    def rowgrads(places, outs, after=(), weight=1):
        def owner(i, me_ref):
            k = jnp.int32(places[0][0])
            for at, (other, _, _) in enumerate(places):
                k = jnp.where(i == at, other, k)
            return (0, k ^ me_ref[0], 0)

        spec = pl.BlockSpec((1, feats, h), owner)
        fixed = whole
        return run(
            functools.partial(rowgrad_kernel, [(out, at) for _, out, at in places]),
            "rowgrad",
            [shape(size * many, rows) for many in outs],
            [me_arr, grads, score, gate_w, up_w],
            [fixed((2, rows, h)), fixed((16, rows)), spec, spec],
            [fixed((size * many, rows)) for many in outs],
            after,
            grid=(len(places),),
            scalars=1,
            weight=weight,
            mib=59,
        )

    far = list(range(n - nx, n))
    mids = list(range(2 * nx, n - nx))
    straight = {}

    def send(ks, values):
        for k, v in zip(ks, values):
            straight[k] = swap(v, k)

    send(far[1:], rowgrads([(k, i, 0) for i, k in enumerate(far[1:])], [1] * (nx - 1)))
    near, sent = rowgrads(
        [(nx + xo, 0, xo * size) for xo in range(nx)] + [(far[0], 1, 0)],
        [nx, 1],
        x_parts[1:],
        weight=LONG,
    )
    near = swap(near, nx)
    send(far[:1], [sent])
    tile_w = 256
    part_spec = pl.BlockSpec((2, block, tile_w), lambda i: (0, 0, i))
    column_w = pl.BlockSpec((2, rows, tile_w), lambda i: (0, 0, i))
    x_spec = whole((rows, 2 * block))
    w_part, _ = run(
        functools.partial(first_weights_kernel, rows),
        "weights",
        [shape(2, block, h), shape(8, 128, dtype=F32)],
        [my_core, x_parts[0], x_own_came, grads, g_own_came],
        [smem(), x_spec, x_spec, column_w, column_w],
        [part_spec, whole((8, 128))],
        grid=(h // tile_w,),
        scratch=[pltpu.VMEM((block, 2 * rows), BF16), pltpu.VMEM((2 * rows, tile_w), BF16)],
    )
    x_came = [swap_dp(v, 1) for v in x_parts[1:]]
    last = mids[::-1]
    own, *sent = rowgrads(
        [(k, i, 0) for i, k in enumerate([0, *range(1, nx), *last])],
        [1] * (nx + len(last)),
        x_came,
        weight=LONG,
    )
    by_column, sent = sent[: nx - 1], sent[nx - 1 :]
    send(last, sent)

    g_came = [swap_dp(v, 1) for v in g_parts[1:]]
    fence(g_parts[1:])

    sent = call(
        functools.partial(second_back_kernel, nx, size),
        "second_back",
        [shape(2 * size, rows)] * (nx - 1),
        [near, *by_column],
        [straight[k] for k in far[1:]],
    )
    columns = [swap(v, xo) for xo, v in enumerate(sent, 1)]

    def combine(parts, refs, carried, outs):
        return call(
            functools.partial(combine_kernel, n, cap, feats, parts, bool(carried)),
            "combine",
            outs,
            [me_arr, ids_t, metas, *refs, *carried],
            scalars=1,
        )

    parts = [(0, 0, 0), (nx, 1, 0)] + [(k, i, 0) for i, k in enumerate(far, 2)]
    sums = combine(
        parts,
        [own, near, *[straight[k] for k in far]],
        [],
        [shape(feats, n * toks, dtype=F32), shape(2, 16, toks, dtype=F32)],
    )

    others = ny - 1
    out_spec = pl.BlockSpec((1, block, tile_w), lambda i: (0, 0, i))
    pairs = lambda ours, theirs: [v for both in zip(ours, theirs) for v in both]
    grad_gate_w, grad_up_w, _ = run(
        functools.partial(rest_weights_kernel, rows, others),
        "weights_rest",
        [shape(1, block, h)] * 2 + [shape(8, 128, dtype=F32)],
        [my_core, *pairs(x_parts[1:], x_came), *pairs(g_parts[1:], g_came), w_part],
        [smem()] + [x_spec] * (2 * others) + [column_w] * (2 * others) + [part_spec],
        [out_spec, out_spec, whole((8, 128))],
        grid=(h // tile_w,),
        scratch=[
            pltpu.VMEM((block, 2 * others * rows), BF16),
            pltpu.VMEM((2 * others * rows, tile_w), BF16),
        ],
    )

    parts = [(k, i, 0) for i, k in enumerate(last)]
    for i in range(nx - 1):
        parts += [(i + 1, len(last) + i, 0), (nx + i + 1, len(last) + i, size)]
    summed, gg = combine(
        parts,
        [*[straight[k] for k in last], *columns],
        sums,
        [shape(feats, n * toks), shape(2, toks)],
    )
    return summed.T, grad_gate_w, grad_up_w, gg.T


def solution(mesh):
    placed = (
        P(("dp", "expert"), None),
        P(("dp", "expert"), None),
        P(("dp", "expert"), None),
        P(("dp", "expert"), None),
        P("expert", None, None),
        P("expert", None, None),
        P("expert", None, None),
    )
    return jax.shard_map(
        local,
        mesh=mesh,
        in_specs=placed,
        out_specs=(
            P("dp", "expert"),
            P("expert", "dp", None),
            P("expert", "dp", None),
            P(("dp", "expert"), None),
        ),
        check_vma=False,
    )
```

time: 228 us -> 207 us (0.908)
  starting transfers between devices: 45.6 us -> 26.3 us
  waiting for transfers between devices: 101 us -> 91.3 us
  Pallas kernels: 73.4 us -> 78.5 us
    ppermute x15, starting transfers between devices: 42.6 us -> 23 us  [swap(): return lax.ppermute(v, 'expert', [(i, i ^ k) for i in range(n)])]
    ppermute x15, waiting for transfers between devices: 101 us -> 85.3 us  [swap(): return lax.ppermute(v, 'expert', [(i, i ^ k) for i in range(n)])]
    ppermute x4 -> x6, waiting for transfers between devices: 0.01 us -> 6.01 us  [swap_dp(): return lax.ppermute(v, 'dp', [(i, i ^ q) for i in range(ndp)])]
    pallas_call x14 -> x16, Pallas kernels: 73.4 us -> 78.5 us  [run(): pl.pallas_call(trimmed, grid_spec=pltpu.PrefetchScalarGridSpec(num_scalar...]
    unnamed x34 -> x44, local copies, waits for them, and re-layouts: 7.47 us -> 9.03 us
  transfers between devices with their start and end apart: 19 -> 21, of which waited for: 7 -> 13; matrix products, arithmetic and copies ran while one was open for 0% -> 0% of each run, Pallas kernels for 29% -> 32%
where the time goes in v3:
time: 207 us; the launch traced here: 206 us
  waiting for transfers between devices  91.3 us (44%)
  Pallas kernels  78.5 us (38%)
  starting transfers between devices  26.3 us (13%)
  local copies, waits for them, and re-layouts  9.03 us (4%)
    ppermute x15, waiting for transfers between devices, swap(): return lax.ppermute(v, 'expert', [(i, i ^ k) for i in range(n)])  85.3 us
    pallas_call x16, Pallas kernels, run(): pl.pallas_call(trimmed, grid_spec=pltpu.PrefetchScalarGridSpec(num_scalar...  78.5 us
    ppermute x15, starting transfers between devices, swap(): return lax.ppermute(v, 'expert', [(i, i ^ k) for i in range(n)])  23 us
    unnamed x44, local copies, waits for them, and re-layouts  9.03 us
    ppermute x6, waiting for transfers between devices, swap_dp(): return lax.ppermute(v, 'dp', [(i, i ^ q) for i in range(ndp)])  6.01 us
  transfers between devices with their start and end apart: 21, of which 13 were waited for; matrix products, arithmetic and copies ran while one was open for 0% of the time, Pallas kernels for 32%

profile of v3, /device:TPU:0, one launch (start us, length us, event | category | flops | bytes accessed | tf_op | source)
XLA Modules:
  0.0 205.9 jit_solution(3259181699142272403)
XLA Ops:
  0.6 3.8 %prep.1 = (bf16[16,128]{1,0:T(8,128)(2,1)}, bf16[96,3712]{1,0:T(8,128)(2,1)}, bf16[128,3712]{1,0:T(8,128)(2,1)}, bf16[48,3584]{1,0:T(8,128)(2,1)}, bf16[48,3712]{1,0:T(8,128)(2,1)}, /*index=5*/bf16[192,3584]{1,0:T(8,128)(2,1)}) custom-call(s32[1]{0:T(128)} %bitcast.refs_0_, s32[2,128]{1,0:T(2,128)} %bitcast.7, bf16[2,128]{1,0:T(2,128)(2,1)} %bitcast.10, ...), custom_call_target="tpu_custom_call" | custom-call | flops 1099511627776 | bytes 1 | tf_op jit(solution)/shard_map/prep/pallas_call | solution.py:339
  4.5 3.0 %collective-permute-start.2 = (bf16[192,3584]{1,0:T(8,128)(2,1)}, bf16[192,3584]{1,0:T(8,128)(2,1)S(1)}, u32[]{:S(2)}, u32[]{:S(2)}) collective-permute-start(bf16[192,3584]{1,0:T(8,128)(2,1)} %get-tuple-element.46), channel_id=1, source_target_pairs={{0,1},{1,0},{2,3},{3,2},{4,5},{5,4},{6,7},{7,6},{8,9},{9,8},{10,11... | collective-permute-start | bytes 4128776 | tf_op jit(solution)/shard_map/ppermute | solution.py:322
  7.5 1.6 collective-permute-start
  9.1 2.6 %collective-permute-start.1 = (bf16[128,3712]{1,0:T(8,128)(2,1)}, bf16[128,3712]{1,0:T(8,128)(2,1)}, u32[]{:S(2)}, u32[]{:S(2)}) collective-permute-start(bf16[128,3712]{1,0:T(8,128)(2,1)} %get-tuple-element.43), channel_id=1, source_target_pairs={{0,4},{1,5},{2,6},{3,7},{4,0},{5,1},{6,2},{7,3},{8,12},{9,13},{10,... | collective-permute-start | bytes 2850824 | tf_op jit(solution)/shard_map/ppermute | solution.py:322
  11.6 26.2 %collective-permute-done.2.refs_2_ = bf16[192,3584]{1,0:T(8,128)(2,1)S(1)} collective-permute-done((bf16[192,3584]{1,0:T(8,128)(2,1)}, bf16[192,3584]{1,0:T(8,128)(2,1)S(1)}, u32[]{:S(2)}, u32[]{:S(2)}) %collective-permute-start.2) | collective-permute-done | bytes 1376288 | tf_op jit(solution)/shard_map/ppermute | solution.py:322
  37.9 1.1 copy-done.21
  38.9 3.9 %second.1 = (bf16[96,3584]{1,0:T(8,128)(2,1)}, bf16[96,3584]{1,0:T(8,128)(2,1)}, bf16[96,3584]{1,0:T(8,128)(2,1)}, bf16[96,3584]{1,0:T(8,128)(2,1)}) custom-call(bf16[16,128]{1,0:T(8,128)(2,1)} %get-tuple-element.45.refs_0_.refs_3_.refs_7_, bf16[128,3584]{1,0:T(8,128)(2,1)} %refs_1_.1, bf16[192,3584]{1,0:T(8,128)(2,1)} %copy-done.21, ...), custom_call_target="tpu_custom_call" | custom-call | flops 1099511627776 | bytes 1 | tf_op jit(solution)/shard_map/second/pallas_call | solution.py:339
  42.8 10.1 %collective-permute-done.1.refs_0_ = bf16[128,3712]{1,0:T(8,128)(2,1)} collective-permute-done((bf16[128,3712]{1,0:T(8,128)(2,1)}, bf16[128,3712]{1,0:T(8,128)(2,1)}, u32[]{:S(2)}, u32[]{:S(2)}) %collective-permute-start.1) | collective-permute-done | bytes 950304 | tf_op jit(solution)/shard_map/ppermute | solution.py:322
  52.9 3.3 %third.1 = (bf16[144,3712]{1,0:T(8,128)(2,1)}, bf16[48,3712]{1,0:T(8,128)(2,1)}, bf16[48,3712]{1,0:T(8,128)(2,1)}, bf16[48,3712]{1,0:T(8,128)(2,1)}) custom-call(bf16[128,3712]{1,0:T(8,128)(2,1)} %collective-permute-done.1.refs_0_, bf16[96,3712]{1,0:T(8,128)(2,1)} %collective-permute-done.refs_1_.refs_2_, bf16[48,3712]{1,0:T(8,128)(2,1)} %get-tuple-element.44.refs_2_, ...), custom_call_target="tpu_custom_call" | custom-call | flops 1099511627776 | bytes 1 | tf_op jit(solution)/shard_map/third/pallas_call | solution.py:339
  56.3 2.0 collective-permute-start.5
  58.2 1.5 collective-permute-start.3
  59.7 1.0 collective-permute-start.7
  60.8 1.5 collective-permute-start.8
  62.2 17.4 %collective-permute-done.4.refs_1_.refs_5_ = bf16[48,3712]{1,0:T(8,128)(2,1)S(1)} collective-permute-done((bf16[48,3712]{1,0:T(8,128)(2,1)}, bf16[48,3712]{1,0:T(8,128)(2,1)S(1)}, u32[]{:S(2)}, u32[]{:S(2)}) %collective-permute-start.4) | collective-permute-done | bytes 356384 | tf_op jit(solution)/shard_map/ppermute | solution.py:322
  79.7 5.1 %collective-permute-done.5.refs_2_.refs_6_ = bf16[48,3712]{1,0:T(8,128)(2,1)S(1)} collective-permute-done((bf16[48,3712]{1,0:T(8,128)(2,1)}, bf16[48,3712]{1,0:T(8,128)(2,1)S(1)}, u32[]{:S(2)}, u32[]{:S(2)}) %collective-permute-start.5) | collective-permute-done | bytes 356384 | tf_op jit(solution)/shard_map/ppermute | solution.py:322
  84.7 0.7 copy-done.6
  85.5 2.1 %hold.1.refs_10_ = bf16[96,3584]{1,0:T(8,128)(2,1)} custom-call(bf16[96,3584]{1,0:T(8,128)(2,1)} %get-tuple-element.52.refs_0_, bf16[48,3712]{1,0:T(8,128)(2,1)} %copy-done.4, bf16[48,3712]{1,0:T(8,128)(2,1)} %copy-done.6, bf16[48,3712]{1,0:T(8,128)(2,1)} %get-tuple-element.48.refs_3_), custom_call_target="tpu_custom_call" | custom-call | flops 1099511627776 | bytes 1 | tf_op jit(solution)/shard_map/hold/pallas_call | solution.py:339
  87.6 2.0 collective-permute-done.3.refs_4_
  89.6 1.1 copy-done.2
  90.6 1.0 copy-done.5
  91.6 1.0 copy-done.7
  92.6 11.5 %forward.1 = (bf16[384,1792]{1,0:T(8,128)(2,1)}, bf16[384,1792]{1,0:T(8,128)(2,1)}, bf16[384,1024]{1,0:T(8,128)(2,1)S(1)}, f32[384,1024]{1,0:T(8,128)}, f32[384,...) custom-call(s32[1]{0:T(128)} %bitcast.2.refs_0_, bf16[48,3584]{1,0:T(8,128)(2,1)S(1)} %copy-done.8, ...), custom_call_target="tpu_custom_call" | custom-call | flops 1 | bytes 1 | tf_op jit(solution)/shard_map/forward/pallas_call | solution.py:339
  104.2 1.6 collective-permute-start.10
  105.8 3.1 %collective-permute-done.7.refs_0_.refs_2_ = bf16[96,3584]{1,0:T(8,128)(2,1)} collective-permute-done((bf16[96,3584]{1,0:T(8,128)(2,1)}, bf16[96,3584]{1,0:T(8,128)(2,1)}, u32[]{:S(2)}, u32[]{:S(2)}) %collective-permute-start.7) | collective-permute-done | bytes 688160 | tf_op jit(solution)/shard_map/ppermute | solution.py:322
  109.5 9.9 %collective-permute-done.6.refs_1_ = bf16[96,3584]{1,0:T(8,128)(2,1)} collective-permute-done((bf16[96,3584]{1,0:T(8,128)(2,1)}, bf16[96,3584]{1,0:T(8,128)(2,1)}, u32[]{:S(2)}, u32[]{:S(2)}) %collective-permute-start.6) | collective-permute-done | bytes 688160 | tf_op jit(solution)/shard_map/ppermute | solution.py:322
  119.3 8.9 %back.1 = (bf16[2,384,1024]{2,1,0:T(8,128)(2,1)}, bf16[16,384]{1,0:T(8,128)(2,1)}) custom-call(bf16[96,3584]{1,0:T(8,128)(2,1)} %get-tuple-element.47.refs_3_.refs_0_, bf16[96,3584]{1,0:T(8,128)(2,1)} %collective-permute-done.6.refs_1_, bf16[96,3584]{1,0:T(8,128)(2,1)} %collective-permute-done.7.refs_0_.refs_2_, ...), custom_call_target="tpu_custom_call" | custom-call | flops 1 | bytes 1 | tf_op jit(solution)/shard_map/back/pallas_call | solution.py:339
  128.3 1.6 collective-permute-start.17
  129.9 3.8 %rowgrad.3.refs_6_ = bf16[464,384]{1,0:T(8,128)(2,1)} custom-call(s32[1]{0:T(128)} %bitcast.refs_0_, bf16[2,384,1024]{2,1,0:T(8,128)(2,1)} %get-tuple-element.60.refs_1_.refs_3_, bf16[16,384]{1,0:T(8,128)(2,1)} %get-tuple-element.61.refs_2_.refs_5_, bf16[1,3584,1024]{2,1,0:T(8,128)(2,1)} %refs_3_.7, bf16[1,3584,1024]{2,1,0:T(8,128)(2,1)} %refs_4_.7, ...), custom_call_target="tpu_custom_call" | custom-call | flops 1 | bytes 1 | tf_op jit(solution)/shard_map/rowgrad/pallas_call | solution.py:339
  133.7 2.7 %collective-permute-start.16 = (bf16[464,384]{1,0:T(8,128)(2,1)}, bf16[464,384]{1,0:T(8,128)(2,1)}, u32[]{:S(2)}, u32[]{:S(2)}) collective-permute-start(bf16[464,384]{1,0:T(8,128)(2,1)} %rowgrad.3.refs_6_), channel_id=1, source_target_pairs={{0,7},{1,6},{2,5},{3,4},{4,3},{5,2},{6,1},{7,0},{8,15},{9,14},{10,... | collective-permute-start | bytes 1069064 | tf_op jit(solution)/shard_map/ppermute | solution.py:322
  136.4 1.2 collective-permute-done.10.refs_5_.refs_1_
  137.5 6.9 %rowgrad.4 = (bf16[928,384]{1,0:T(8,128)(2,1)}, bf16[464,384]{1,0:T(8,128)(2,1)}) custom-call(s32[1]{0:T(128)} %bitcast.refs_0_, bf16[2,384,1024]{2,1,0:T(8,128)(2,1)} %get-tuple-element.60.refs_1_.refs_3_, bf16[16,384]{1,0:T(8,128)(2,1)} %get-tuple-element.61.refs_2_.refs_5_, bf16[1,3584,1024]{2,1,0:T(8,128)(2,1)} %refs_3_.7, ...), custom_call_target="tpu_custom_call" | custom-call | flops 1099511627776 | bytes 1 | tf_op jit(solution)/shard_map/rowgrad/pallas_call | solution.py:339
  144.7 2.5 %collective-permute-start.19 = (bf16[464,384]{1,0:T(8,128)(2,1)}, bf16[464,384]{1,0:T(8,128)(2,1)}, u32[]{:S(2)}, u32[]{:S(2)}) collective-permute-start(bf16[464,384]{1,0:T(8,128)(2,1)} %get-tuple-element.63.refs_5_), channel_id=1, source_target_pairs={{0,6},{1,7},{2,4},{3,5},{4,2},{5,3},{6,0},{7,1},{8,14},{9,15},{10,... | collective-permute-start | bytes 1069064 | tf_op jit(solution)/shard_map/ppermute | solution.py:322
  147.2 1.0 copy-done.11
  148.2 7.4 %weights.1 = (bf16[2,896,1024]{2,1,0:T(8,128)(2,1)}, f32[8,128]{1,0:T(8,128)S(1)}) custom-call(s32[1]{0:T(128)} %bitcast.4.refs_0_, bf16[384,1792]{1,0:T(8,128)(2,1)} %get-tuple-element.59.refs_1_, bf16[384,1792]{1,0:T(8,128)(2,1)} %collective-permute-done.9.refs_8_.refs_2_, bf16[2,384,1024]{2,1,0:T(8,128)(2,1)S(1)} %copy-done, ...), custom_call_target="tpu_custom_call" | custom-call | flops 1099511627776 | bytes 1 | tf_op jit(solution)/shard_map/weights/pallas_call | solution.py:339
  155.6 0.6 copy-done.20
  156.2 8.3 %rowgrad.5 = (bf16[464,384]{1,0:T(8,128)(2,1)}, bf16[464,384]{1,0:T(8,128)(2,1)}, bf16[464,384]{1,0:T(8,128)(2,1)}, bf16[464,384]{1,0:T(8,128)(2,1)}) custom-call(s32[1]{0:T(128)} %bitcast.refs_0_, bf16[2,384,1024]{2,1,0:T(8,128)(2,1)} %get-tuple-element.60.refs_1_.refs_3_, bf16[16,384]{1,0:T(8,128)(2,1)} %get-tuple-element.61.refs_2_.refs_5_, ...), custom_call_target="tpu_custom_call" | custom-call | flops 1099511627776 | bytes 1 | tf_op jit(solution)/shard_map/rowgrad/pallas_call | solution.py:339
  164.5 1.6 collective-permute-start.13
  166.1 4.6 %collective-permute-done.17.refs_0_.refs_3_ = bf16[2,384,1024]{2,1,0:T(8,128)(2,1)} collective-permute-done((bf16[2,384,1024]{2,1,0:T(8,128)(2,1)}, bf16[2,384,1024]{2,1,0:T(8,128)(2,1)}, u32[]{:S(2)}, u32[]{:S(2)}) %collective-permute-start.17) | collective-permute-done | bytes 1572896 | tf_op jit(solution)/shard_map/ppermute | solution.py:325
  170.8 1.3 collective-permute-start.14
  172.1 1.0 copy-done.17
  173.1 1.0 copy-done.19
  174.1 2.1 %second_back.1.refs_7_ = bf16[928,384]{1,0:T(8,128)(2,1)} custom-call(bf16[928,384]{1,0:T(8,128)(2,1)} %collective-permute-done.15.refs_0_.refs_4_, bf16[464,384]{1,0:T(8,128)(2,1)S(1)} %copy-done.19, bf16[464,384]{1,0:T(8,128)(2,1)} %collective-permute-done.16.refs_2_.refs_6_, f32[8,128]{1,0:T(8,128)S(1)} %fence.3.refs_3_), custom_call_target="tpu_custom_call" | custom-call | flops 1099511627776 | bytes 1 | tf_op jit(solution)/shard_map/second_back/pallas_call | solution.py:339
  176.2 1.5 collective-permute-start.18
  177.7 3.5 %combine.2 = (f32[448,1024]{1,0:T(8,128)S(1)}, f32[2,16,128]{2,1,0:T(8,128)S(1)}) custom-call(s32[1]{0:T(128)} %bitcast.refs_0_, s32[2,128]{1,0:T(2,128)S(1)} %bitcast.8, bf16[8,16,128]{2,1,0:T(8,128)(2,1)S(1)} %copy-done.13, bf16[464,384]{1,0:T(8,128)(2,1)S(1)} %copy-done.18, bf16[928,384]{1,0:T(8,128)(2,1)} %collective-permute-done.15.refs_0_.refs_4_, ...), custom_call_target="tpu_custom_call" | custom-call | flops 1099511627776 | bytes 1 | tf_op jit(solution)/shard_map/combine/pallas_call | solution.py:339
  181.4 8.4 %weights_rest.1 = (bf16[1,896,1024]{2,1,0:T(8,128)(2,1)}, bf16[1,896,1024]{2,1,0:T(8,128)(2,1)}, f32[8,128]{1,0:T(8,128)S(1)}) custom-call(s32[1]{0:T(128)} %bitcast.4.refs_0_, bf16[384,1792]{1,0:T(8,128)(2,1)} %collective-permute-done.10.refs_5_.refs_1_, bf16[384,1792]{1,0:T(8,128)(2,1)} %collective-permute-done.11.refs_5_.refs_2_, ...), custom_call_target="tpu_custom_call" | custom-call | flops 1099511627776 | bytes 1 | tf_op jit(solution)/shard_map/weights_rest/pallas_call | solution.py:339
  189.8 4.3 %collective-permute-done.13.refs_3_ = bf16[464,384]{1,0:T(8,128)(2,1)} collective-permute-done((bf16[464,384]{1,0:T(8,128)(2,1)}, bf16[464,384]{1,0:T(8,128)(2,1)}, u32[]{:S(2)}, u32[]{:S(2)}) %collective-permute-start.13) | collective-permute-done | bytes 356384 | tf_op jit(solution)/shard_map/ppermute | solution.py:322
  194.1 6.7 %collective-permute-done.14.refs_4_ = bf16[464,384]{1,0:T(8,128)(2,1)} collective-permute-done((bf16[464,384]{1,0:T(8,128)(2,1)}, bf16[464,384]{1,0:T(8,128)(2,1)}, u32[]{:S(2)}, u32[]{:S(2)}) %collective-permute-start.14) | collective-permute-done | bytes 356384 | tf_op jit(solution)/shard_map/ppermute | solution.py:322
  201.3 4.7 %combine.3 = (bf16[448,1024]{1,0:T(8,128)(2,1)}, bf16[2,128]{1,0:T(2,128)(2,1)}) custom-call(s32[1]{0:T(128)} %bitcast.refs_0_, s32[2,128]{1,0:T(2,128)S(1)} %bitcast.9, bf16[8,16,128]{2,1,0:T(8,128)(2,1)S(1)} %copy-done.14, bf16[464,384]{1,0:T(8,128)(2,1)} %collective-permute-done.13.refs_3_, bf16[464,384]{1,0:T(8,128)(2,1)} %collective-permute-done.14.refs_4_, ...), custom_call_target="tpu_custom_call" | custom-call | flops 1099511627776 | bytes 1 | tf_op jit(solution)/shard_map/combine/pallas_call | solution.py:339
  (54 shorter events, 1.8 us)
Async XLA Ops:
  4.5 33.4 %collective-permute-start.2 = (bf16[192,3584]{1,0:T(8,128)(2,1)}, bf16[192,3584]{1,0:T(8,128)(2,1)S(1)}, u32[]{:S(2)}, u32[]{:S(2)}) collective-permute-start(bf16[192,3584]{1,0:T(8,128)(2,1)} %get-tuple-element.46), channel_id=1, source_target_pairs={{0,1},{1,0},{2,3},{3,2},{4,5},{5,4},{6,7},{7,6},{8,9},{9,8},{10,11... | collective-permute-start | bytes 4128776 | tf_op jit(solution)/shard_map/ppermute | solution.py:322
  7.5 35.4 %collective-permute-start = (bf16[96,3712]{1,0:T(8,128)(2,1)}, bf16[96,3712]{1,0:T(8,128)(2,1)}, u32[]{:S(2)}, u32[]{:S(2)}) collective-permute-start(bf16[96,3712]{1,0:T(8,128)(2,1)} %get-tuple-element.42), channel_id=1, source_target_pairs={{0,2},{1,3},{2,0},{3,1},{4,6},{5,7},{6,4},{7,5},{8,10},{9,11},{10,... | collective-permute-start | bytes 2138120 | tf_op jit(solution)/shard_map/ppermute | solution.py:322
  9.1 43.9 %collective-permute-start.1 = (bf16[128,3712]{1,0:T(8,128)(2,1)}, bf16[128,3712]{1,0:T(8,128)(2,1)}, u32[]{:S(2)}, u32[]{:S(2)}) collective-permute-start(bf16[128,3712]{1,0:T(8,128)(2,1)} %get-tuple-element.43), channel_id=1, source_target_pairs={{0,4},{1,5},{2,6},{3,7},{4,0},{5,1},{6,2},{7,3},{8,12},{9,13},{10,... | collective-permute-start | bytes 2850824 | tf_op jit(solution)/shard_map/ppermute | solution.py:322
  37.9 1.1 copy-start.21
  56.3 23.4 %collective-permute-start.4 = (bf16[48,3712]{1,0:T(8,128)(2,1)}, bf16[48,3712]{1,0:T(8,128)(2,1)S(1)}, u32[]{:S(2)}, u32[]{:S(2)}) collective-permute-start(bf16[48,3712]{1,0:T(8,128)(2,1)} %get-tuple-element.50), channel_id=1, source_target_pairs={{0,2},{1,3},{2,0},{3,1},{4,6},{5,7},{6,4},{7,5},{8,10},{9,11},{10,... | collective-permute-start | bytes 1069064 | tf_op jit(solution)/shard_map/ppermute | solution.py:322
  56.3 28.5 %collective-permute-start.5 = (bf16[48,3712]{1,0:T(8,128)(2,1)}, bf16[48,3712]{1,0:T(8,128)(2,1)S(1)}, u32[]{:S(2)}, u32[]{:S(2)}) collective-permute-start(bf16[48,3712]{1,0:T(8,128)(2,1)} %get-tuple-element.51), channel_id=1, source_target_pairs={{0,3},{1,2},{2,1},{3,0},{4,7},{5,6},{6,5},{7,4},{8,11},{9,10},{10,... | collective-permute-start | bytes 1069064 | tf_op jit(solution)/shard_map/ppermute | solution.py:322
  58.2 31.3 %collective-permute-start.3 = (bf16[144,3712]{1,0:T(8,128)(2,1)}, bf16[144,3712]{1,0:T(8,128)(2,1)}, u32[]{:S(2)}, u32[]{:S(2)}) collective-permute-start(bf16[144,3712]{1,0:T(8,128)(2,1)} %get-tuple-element.49), channel_id=1, source_target_pairs={{0,1},{1,0},{2,3},{3,2},{4,5},{5,4},{6,7},{7,6},{8,9},{9,8},{10,11... | collective-permute-start | bytes 3207176 | tf_op jit(solution)/shard_map/ppermute | solution.py:322
  59.7 49.1 %collective-permute-start.7 = (bf16[96,3584]{1,0:T(8,128)(2,1)}, bf16[96,3584]{1,0:T(8,128)(2,1)}, u32[]{:S(2)}, u32[]{:S(2)}) collective-permute-start(bf16[96,3584]{1,0:T(8,128)(2,1)} %get-tuple-element.54), channel_id=1, source_target_pairs={{0,4},{1,5},{2,6},{3,7},{4,0},{5,1},{6,2},{7,3},{8,12},{9,13},{10,... | collective-permute-start | bytes 2064392 | tf_op jit(solution)/shard_map/ppermute | solution.py:322
  60.8 48.1 %collective-permute-start.8 = (bf16[96,3584]{1,0:T(8,128)(2,1)}, bf16[96,3584]{1,0:T(8,128)(2,1)}, u32[]{:S(2)}, u32[]{:S(2)}) collective-permute-start(bf16[96,3584]{1,0:T(8,128)(2,1)} %get-tuple-element.55), channel_id=1, source_target_pairs={{0,6},{1,7},{2,4},{3,5},{4,2},{5,3},{6,0},{7,1},{8,14},{9,15},{10,... | collective-permute-start | bytes 2064392 | tf_op jit(solution)/shard_map/ppermute | solution.py:322
  79.7 5.1 %copy-start.4 = (bf16[48,3712]{1,0:T(8,128)(2,1)}, bf16[48,3712]{1,0:T(8,128)(2,1)S(1)}, u32[]{:S(2)}) copy-start(bf16[48,3712]{1,0:T(8,128)(2,1)S(1)} %collective-permute-done.4.refs_1_.refs_5_) | copy-start | bytes 1069060
  84.7 0.7 copy-start.6
  85.5 4.1 %copy-start.3 = (bf16[48,3712]{1,0:T(8,128)(2,1)S(1)}, bf16[48,3712]{1,0:T(8,128)(2,1)}, u32[]{:S(2)}) copy-start(bf16[48,3712]{1,0:T(8,128)(2,1)} %get-tuple-element.48.refs_3_) | copy-start | bytes 1069060
  85.5 4.1 %copy-start.8 = (bf16[48,3584]{1,0:T(8,128)(2,1)S(1)}, bf16[48,3584]{1,0:T(8,128)(2,1)}, u32[]{:S(2)}) copy-start(bf16[48,3584]{1,0:T(8,128)(2,1)} %get-tuple-element.41.refs_1_) | copy-start | bytes 1032196
  85.5 4.1 %copy-start.9 = (bf16[16,128]{1,0:T(8,128)(2,1)S(1)}, bf16[16,128]{1,0:T(8,128)(2,1)}, u32[]{:S(2)}) copy-start(bf16[16,128]{1,0:T(8,128)(2,1)} %get-tuple-element.45.refs_0_.refs_3_.refs_7_) | copy-start | bytes 12292
  87.6 31.8 %collective-permute-start.6 = (bf16[96,3584]{1,0:T(8,128)(2,1)}, bf16[96,3584]{1,0:T(8,128)(2,1)}, u32[]{:S(2)}, u32[]{:S(2)}) collective-permute-start(bf16[96,3584]{1,0:T(8,128)(2,1)} %hold.1.refs_10_), channel_id=1, source_target_pairs={{0,2},{1,3},{2,0},{3,1},{4,6},{5,7},{6,4},{7,5},{8,10},{9,11},{10,... | collective-permute-start | bytes 2064392 | tf_op jit(solution)/shard_map/ppermute | solution.py:322
  89.5 1.1 copy-start.2
  90.6 1.0 copy-start.5
  91.6 1.0 copy-start.7
  104.1 4.8 %copy-start.1 = (bf16[384,1024]{1,0:T(8,128)(2,1)}, bf16[384,1024]{1,0:T(8,128)(2,1)S(1)}, u32[]{:S(2)}) copy-start(bf16[384,1024]{1,0:T(8,128)(2,1)S(1)} %get-tuple-element.56.refs_4_) | copy-start | bytes 2359300
  104.1 4.8 %copy-start.12 = (bf16[8,16,128]{2,1,0:T(8,128)(2,1)}, bf16[8,16,128]{2,1,0:T(8,128)(2,1)S(1)}, u32[]{:S(2)}) copy-start(bf16[8,16,128]{2,1,0:T(8,128)(2,1)S(1)} %get-tuple-element.53.refs_2_) | copy-start | bytes 98308
  104.1 15.3 %collective-permute-start.9 = (bf16[384,1792]{1,0:T(8,128)(2,1)}, bf16[384,1792]{1,0:T(8,128)(2,1)}, u32[]{:S(2)}, u32[]{:S(2)}) collective-permute-start(bf16[384,1792]{1,0:T(8,128)(2,1)} %get-tuple-element.59.refs_1_), channel_id=1, source_target_pairs={{0,8},{8,0},{16,24},{24,16},{1,9},{9,1},{17,25},{25,17},{2,10},{10... | collective-permute-start | bytes 4128776 | tf_op jit(solution)/shard_map/ppermute | solution.py:325
  104.2 33.4 %collective-permute-start.10 = (bf16[384,1792]{1,0:T(8,128)(2,1)}, bf16[384,1792]{1,0:T(8,128)(2,1)}, u32[]{:S(2)}, u32[]{:S(2)}) collective-permute-start(bf16[384,1792]{1,0:T(8,128)(2,1)} %get-tuple-element.62), channel_id=1, source_target_pairs={{0,16},{8,24},{16,0},{24,8},{1,17},{9,25},{17,1},{25,9},{2,18},{10... | collective-permute-start | bytes 4128776 | tf_op jit(solution)/shard_map/ppermute | solution.py:325
  108.9 0.6 copy-start.10
  128.3 18.9 %collective-permute-start.12 = (bf16[2,384,1024]{2,1,0:T(8,128)(2,1)}, bf16[2,384,1024]{2,1,0:T(8,128)(2,1)}, u32[]{:S(2)}, u32[]{:S(2)}) collective-permute-start(bf16[2,384,1024]{2,1,0:T(8,128)(2,1)} %get-tuple-element.60.refs_1_.refs_3_), channel_id=1, source_target_pairs={{0,8},{8,0},{16,24},{24,16},{1,9},{9,1},{17,25},{25,17},{2,10},{10... | collective-permute-start | bytes 4718600 | tf_op jit(solution)/shard_map/ppermute | solution.py:325
  128.3 42.5 %collective-permute-start.17 = (bf16[2,384,1024]{2,1,0:T(8,128)(2,1)}, bf16[2,384,1024]{2,1,0:T(8,128)(2,1)}, u32[]{:S(2)}, u32[]{:S(2)}) collective-permute-start(bf16[2,384,1024]{2,1,0:T(8,128)(2,1)} %get-tuple-element.60.refs_1_.refs_3_), channel_id=1, source_target_pairs={{0,16},{8,24},{16,0},{24,8},{1,17},{9,25},{17,1},{25,9},{2,18},{10... | collective-permute-start | bytes 4718600 | tf_op jit(solution)/shard_map/ppermute | solution.py:325
  133.7 39.4 %collective-permute-start.16 = (bf16[464,384]{1,0:T(8,128)(2,1)}, bf16[464,384]{1,0:T(8,128)(2,1)}, u32[]{:S(2)}, u32[]{:S(2)}) collective-permute-start(bf16[464,384]{1,0:T(8,128)(2,1)} %rowgrad.3.refs_6_), channel_id=1, source_target_pairs={{0,7},{1,6},{2,5},{3,4},{4,3},{5,2},{6,1},{7,0},{8,15},{9,14},{10,... | collective-permute-start | bytes 1069064 | tf_op jit(solution)/shard_map/ppermute | solution.py:322
  137.5 9.7 %copy-start = (bf16[2,384,1024]{2,1,0:T(8,128)(2,1)S(1)}, bf16[2,384,1024]{2,1,0:T(8,128)(2,1)}, u32[]{:S(2)}) copy-start(bf16[2,384,1024]{2,1,0:T(8,128)(2,1)} %get-tuple-element.60.refs_1_.refs_3_) | copy-start | bytes 4718596
  144.4 28.7 %collective-permute-start.15 = (bf16[928,384]{1,0:T(8,128)(2,1)}, bf16[928,384]{1,0:T(8,128)(2,1)}, u32[]{:S(2)}, u32[]{:S(2)}) collective-permute-start(bf16[928,384]{1,0:T(8,128)(2,1)} %get-tuple-element.67), channel_id=1, source_target_pairs={{0,2},{1,3},{2,0},{3,1},{4,6},{5,7},{6,4},{7,5},{8,10},{9,11},{10,... | collective-permute-start | bytes 2138120 | tf_op jit(solution)/shard_map/ppermute | solution.py:322
  144.7 32.9 %collective-permute-start.19 = (bf16[464,384]{1,0:T(8,128)(2,1)}, bf16[464,384]{1,0:T(8,128)(2,1)}, u32[]{:S(2)}, u32[]{:S(2)}) collective-permute-start(bf16[464,384]{1,0:T(8,128)(2,1)} %get-tuple-element.63.refs_5_), channel_id=1, source_target_pairs={{0,6},{1,7},{2,4},{3,5},{4,2},{5,3},{6,0},{7,1},{8,14},{9,15},{10,... | collective-permute-start | bytes 1069064 | tf_op jit(solution)/shard_map/ppermute | solution.py:322
  147.2 9.1 %collective-permute-start.11 = (bf16[384,1792]{1,0:T(8,128)(2,1)}, bf16[384,1792]{1,0:T(8,128)(2,1)}, u32[]{:S(2)}, u32[]{:S(2)}) collective-permute-start(bf16[384,1792]{1,0:T(8,128)(2,1)} %collective-permute-done.10.refs_5_.refs_1_), channel_id=1, source_target_pairs={{0,8},{8,0},{16,24},{24,16},{1,9},{9,1},{17,25},{25,17},{2,10},{10... | collective-permute-start | bytes 4128776 | tf_op jit(solution)/shard_map/ppermute | solution.py:325
  147.2 1.0 copy-start.11
  155.6 0.6 copy-start.20
  164.5 29.6 %collective-permute-start.13 = (bf16[464,384]{1,0:T(8,128)(2,1)}, bf16[464,384]{1,0:T(8,128)(2,1)}, u32[]{:S(2)}, u32[]{:S(2)}) collective-permute-start(bf16[464,384]{1,0:T(8,128)(2,1)} %get-tuple-element.65), channel_id=1, source_target_pairs={{0,5},{1,4},{2,7},{3,6},{4,1},{5,0},{6,3},{7,2},{8,13},{9,12},{10,... | collective-permute-start | bytes 1069064 | tf_op jit(solution)/shard_map/ppermute | solution.py:322
  170.8 30.0 %collective-permute-start.14 = (bf16[464,384]{1,0:T(8,128)(2,1)}, bf16[464,384]{1,0:T(8,128)(2,1)}, u32[]{:S(2)}, u32[]{:S(2)}) collective-permute-start(bf16[464,384]{1,0:T(8,128)(2,1)} %get-tuple-element.66), channel_id=1, source_target_pairs={{0,4},{1,5},{2,6},{3,7},{4,0},{5,1},{6,2},{7,3},{8,12},{9,13},{10,... | collective-permute-start | bytes 1069064 | tf_op jit(solution)/shard_map/ppermute | solution.py:322
  172.1 1.0 copy-start.17
  173.1 1.0 copy-start.19
  174.1 3.6 %copy-start.13 = (bf16[8,16,128]{2,1,0:T(8,128)(2,1)S(1)}, bf16[8,16,128]{2,1,0:T(8,128)(2,1)}, u32[]{:S(2)}) copy-start(bf16[8,16,128]{2,1,0:T(8,128)(2,1)} %copy-done.12) | copy-start | bytes 98308
  174.1 3.6 %copy-start.15 = (s32[128,2]{0,1:T(2,128)S(1)}, s32[128,2]{0,1:T(2,128)}, u32[]{:S(2)}) copy-start(s32[128,2]{0,1:T(2,128)} %param.10) | copy-start | bytes 3076
  174.1 3.6 %copy-start.18 = (bf16[464,384]{1,0:T(8,128)(2,1)S(1)}, bf16[464,384]{1,0:T(8,128)(2,1)}, u32[]{:S(2)}) copy-start(bf16[464,384]{1,0:T(8,128)(2,1)} %get-tuple-element.69.refs_1_.refs_3_) | copy-start | bytes 1069060
  176.2 25.1 %collective-permute-start.18 = (bf16[928,384]{1,0:T(8,128)(2,1)}, bf16[928,384]{1,0:T(8,128)(2,1)}, u32[]{:S(2)}, u32[]{:S(2)}) collective-permute-start(bf16[928,384]{1,0:T(8,128)(2,1)} %second_back.1.refs_7_), channel_id=1, source_target_pairs={{0,1},{1,0},{2,3},{3,2},{4,5},{5,4},{6,7},{7,6},{8,9},{9,8},{10,11... | collective-permute-start | bytes 2138120 | tf_op jit(solution)/shard_map/ppermute | solution.py:322
  177.6 3.8 %collective-permute-start.20 = (bf16[2,384,1024]{2,1,0:T(8,128)(2,1)}, bf16[2,384,1024]{2,1,0:T(8,128)(2,1)}, u32[]{:S(2)}, u32[]{:S(2)}) collective-permute-start(bf16[2,384,1024]{2,1,0:T(8,128)(2,1)} %collective-permute-done.17.refs_0_.refs_3_), channel_id=1, source_target_pairs={{0,8},{8,0},{16,24},{24,16},{1,9},{9,1},{17,25},{25,17},{2,10},{10... | collective-permute-start | bytes 4718600 | tf_op jit(solution)/shard_map/ppermute | solution.py:325
  181.4 19.9 %copy-start.14 = (bf16[8,16,128]{2,1,0:T(8,128)(2,1)S(1)}, bf16[8,16,128]{2,1,0:T(8,128)(2,1)}, u32[]{:S(2)}) copy-start(bf16[8,16,128]{2,1,0:T(8,128)(2,1)} %copy-done.12) | copy-start | bytes 98308
  181.4 19.9 %copy-start.16 = (s32[128,2]{0,1:T(2,128)S(1)}, s32[128,2]{0,1:T(2,128)}, u32[]{:S(2)}) copy-start(s32[128,2]{0,1:T(2,128)} %param.10) | copy-start | bytes 3076

commit v4 on v3

--- a/solution.py
+++ b/solution.py
@@ -72,36 +72,37 @@
     weight = jnp.where(first, gates[0:1, :], 0.0) + jnp.where(second, gates[1:2, :], 0.0)
     meta = jnp.concatenate([code, weight], axis=0).astype(BF16)
     meta_ref[...] = meta
-    near_ref, all_ref, rest, y_refs = out_refs[0], out_refs[1], out_refs[2 : 1 - nx], out_refs[1 - nx :]
+    halves = 2 * (nx - 1)
+    near_ref, rest, y_refs = out_refs[0], out_refs[1:-halves], out_refs[-halves:]
     copies[2].wait()
     tokens = tok_ref[...]
-    all_ref[:, 0 : tokens.shape[1]] = tokens
-    add_routing(all_ref, 0, toks, tokens.shape[1], meta)
     near = [(nx + xo, near_ref, xo * cap) for xo in range(nx)]
     pick_rows(cap, code, meta, tokens, near + [(j, ref, 0) for j, ref in enumerate(rest)])
-    by_column = [(zk * nx + xo, y_refs[xo - 1], zk * cap) for zk in range(nz) for xo in range(1, nx)]
+    by_column = [
+        (zk * nx + xo, y_refs[2 * xo - 2 + zk // 2], zk % 2 * cap) for zk in range(nz) for xo in range(1, nx)
+    ]
     copies[3].wait()
     pick_rows(cap, code, meta, cot_ref[...], by_column)
 
 
 def second_kernel(n, nx, cap, meta_ref, cot_ref, *refs):
     nz = n // nx
-    came, y_refs = refs[: nx - 1], refs[nx - 1 :]
+    came, y_refs = refs[: 2 * nx - 2], refs[2 * nx - 2 :]
     meta = meta_ref[...]
     own = [(zk * nx, y_refs[zk], 0) for zk in range(nz)]
     pick_rows(cap, meta.astype(F32)[0:n, :], meta, cot_ref[...], own)
     for xo in range(1, nx):
         for zk in range(nz):
-            y_refs[zk][xo * cap : (xo + 1) * cap, :] = came[xo - 1][zk * cap : (zk + 1) * cap, :]
-
-
-def third_kernel(n, nx, cap, all_ref, near_ref, *refs):
+            at = zk % 2 * cap
+            y_refs[zk][xo * cap : (xo + 1) * cap, :] = came[2 * xo - 2 + zk // 2][at : at + cap, :]
+
+
+def third_kernel(n, nx, cap, all_ref, meta_ref, near_ref, *refs):
     own, x_refs, here_ref, pass_refs = refs[: nx - 1], refs[nx - 1 : 2 * nx - 2], refs[2 * nx - 2], refs[2 * nx - 1 :]
-    toks, wide = all_ref.shape
-    meta = all_ref[0 : 2 * n, wide - toks :]
+    meta = meta_ref[...]
     dest = [(2 * nx, here_ref, 0)] + [(2 * nx + xo, x_refs[xo - 1], 2 * cap) for xo in range(1, nx)]
     dest += [(3 * nx + xo, pass_refs[xo], 0) for xo in range(nx)]
-    pick_rows(cap, meta.astype(F32)[0:n, :], meta, all_ref[:, 0 : wide - toks], dest)
+    pick_rows(cap, meta.astype(F32)[0:n, :], meta, all_ref[...], dest)
     for xo in range(1, nx):
         x_refs[xo - 1][0:cap, :] = own[xo - 1][...]
         x_refs[xo - 1][cap : 2 * cap, :] = near_ref[xo * cap : (xo + 1) * cap, :]
@@ -120,37 +121,41 @@
     out_ref[...] = in_ref[...]
 
 
+def copy_kernel(*refs):
+    count = len(refs) // 2
+    for src, out in zip(refs[:count], refs[count:]):
+        out[...] = src[...]
+
+
 def fence_kernel(out_ref):
     out_ref[...] = jnp.zeros_like(out_ref)
 
 
-def forward_kernel(n, nx, cap, count, ny, place_ref, *refs):
+def gather_kernel(n, nx, cap, count, ny, place_ref, *refs):
     found = found_x(n, nx, cap, refs[:count])
-    meta_ref, gate_ref, up_ref, *out_refs = refs[count:]
-    part_refs, out_refs = out_refs[:ny], out_refs[ny:]
-    hidden_ref, pa_ref, pb_ref, metas_ref, w_ref, rows_ref = out_refs
+    meta_ref, *part_refs = refs[count : count + 1 + ny]
+    rows_ref, w_ref, metas_ref = refs[count + 1 + ny :]
     toks = meta_ref.shape[1]
     d = rows_ref.shape[1]
+    slot = lax.broadcasted_iota(jnp.int32, (cap, toks), 0).astype(F32)
+    for j, (ref, at) in enumerate(found):
+        row = j * cap
+        rows_ref[row : row + cap, :] = ref[at : at + cap, 0:d]
+        if j:
+            metas_ref[j] = ref[at : at + 2 * n, d:]
+        else:
+            metas_ref[j] = meta_ref[...]
+        meta = metas_ref[j].astype(F32)
+        picked = jnp.where(slot == meta[j : j + 1, :], meta[n + j : n + j + 1, :], 0.0)
+        total = jnp.sum(picked, axis=1, keepdims=True)
+        w_ref[row : row + cap, :] = jnp.broadcast_to(total, (cap, w_ref.shape[1]))
     width = part_refs[0].shape[1]
-
-    @pl.when(pl.program_id(0) == 0)
-    def _():
-        slot = lax.broadcasted_iota(jnp.int32, (cap, toks), 0).astype(F32)
-        for j, (ref, at) in enumerate(found):
-            row = j * cap
-            rows_ref[row : row + cap, :] = ref[at : at + cap, 0:d]
-            if j:
-                metas_ref[j] = ref[at : at + 2 * n, d:]
-            else:
-                metas_ref[j] = meta_ref[...]
-            meta = metas_ref[j].astype(F32)
-            picked = jnp.where(slot == meta[j : j + 1, :], meta[n + j : n + j + 1, :], 0.0)
-            total = jnp.sum(picked, axis=1, keepdims=True)
-            w_ref[row : row + cap, :] = jnp.broadcast_to(total, (cap, w_ref.shape[1]))
-        for yo, ref in enumerate(part_refs):
-            at = pl.multiple_of((place_ref[0] ^ yo) * width, 128)
-            ref[...] = rows_ref[:, pl.ds(at, width)]
-
+    for yo, ref in enumerate(part_refs):
+        at = pl.multiple_of((place_ref[0] ^ yo) * width, 128)
+        ref[...] = rows_ref[:, pl.ds(at, width)]
+
+
+def forward_kernel(rows_ref, w_ref, gate_ref, up_ref, hidden_ref, pa_ref, pb_ref):
     a = jnp.dot(rows_ref[...], gate_ref[0], preferred_element_type=F32)
     b = jnp.dot(rows_ref[...], up_ref[0], preferred_element_type=F32)
     w = w_ref[:, 0:1]
@@ -161,10 +166,14 @@
     pb_ref[...] = w * silu
 
 
-def back_kernel(count, *refs):
+def back_kernel(count, steps, me_ref, *refs):
+    del me_ref
     y_refs = refs[:count]
-    hidden_ref, pa_ref, pb_ref, down_ref, grads_ref, score_ref, rows_ref, part_ref = refs[count:]
+    hidden_ref, pa_ref, pb_ref, down_ref, gate_ref, up_ref, grads_ref, score_ref, *refs = refs[count:]
+    out_refs, (rows_ref, part_ref, all_ref) = refs[:-3], refs[-3:]
     step = pl.program_id(0)
+    tile = down_ref.shape[1]
+    feats = gate_ref.shape[1]
 
     @pl.when(step == 0)
     def _():
@@ -174,21 +183,40 @@
             row += ref.shape[0]
         part_ref[...] = jnp.zeros_like(part_ref)
 
-    back = lax.dot_general(rows_ref[...], down_ref[0], NT, preferred_element_type=F32)
-    grads_ref[0] = (back * pa_ref[...]).astype(BF16)
-    grads_ref[1] = (back * pb_ref[...]).astype(BF16)
-    prod = back * hidden_ref[...].astype(F32)
-    part = part_ref[...]
-    for c in range(prod.shape[1] // 128):
-        part = part + prod[:, c * 128 : (c + 1) * 128]
-    part_ref[...] = part
-
-    @pl.when(step == pl.num_programs(0) - 1)
+    @pl.when(step < steps)
+    def _():
+        back = lax.dot_general(rows_ref[...], down_ref[0], NT, preferred_element_type=F32)
+        da = (back * pa_ref[...]).astype(BF16)
+        db = (back * pb_ref[...]).astype(BF16)
+        grads_ref[0] = da
+        grads_ref[1] = db
+        at = pl.ds(pl.multiple_of(step * tile, tile), tile)
+        all_ref[0, :, at] = da
+        all_ref[1, :, at] = db
+        prod = back * hidden_ref[...].astype(F32)
+        part = part_ref[...]
+        for c in range(prod.shape[1] // 128):
+            part = part + prod[:, c * 128 : (c + 1) * 128]
+        part_ref[...] = part
+
+    @pl.when(step == steps - 1)
     def _():
         total = jnp.sum(jnp.transpose(part_ref[...]), axis=0, keepdims=True)
         shape = score_ref.shape
         top = lax.broadcasted_iota(jnp.int32, shape, 0) == 0
         score_ref[...] = jnp.where(top, jnp.broadcast_to(total, shape), 0.0).astype(BF16)
+
+    @pl.when(step >= steps)
+    def _():
+        val = lax.dot_general(gate_ref[0], all_ref[0], NT, preferred_element_type=F32)
+        val = val + lax.dot_general(up_ref[0], all_ref[1], NT, preferred_element_type=F32)
+        val = val.astype(BF16)
+        for i, out in enumerate(out_refs):
+
+            @pl.when(step == steps + i)
+            def _():
+                out[0:feats, :] = val
+                out[feats:, :] = score_ref[...]
 
 
 def rowgrad_kernel(places, dest_ref, grads_ref, score_ref, gate_ref, up_ref, *out_refs):
@@ -212,19 +240,18 @@
         out[size:, :] = came_ref[(i + 1) * size : (i + 2) * size, :]
 
 
-def combine_kernel(n, cap, feats, parts, last, me_ref, ids_ref, metas_ref, *refs):
+def combine_kernel(n, cap, feats, parts, more, last, me_ref, ids_ref, metas_ref, *refs):
     me = me_ref[0]
     rows = n * cap
     toks = metas_ref.shape[2]
     metas = [metas_ref[j].astype(F32) for j in range(n)]
-    if last:
-        total_ref, part_ref, out_ref, gates_ref = refs[-4:]
-        total = total_ref[...]
-        gg = [part_ref[0], part_ref[1]]
+    if more:
+        total = refs[-4][...]
+        gg = [refs[-3][0], refs[-3][1]]
     else:
-        total_ref, part_ref = refs[-2:]
         total = jnp.zeros((feats, n * toks), F32)
         gg = [jnp.zeros((16, toks), F32)] * 2
+    out_ref, gates_ref = refs[-2:]
     row = lax.broadcasted_iota(jnp.int32, (rows, n * toks), 0).astype(F32)
     for k, which, at in parts:
         wanted = []
@@ -239,9 +266,9 @@
         score = jnp.dot(got, pick[:, 0:toks], preferred_element_type=F32)
         gg = [gg[c] + jnp.where(ids_ref[c : c + 1, :] == (me ^ k), score, 0.0) for c in (0, 1)]
     if not last:
-        total_ref[...] = total
-        part_ref[0] = gg[0]
-        part_ref[1] = gg[1]
+        out_ref[...] = total
+        gates_ref[0] = gg[0]
+        gates_ref[1] = gg[1]
         return
     for j in range(n):
         place = pl.multiple_of((me ^ j) * toks, toks)
@@ -364,11 +391,12 @@
 
     sources = [ids_t, gates_t, tokens, cotangent]
     outs = (
-        [shape(2 * n, toks), shape(nx * cap, wide), shape(toks, wide), shape(cap, d)]
+        [shape(2 * n, toks), shape(nx * cap, wide), shape(cap, d)]
         + [shape(cap, wide)] * (nx - 1)
-        + [shape(nz * cap, d)] * (nx - 1)
-    )
-    meta, x_near, x_all, x_own, *made = run(
+        + [shape(nz // 2 * cap, d)] * (2 * nx - 2)
+    )
+    x_all = swap(tokens, 2 * nx)
+    meta, x_near, x_own, *made = run(
         functools.partial(prep_kernel, n, nx, cap),
         "prep",
         outs,
@@ -381,21 +409,23 @@
     )
     x_side, y_side = made[: nx - 1], made[nx - 1 :]
     x_near = swap(x_near, nx)
-    x_all = swap(x_all, 2 * nx)
-    y_side = [swap(v, xo) for xo, v in enumerate(y_side, 1)]
+    meta_all = swap(meta, 2 * nx)
+    y_side = [swap(v, i // 2 + 1) for i, v in enumerate(y_side)]
     y_sent = call(
         functools.partial(second_kernel, n, nx, cap),
         "second",
         [shape(nx * cap, d)] * nz,
         [meta, cotangent, *y_side],
+        weight=1,
         mib=59,
     )
     made = call(
         functools.partial(third_kernel, n, nx, cap),
         "third",
         [shape((nz - 1) * cap, wide)] * (nx - 1) + [shape(cap, wide)] * (1 + nx),
-        [x_all, x_near, *x_side],
+        [x_all, meta_all, x_near, *x_side],
         mib=59,
+        weight=1,
     )
     x_side = [swap(v, xo) for xo, v in enumerate(made[: nx - 1], 1)]
     x_mid, x_passed = made[nx - 1], made[nx:]
@@ -408,40 +438,58 @@
     tile = 256
     steps = h // tile
     column = pl.BlockSpec((rows, tile), lambda i: (0, i))
-    *x_parts, hidden, pa, pb, metas = run(
-        functools.partial(forward_kernel, n, nx, cap, len(got_x), ny),
-        "forward",
+    *x_parts, x_rows, row_w, metas = call(
+        functools.partial(gather_kernel, n, nx, cap, len(got_x), ny),
+        "gather",
         [shape(rows, 2 * block)] * ny
-        + [shape(rows, h), shape(rows, h, dtype=F32), shape(rows, h, dtype=F32)]
-        + [shape(n, 2 * n, toks)],
-        [my_y, *got_x, meta, gate_w, up_w],
-        [smem()]
-        + [whole(v.shape) for v in got_x]
-        + [whole((2 * n, toks))]
-        + [pl.BlockSpec((1, d, tile), lambda i: (0, 0, i))] * 2,
-        [whole((rows, 2 * block))] * ny
-        + [column] * 3
-        + [whole((n, 2 * n, toks))],
-        grid=(steps,),
-        scratch=[pltpu.VMEM((rows, 128), F32), pltpu.VMEM((rows, d), BF16)],
+        + [shape(rows, d), shape(rows, 128, dtype=F32), shape(n, 2 * n, toks)],
+        [my_y, *got_x, meta],
+        scalars=1,
         weight=1,
     )
     x_own_came = swap_dp(x_parts[0], 1)
     x_parts = [x_parts[0]] + [swap_dp(v, 2 * yo) for yo, v in enumerate(x_parts[1:], 1)]
+    hidden, pa, pb = run(
+        forward_kernel,
+        "forward",
+        [shape(rows, h), shape(rows, h, dtype=F32), shape(rows, h, dtype=F32)],
+        [x_rows, row_w, gate_w, up_w],
+        [whole((rows, d)), whole((rows, 128))]
+        + [pl.BlockSpec((1, d, tile), lambda i: (0, 0, i))] * 2,
+        [column] * 3,
+        grid=(steps,),
+        weight=1,
+    )
     fence(y_z)
     got_y = [y_sent[0], y_near, *y_z]
-    grads, score = run(
-        functools.partial(back_kernel, len(got_y)),
+    first_sent = list(range(n - nx + 1, n))
+    held = lambda i: jnp.minimum(i, steps - 1)
+    column_b = pl.BlockSpec((rows, tile), lambda i, _: (0, held(i)))
+
+    def first_owner(i, me_ref):
+        k = jnp.maximum(i - steps, 0) + first_sent[0]
+        return (0, k ^ me_ref[0], 0)
+
+    out_spec = pl.BlockSpec((1, feats, h), first_owner)
+    grads, score, *sent = run(
+        functools.partial(back_kernel, len(got_y), steps),
         "back",
-        [shape(2, rows, h), shape(16, rows)],
-        [*got_y, hidden, pa, pb, down_w],
+        [shape(2, rows, h), shape(16, rows)] + [shape(size, rows)] * (nx - 1),
+        [me_arr, *got_y, hidden, pa, pb, down_w, gate_w, up_w],
         [whole(v.shape) for v in got_y]
-        + [column] * 3
-        + [pl.BlockSpec((1, tile, d), lambda i: (0, i, 0))],
-        [pl.BlockSpec((2, rows, tile), lambda i: (0, 0, i)), whole((16, rows))],
+        + [column_b] * 3
+        + [pl.BlockSpec((1, tile, d), lambda i, _: (0, held(i), 0)), out_spec, out_spec],
+        [pl.BlockSpec((2, rows, tile), lambda i, _: (0, 0, held(i)))]
+        + [whole((16, rows))]
+        + [whole((size, rows))] * (nx - 1),
         after=[x_own_came],
-        grid=(steps,),
-        scratch=[pltpu.VMEM((rows, d), BF16), pltpu.VMEM((rows, 128), F32)],
+        grid=(steps + nx - 1,),
+        scalars=1,
+        scratch=[
+            pltpu.VMEM((rows, d), BF16),
+            pltpu.VMEM((rows, 128), F32),
+            pltpu.VMEM((2, rows, h), BF16),
+        ],
         weight=1,
         mib=59,
     )
@@ -479,7 +527,10 @@
         for k, v in zip(ks, values):
             straight[k] = swap(v, k)
 
-    send(far[1:], rowgrads([(k, i, 0) for i, k in enumerate(far[1:])], [1] * (nx - 1)))
+    sent = call(
+        copy_kernel, "hold", [shape(size, rows)] * (nx - 1), sent, weight=1, mib=59
+    )
+    send(first_sent, sent)
     near, sent = rowgrads(
         [(nx + xo, 0, xo * size) for xo in range(nx)] + [(far[0], 1, 0)],
         [nx, 1],
@@ -525,9 +576,11 @@
     )
     columns = [swap(v, xo) for xo, v in enumerate(sent, 1)]
 
-    def combine(parts, refs, carried, outs):
+    sum_shapes = [shape(feats, n * toks, dtype=F32), shape(2, 16, toks, dtype=F32)]
+
+    def combine(parts, refs, carried, outs, final):
         return call(
-            functools.partial(combine_kernel, n, cap, feats, parts, bool(carried)),
+            functools.partial(combine_kernel, n, cap, feats, parts, bool(carried), final),
             "combine",
             outs,
             [me_arr, ids_t, metas, *refs, *carried],
@@ -539,7 +592,8 @@
         parts,
         [own, near, *[straight[k] for k in far]],
         [],
-        [shape(feats, n * toks, dtype=F32), shape(2, 16, toks, dtype=F32)],
+        sum_shapes,
+        False,
     )
 
     others = ny - 1
@@ -559,14 +613,16 @@
         ],
     )
 
-    parts = [(k, i, 0) for i, k in enumerate(last)]
+    parts = []
     for i in range(nx - 1):
-        parts += [(i + 1, len(last) + i, 0), (nx + i + 1, len(last) + i, size)]
+        parts += [(i + 1, i, 0), (nx + i + 1, i, size)]
+    sums = combine(parts, columns, sums, sum_shapes, False)
     summed, gg = combine(
-        parts,
-        [*[straight[k] for k in last], *columns],
+        [(k, i, 0) for i, k in enumerate(last)],
+        [straight[k] for k in last],
         sums,
         [shape(feats, n * toks), shape(2, toks)],
+        True,
     )
     return summed.T, grad_gate_w, grad_up_w, gg.T
 

time: 207 us -> 202 us (0.976)
  waiting for transfers between devices: 91.3 us -> 78.2 us
  Pallas kernels: 78.5 us -> 82.1 us
  local copies, waits for them, and re-layouts: 9.03 us -> 12.2 us
    ppermute x15 -> x17, waiting for transfers between devices: 85.3 us -> 75.6 us  [swap(): return lax.ppermute(v, 'expert', [(i, i ^ k) for i in range(n)])]
    pallas_call x16 -> x18, Pallas kernels: 78.5 us -> 82.1 us  [run(): pl.pallas_call(trimmed, grid_spec=pltpu.PrefetchScalarGridSpec(num_scalar...]
    ppermute x6, waiting for transfers between devices: 6.01 us -> 2.59 us  [swap_dp(): return lax.ppermute(v, 'dp', [(i, i ^ q) for i in range(ndp)])]
    unnamed x44 -> x56, local copies, waits for them, and re-layouts: 9.03 us -> 12.2 us
    ppermute x15 -> x17, starting transfers between devices: 23 us -> 24.8 us  [swap(): return lax.ppermute(v, 'expert', [(i, i ^ k) for i in range(n)])]
  transfers between devices with their start and end apart: 21 -> 23, of which waited for: 13 -> 9; matrix products, arithmetic and copies ran while one was open for 0% -> 0% of each run, Pallas kernels for 32% -> 37%
where the time goes in v4:
time: 202 us; the launch traced here: 201 us
  Pallas kernels  82.1 us (41%)
  waiting for transfers between devices  78.2 us (39%)
  starting transfers between devices  28 us (14%)
  local copies, waits for them, and re-layouts  12.2 us (6%)
    pallas_call x18, Pallas kernels, run(): pl.pallas_call(trimmed, grid_spec=pltpu.PrefetchScalarGridSpec(num_scalar...  82.1 us
    ppermute x17, waiting for transfers between devices, swap(): return lax.ppermute(v, 'expert', [(i, i ^ k) for i in range(n)])  75.6 us
    ppermute x17, starting transfers between devices, swap(): return lax.ppermute(v, 'expert', [(i, i ^ k) for i in range(n)])  24.8 us
    unnamed x56, local copies, waits for them, and re-layouts  12.2 us
  transfers between devices with their start and end apart: 23, of which 9 were waited for; matrix products, arithmetic and copies ran while one was open for 0% of the time, Pallas kernels for 37%

profile of v4, /device:TPU:0, one launch (start us, length us, event | category | flops | bytes accessed | tf_op | source)
XLA Modules:
  0.0 201.4 jit_solution(2395301635857025411)
XLA Ops:
  0.6 4.1 %collective-permute-start.1 = (bf16[128,3584]{1,0:T(8,128)(2,1)}, bf16[128,3584]{1,0:T(8,128)(2,1)}, u32[]{:S(2)}, u32[]{:S(2)}) collective-permute-start(bf16[128,3584]{1,0:T(8,128)(2,1)} %refs_3_.4), channel_id=1, source_target_pairs={{0,4},{1,5},{2,6},{3,7},{4,0},{5,1},{6,2},{7,3},{8,12},{9,13},{10,... | collective-permute-start | bytes 2752520 | tf_op jit(solution)/shard_map/ppermute | solution.py:349
  4.7 3.4 %prep.1 = (bf16[16,128]{1,0:T(8,128)(2,1)}, bf16[96,3712]{1,0:T(8,128)(2,1)}, bf16[48,3584]{1,0:T(8,128)(2,1)}, bf16[48,3712]{1,0:T(8,128)(2,1)}, bf16[96,3584]{1,0:T(8,128)(2,1)}, /*index=5*/bf16[96,3584]{1,0:T(8,128)(2,1)}) custom-call(s32[1]{0:T(128)} %bitcast.refs_0_, s32[2,128]{1,0:T(2,128)} %bitcast.7, bf16[2,128]{1,0:T(2,128)(2,1)} %bitcast.11, ...), custom_call_target="tpu_custom_call" | custom-call | flops 1099511627776 | bytes 1 | tf_op jit(solution)/shard_map/prep/pallas_call | solution.py:366
  8.2 1.6 collective-permute-start
  9.8 1.5 collective-permute-start.3
  12.2 16.2 %collective-permute-done.3.refs_2_ = bf16[96,3584]{1,0:T(8,128)(2,1)S(1)} collective-permute-done((bf16[96,3584]{1,0:T(8,128)(2,1)}, bf16[96,3584]{1,0:T(8,128)(2,1)S(1)}, u32[]{:S(2)}, u32[]{:S(2)}) %collective-permute-start.3) | collective-permute-done | bytes 688160 | tf_op jit(solution)/shard_map/ppermute | solution.py:349
  28.4 13.0 %collective-permute-done.4.refs_3_ = bf16[96,3584]{1,0:T(8,128)(2,1)S(1)} collective-permute-done((bf16[96,3584]{1,0:T(8,128)(2,1)}, bf16[96,3584]{1,0:T(8,128)(2,1)S(1)}, u32[]{:S(2)}, u32[]{:S(2)}) %collective-permute-start.4) | collective-permute-done | bytes 688160 | tf_op jit(solution)/shard_map/ppermute | solution.py:349
  41.4 0.8 copy-done.26
  42.2 3.8 %second.1 = (bf16[96,3584]{1,0:T(8,128)(2,1)}, bf16[96,3584]{1,0:T(8,128)(2,1)}, bf16[96,3584]{1,0:T(8,128)(2,1)}, bf16[96,3584]{1,0:T(8,128)(2,1)}) custom-call(bf16[16,128]{1,0:T(8,128)(2,1)} %get-tuple-element.48.refs_0_.refs_4_.refs_7_, bf16[128,3584]{1,0:T(8,128)(2,1)} %refs_1_.1, bf16[96,3584]{1,0:T(8,128)(2,1)} %copy-done.25, ...), custom_call_target="tpu_custom_call" | custom-call | flops 1 | bytes 1 | tf_op jit(solution)/shard_map/second/pallas_call | solution.py:366
  46.9 3.3 %third.1 = (bf16[144,3712]{1,0:T(8,128)(2,1)}, bf16[48,3712]{1,0:T(8,128)(2,1)}, bf16[48,3712]{1,0:T(8,128)(2,1)}, bf16[48,3712]{1,0:T(8,128)(2,1)}) custom-call(bf16[128,3584]{1,0:T(8,128)(2,1)} %collective-permute-done.1.refs_0_, bf16[16,128]{1,0:T(8,128)(2,1)} %copy-done.27, bf16[96,3712]{1,0:T(8,128)(2,1)} %copy-done, ...), custom_call_target="tpu_custom_call" | custom-call | flops 1 | bytes 1 | tf_op jit(solution)/shard_map/third/pallas_call | solution.py:366
  50.7 2.5 %collective-permute-start.7 = (bf16[48,3712]{1,0:T(8,128)(2,1)}, bf16[48,3712]{1,0:T(8,128)(2,1)S(1)}, u32[]{:S(2)}, u32[]{:S(2)}) collective-permute-start(bf16[48,3712]{1,0:T(8,128)(2,1)} %get-tuple-element.56), channel_id=1, source_target_pairs={{0,3},{1,2},{2,1},{3,0},{4,7},{5,6},{6,5},{7,4},{8,11},{9,10},{10,... | collective-permute-start | bytes 1069064 | tf_op jit(solution)/shard_map/ppermute | solution.py:349
  53.2 1.3 collective-permute-start.9
  54.4 1.5 collective-permute-start.10
  56.5 18.3 %collective-permute-done.6.refs_1_.refs_5_ = bf16[48,3712]{1,0:T(8,128)(2,1)S(1)} collective-permute-done((bf16[48,3712]{1,0:T(8,128)(2,1)}, bf16[48,3712]{1,0:T(8,128)(2,1)S(1)}, u32[]{:S(2)}, u32[]{:S(2)}) %collective-permute-start.6) | collective-permute-done | bytes 356384 | tf_op jit(solution)/shard_map/ppermute | solution.py:349
  74.8 6.6 %collective-permute-done.7.refs_2_.refs_6_ = bf16[48,3712]{1,0:T(8,128)(2,1)S(1)} collective-permute-done((bf16[48,3712]{1,0:T(8,128)(2,1)}, bf16[48,3712]{1,0:T(8,128)(2,1)S(1)}, u32[]{:S(2)}, u32[]{:S(2)}) %collective-permute-start.7) | collective-permute-done | bytes 356384 | tf_op jit(solution)/shard_map/ppermute | solution.py:349
  81.4 0.8 copy-done.9
  82.2 2.1 %hold.2.refs_8_ = bf16[96,3584]{1,0:T(8,128)(2,1)} custom-call(bf16[96,3584]{1,0:T(8,128)(2,1)} %get-tuple-element.57.refs_0_, bf16[48,3712]{1,0:T(8,128)(2,1)} %copy-done.7, bf16[48,3712]{1,0:T(8,128)(2,1)} %copy-done.9, bf16[48,3712]{1,0:T(8,128)(2,1)} %get-tuple-element.53.refs_3_), custom_call_target="tpu_custom_call" | custom-call | flops 1099511627776 | bytes 1 | tf_op jit(solution)/shard_map/hold/pallas_call | solution.py:366
  84.3 4.3 %collective-permute-done.5.refs_4_ = bf16[144,3712]{1,0:T(8,128)(2,1)} collective-permute-done((bf16[144,3712]{1,0:T(8,128)(2,1)}, bf16[144,3712]{1,0:T(8,128)(2,1)}, u32[]{:S(2)}, u32[]{:S(2)}) %collective-permute-start.5) | collective-permute-done | bytes 1069088 | tf_op jit(solution)/shard_map/ppermute | solution.py:349
  88.6 1.1 copy-done.5
  89.7 1.0 copy-done.8
  90.7 1.0 copy-done.10
  91.7 3.9 %gather.1 = (bf16[384,1792]{1,0:T(8,128)(2,1)}, bf16[384,1792]{1,0:T(8,128)(2,1)}, bf16[384,3584]{1,0:T(8,128)(2,1)}, f32[384,128]{1,0:T(8,128)S(1)}, bf16[8,16,128]{2,1,0:T(8,128)(2,1)S(1)}) custom-call(s32[1]{0:T(128)} %bitcast.2.refs_0_, bf16[48,3584]{1,0:T(8,128)(2,1)S(1)} %copy-done.11, bf16[96,3712]{1,0:T(8,128)(2,1)S(1)} %copy-done.1, ...), custom_call_target="tpu_custom_call" | custom-call | flops 1 | bytes 1 | tf_op jit(solution)/shard_map/gather/pallas_call | solution.py:366
  95.6 1.5 collective-permute-start.12
  97.1 10.3 %forward.1 = (bf16[384,1024]{1,0:T(8,128)(2,1)S(1)}, f32[384,1024]{1,0:T(8,128)S(1)}, f32[384,1024]{1,0:T(8,128)S(1)}) custom-call(bf16[384,3584]{1,0:T(8,128)(2,1)} %get-tuple-element.61.refs_0_, f32[384,128]{1,0:T(8,128)S(1)} %get-tuple-element.62.refs_1_, bf16[1,3584,1024]{2,1,0:T(8,128)(2,1)} %refs_3_.7, bf16[1,3584,1024]{2,1,0:T(8,128)(2,1)} %refs_4_.5, ...), custom_call_target="tpu_custom_call" | custom-call | flops 1 | bytes 1 | tf_op jit(solution)/shard_map/forward/pallas_call | solution.py:366
  107.4 1.1 copy-done.2
  108.6 1.1 copy-done.3
  110.0 0.6 copy-done.16
  110.6 4.8 %collective-permute-done.8.refs_2_ = bf16[96,3584]{1,0:T(8,128)(2,1)} collective-permute-done((bf16[96,3584]{1,0:T(8,128)(2,1)}, bf16[96,3584]{1,0:T(8,128)(2,1)}, u32[]{:S(2)}, u32[]{:S(2)}) %collective-permute-start.8) | collective-permute-done | bytes 688160 | tf_op jit(solution)/shard_map/ppermute | solution.py:349
  115.4 11.3 %back.1 = (bf16[2,384,1024]{2,1,0:T(8,128)(2,1)}, bf16[16,384]{1,0:T(8,128)(2,1)}, bf16[464,384]{1,0:T(8,128)(2,1)}) custom-call(s32[1]{0:T(128)} %bitcast.refs_0_, bf16[96,3584]{1,0:T(8,128)(2,1)} %get-tuple-element.52.refs_4_.refs_1_, bf16[96,3584]{1,0:T(8,128)(2,1)} %collective-permute-done.8.refs_2_, ...), custom_call_target="tpu_custom_call" | custom-call | flops 1 | bytes 1 | tf_op jit(solution)/shard_map/back/pallas_call | solution.py:366
  126.7 1.6 collective-permute-start.19
  128.3 1.7 hold.3.refs_6_
  130.0 2.9 %collective-permute-start.18 = (bf16[464,384]{1,0:T(8,128)(2,1)}, bf16[464,384]{1,0:T(8,128)(2,1)}, u32[]{:S(2)}, u32[]{:S(2)}) collective-permute-start(bf16[464,384]{1,0:T(8,128)(2,1)} %hold.3.refs_6_), channel_id=1, source_target_pairs={{0,7},{1,6},{2,5},{3,4},{4,3},{5,2},{6,1},{7,0},{8,15},{9,14},{10,... | collective-permute-start | bytes 1069064 | tf_op jit(solution)/shard_map/ppermute | solution.py:349
  132.9 6.9 %rowgrad.2 = (bf16[928,384]{1,0:T(8,128)(2,1)}, bf16[464,384]{1,0:T(8,128)(2,1)}) custom-call(s32[1]{0:T(128)} %bitcast.refs_0_, bf16[2,384,1024]{2,1,0:T(8,128)(2,1)} %get-tuple-element.67.refs_1_.refs_3_, bf16[16,384]{1,0:T(8,128)(2,1)} %get-tuple-element.68.refs_1_.refs_2_, bf16[1,3584,1024]{2,1,0:T(8,128)(2,1)} %refs_3_.7, ...), custom_call_target="tpu_custom_call" | custom-call | flops 1099511627776 | bytes 1 | tf_op jit(solution)/shard_map/rowgrad/pallas_call | solution.py:366
  140.1 0.9 collective-permute-start.21
  141.1 1.0 copy-done.18
  142.0 7.4 %weights.1 = (bf16[2,896,1024]{2,1,0:T(8,128)(2,1)}, f32[8,128]{1,0:T(8,128)S(1)}) custom-call(s32[1]{0:T(128)} %bitcast.4.refs_0_, bf16[384,1792]{1,0:T(8,128)(2,1)} %get-tuple-element.66.refs_1_, bf16[384,1792]{1,0:T(8,128)(2,1)} %collective-permute-done.11.refs_11_.refs_2_, bf16[2,384,1024]{2,1,0:T(8,128)(2,1)S(1)} %copy-done.17, ...), custom_call_target="tpu_custom_call" | custom-call | flops 1099511627776 | bytes 1 | tf_op jit(solution)/shard_map/weights/pallas_call | solution.py:366
  149.5 0.6 copy-done.24
  150.1 8.2 %rowgrad.3 = (bf16[464,384]{1,0:T(8,128)(2,1)}, bf16[464,384]{1,0:T(8,128)(2,1)}, bf16[464,384]{1,0:T(8,128)(2,1)}, bf16[464,384]{1,0:T(8,128)(2,1)}) custom-call(s32[1]{0:T(128)} %bitcast.refs_0_, bf16[2,384,1024]{2,1,0:T(8,128)(2,1)} %get-tuple-element.67.refs_1_.refs_3_, bf16[16,384]{1,0:T(8,128)(2,1)} %get-tuple-element.68.refs_1_.refs_2_, ...), custom_call_target="tpu_custom_call" | custom-call | flops 1099511627776 | bytes 1 | tf_op jit(solution)/shard_map/rowgrad/pallas_call | solution.py:366
  158.3 3.2 %collective-permute-start.15 = (bf16[464,384]{1,0:T(8,128)(2,1)}, bf16[464,384]{1,0:T(8,128)(2,1)}, u32[]{:S(2)}, u32[]{:S(2)}) collective-permute-start(bf16[464,384]{1,0:T(8,128)(2,1)} %get-tuple-element.73), channel_id=1, source_target_pairs={{0,5},{1,4},{2,7},{3,6},{4,1},{5,0},{6,3},{7,2},{8,13},{9,12},{10,... | collective-permute-start | bytes 1069064 | tf_op jit(solution)/shard_map/ppermute | solution.py:349
  161.5 2.4 %collective-permute-done.19.refs_0_.refs_3_ = bf16[2,384,1024]{2,1,0:T(8,128)(2,1)} collective-permute-done((bf16[2,384,1024]{2,1,0:T(8,128)(2,1)}, bf16[2,384,1024]{2,1,0:T(8,128)(2,1)}, u32[]{:S(2)}, u32[]{:S(2)}) %collective-permute-start.19) | collective-permute-done | bytes 1572896 | tf_op jit(solution)/shard_map/ppermute | solution.py:352
  163.8 2.6 %collective-permute-start.16 = (bf16[464,384]{1,0:T(8,128)(2,1)}, bf16[464,384]{1,0:T(8,128)(2,1)}, u32[]{:S(2)}, u32[]{:S(2)}) collective-permute-start(bf16[464,384]{1,0:T(8,128)(2,1)} %get-tuple-element.74), channel_id=1, source_target_pairs={{0,4},{1,5},{2,6},{3,7},{4,0},{5,1},{6,2},{7,3},{8,12},{9,13},{10,... | collective-permute-start | bytes 1069064 | tf_op jit(solution)/shard_map/ppermute | solution.py:349
  166.5 1.0 copy-done.21
  167.5 1.0 copy-done.23
  168.4 2.1 %second_back.1.refs_7_ = bf16[928,384]{1,0:T(8,128)(2,1)} custom-call(bf16[928,384]{1,0:T(8,128)(2,1)} %collective-permute-done.17.refs_0_.refs_4_, bf16[464,384]{1,0:T(8,128)(2,1)S(1)} %copy-done.23, bf16[464,384]{1,0:T(8,128)(2,1)} %collective-permute-done.18.refs_2_.refs_6_, f32[8,128]{1,0:T(8,128)S(1)} %fence.3.refs_3_), custom_call_target="tpu_custom_call" | custom-call | flops 1099511627776 | bytes 1 | tf_op jit(solution)/shard_map/second_back/pallas_call | solution.py:366
  171.1 3.5 %combine.3 = (f32[448,1024]{1,0:T(8,128)S(1)}, f32[2,16,128]{2,1,0:T(8,128)S(1)}) custom-call(s32[1]{0:T(128)} %bitcast.refs_0_, s32[2,128]{1,0:T(2,128)S(1)} %bitcast.8, bf16[8,16,128]{2,1,0:T(8,128)(2,1)S(1)} %copy-done.14, bf16[464,384]{1,0:T(8,128)(2,1)S(1)} %copy-done.22, bf16[928,384]{1,0:T(8,128)(2,1)} %collective-permute-done.17.refs_0_.refs_4_, ...), custom_call_target="tpu_custom_call" | custom-call | flops 1099511627776 | bytes 1 | tf_op jit(solution)/shard_map/combine/pallas_call | solution.py:366
  174.8 8.4 %weights_rest.1 = (bf16[1,896,1024]{2,1,0:T(8,128)(2,1)}, bf16[1,896,1024]{2,1,0:T(8,128)(2,1)}, f32[8,128]{1,0:T(8,128)S(1)}) custom-call(s32[1]{0:T(128)} %bitcast.4.refs_0_, bf16[384,1792]{1,0:T(8,128)(2,1)} %collective-permute-done.12.refs_5_.refs_1_, bf16[384,1792]{1,0:T(8,128)(2,1)} %collective-permute-done.13.refs_5_.refs_2_, ...), custom_call_target="tpu_custom_call" | custom-call | flops 1099511627776 | bytes 1 | tf_op jit(solution)/shard_map/weights_rest/pallas_call | solution.py:366
  183.2 12.4 %collective-permute-done.20.refs_3_ = bf16[928,384]{1,0:T(8,128)(2,1)} collective-permute-done((bf16[928,384]{1,0:T(8,128)(2,1)}, bf16[928,384]{1,0:T(8,128)(2,1)}, u32[]{:S(2)}, u32[]{:S(2)}) %collective-permute-start.20) | collective-permute-done | bytes 712736 | tf_op jit(solution)/shard_map/ppermute | solution.py:349
  195.6 2.3 %combine.4 = (f32[448,1024]{1,0:T(8,128)S(1)}, f32[2,16,128]{2,1,0:T(8,128)S(1)}) custom-call(s32[1]{0:T(128)} %bitcast.refs_0_, s32[2,128]{1,0:T(2,128)S(1)} %bitcast.9, bf16[8,16,128]{2,1,0:T(8,128)(2,1)S(1)} %copy-done.15, bf16[928,384]{1,0:T(8,128)(2,1)} %collective-permute-done.20.refs_3_, f32[448,1024]{1,0:T(8,128)S(1)} %get-tuple-element.78.refs_4_, ...), custom_call_target="tpu_custom_call" | custom-call | flops 1099511627776 | bytes 1 | tf_op jit(solution)/shard_map/combine/pallas_call | solution.py:366
  197.9 3.4 %combine.5 = (bf16[448,1024]{1,0:T(8,128)(2,1)}, bf16[2,128]{1,0:T(2,128)(2,1)}) custom-call(s32[1]{0:T(128)} %bitcast.refs_0_, s32[2,128]{1,0:T(2,128)S(1)} %bitcast.10, bf16[8,16,128]{2,1,0:T(8,128)(2,1)S(1)} %copy-done.15, bf16[464,384]{1,0:T(8,128)(2,1)} %collective-permute-done.15.refs_3_, bf16[464,384]{1,0:T(8,128)(2,1)} %collective-permute-done.16.refs_4_, ...), custom_call_target="tpu_custom_call" | custom-call | flops 1099511627776 | bytes 1 | tf_op jit(solution)/shard_map/combine/pallas_call | solution.py:366
  (72 shorter events, 4.2 us)
Async XLA Ops:
  0.6 45.4 %collective-permute-start.1 = (bf16[128,3584]{1,0:T(8,128)(2,1)}, bf16[128,3584]{1,0:T(8,128)(2,1)}, u32[]{:S(2)}, u32[]{:S(2)}) collective-permute-start(bf16[128,3584]{1,0:T(8,128)(2,1)} %refs_3_.4), channel_id=1, source_target_pairs={{0,4},{1,5},{2,6},{3,7},{4,0},{5,1},{6,2},{7,3},{8,12},{9,13},{10,... | collective-permute-start | bytes 2752520 | tf_op jit(solution)/shard_map/ppermute | solution.py:349
  8.2 37.8 %collective-permute-start = (bf16[96,3712]{1,0:T(8,128)(2,1)}, bf16[96,3712]{1,0:T(8,128)(2,1)S(1)}, u32[]{:S(2)}, u32[]{:S(2)}) collective-permute-start(bf16[96,3712]{1,0:T(8,128)(2,1)} %get-tuple-element.47), channel_id=1, source_target_pairs={{0,2},{1,3},{2,0},{3,1},{4,6},{5,7},{6,4},{7,5},{8,10},{9,11},{10,... | collective-permute-start | bytes 2138120 | tf_op jit(solution)/shard_map/ppermute | solution.py:349
  9.8 18.6 %collective-permute-start.3 = (bf16[96,3584]{1,0:T(8,128)(2,1)}, bf16[96,3584]{1,0:T(8,128)(2,1)S(1)}, u32[]{:S(2)}, u32[]{:S(2)}) collective-permute-start(bf16[96,3584]{1,0:T(8,128)(2,1)} %get-tuple-element.50), channel_id=1, source_target_pairs={{0,1},{1,0},{2,3},{3,2},{4,5},{5,4},{6,7},{7,6},{8,9},{9,8},{10,11... | collective-permute-start | bytes 2064392 | tf_op jit(solution)/shard_map/ppermute | solution.py:349
  11.3 30.1 %collective-permute-start.4 = (bf16[96,3584]{1,0:T(8,128)(2,1)}, bf16[96,3584]{1,0:T(8,128)(2,1)S(1)}, u32[]{:S(2)}, u32[]{:S(2)}) collective-permute-start(bf16[96,3584]{1,0:T(8,128)(2,1)} %get-tuple-element.51), channel_id=1, source_target_pairs={{0,1},{1,0},{2,3},{3,2},{4,5},{5,4},{6,7},{7,6},{8,9},{9,8},{10,11... | collective-permute-start | bytes 2064392 | tf_op jit(solution)/shard_map/ppermute | solution.py:349
  11.8 34.2 %collective-permute-start.2 = (bf16[16,128]{1,0:T(8,128)(2,1)}, bf16[16,128]{1,0:T(8,128)(2,1)S(1)}, u32[]{:S(2)}, u32[]{:S(2)}) collective-permute-start(bf16[16,128]{1,0:T(8,128)(2,1)} %get-tuple-element.48.refs_0_.refs_4_.refs_7_), channel_id=1, source_target_pairs={{0,4},{1,5},{2,6},{3,7},{4,0},{5,1},{6,2},{7,3},{8,12},{9,13},{10,... | collective-permute-start | bytes 12296 | tf_op jit(solution)/shard_map/ppermute | solution.py:349
  28.4 13.0 %copy-start.25 = (bf16[96,3584]{1,0:T(8,128)(2,1)}, bf16[96,3584]{1,0:T(8,128)(2,1)S(1)}, u32[]{:S(2)}) copy-start(bf16[96,3584]{1,0:T(8,128)(2,1)S(1)} %collective-permute-done.3.refs_2_) | copy-start | bytes 2064388
  41.4 0.8 copy-start.26
  46.0 0.9 copy-start
  50.2 24.6 %collective-permute-start.6 = (bf16[48,3712]{1,0:T(8,128)(2,1)}, bf16[48,3712]{1,0:T(8,128)(2,1)S(1)}, u32[]{:S(2)}, u32[]{:S(2)}) collective-permute-start(bf16[48,3712]{1,0:T(8,128)(2,1)} %get-tuple-element.55), channel_id=1, source_target_pairs={{0,2},{1,3},{2,0},{3,1},{4,6},{5,7},{6,4},{7,5},{8,10},{9,11},{10,... | collective-permute-start | bytes 1069064 | tf_op jit(solution)/shard_map/ppermute | solution.py:349
  50.7 30.8 %collective-permute-start.7 = (bf16[48,3712]{1,0:T(8,128)(2,1)}, bf16[48,3712]{1,0:T(8,128)(2,1)S(1)}, u32[]{:S(2)}, u32[]{:S(2)}) collective-permute-start(bf16[48,3712]{1,0:T(8,128)(2,1)} %get-tuple-element.56), channel_id=1, source_target_pairs={{0,3},{1,2},{2,1},{3,0},{4,7},{5,6},{6,5},{7,4},{8,11},{9,10},{10,... | collective-permute-start | bytes 1069064 | tf_op jit(solution)/shard_map/ppermute | solution.py:349
  53.2 55.4 %collective-permute-start.9 = (bf16[96,3584]{1,0:T(8,128)(2,1)}, bf16[96,3584]{1,0:T(8,128)(2,1)}, u32[]{:S(2)}, u32[]{:S(2)}) collective-permute-start(bf16[96,3584]{1,0:T(8,128)(2,1)} %get-tuple-element.59), channel_id=1, source_target_pairs={{0,4},{1,5},{2,6},{3,7},{4,0},{5,1},{6,2},{7,3},{8,12},{9,13},{10,... | collective-permute-start | bytes 2064392 | tf_op jit(solution)/shard_map/ppermute | solution.py:349
  54.4 54.1 %collective-permute-start.10 = (bf16[96,3584]{1,0:T(8,128)(2,1)}, bf16[96,3584]{1,0:T(8,128)(2,1)}, u32[]{:S(2)}, u32[]{:S(2)}) collective-permute-start(bf16[96,3584]{1,0:T(8,128)(2,1)} %get-tuple-element.60), channel_id=1, source_target_pairs={{0,6},{1,7},{2,4},{3,5},{4,2},{5,3},{6,0},{7,1},{8,14},{9,15},{10,... | collective-permute-start | bytes 2064392 | tf_op jit(solution)/shard_map/ppermute | solution.py:349
  56.0 32.6 %collective-permute-start.5 = (bf16[144,3712]{1,0:T(8,128)(2,1)}, bf16[144,3712]{1,0:T(8,128)(2,1)}, u32[]{:S(2)}, u32[]{:S(2)}) collective-permute-start(bf16[144,3712]{1,0:T(8,128)(2,1)} %get-tuple-element.54), channel_id=1, source_target_pairs={{0,1},{1,0},{2,3},{3,2},{4,5},{5,4},{6,7},{7,6},{8,9},{9,8},{10,11... | collective-permute-start | bytes 3207176 | tf_op jit(solution)/shard_map/ppermute | solution.py:349
  74.8 6.6 %copy-start.7 = (bf16[48,3712]{1,0:T(8,128)(2,1)}, bf16[48,3712]{1,0:T(8,128)(2,1)S(1)}, u32[]{:S(2)}) copy-start(bf16[48,3712]{1,0:T(8,128)(2,1)S(1)} %collective-permute-done.6.refs_1_.refs_5_) | copy-start | bytes 1069060
  81.4 0.8 copy-start.9
  82.2 6.4 %copy-start.1 = (bf16[96,3712]{1,0:T(8,128)(2,1)S(1)}, bf16[96,3712]{1,0:T(8,128)(2,1)}, u32[]{:S(2)}) copy-start(bf16[96,3712]{1,0:T(8,128)(2,1)} %copy-done) | copy-start | bytes 2138116
  82.2 6.4 %copy-start.6 = (bf16[48,3712]{1,0:T(8,128)(2,1)S(1)}, bf16[48,3712]{1,0:T(8,128)(2,1)}, u32[]{:S(2)}) copy-start(bf16[48,3712]{1,0:T(8,128)(2,1)} %get-tuple-element.53.refs_3_) | copy-start | bytes 1069060
  82.2 6.4 %copy-start.11 = (bf16[48,3584]{1,0:T(8,128)(2,1)S(1)}, bf16[48,3584]{1,0:T(8,128)(2,1)}, u32[]{:S(2)}) copy-start(bf16[48,3584]{1,0:T(8,128)(2,1)} %get-tuple-element.46.refs_1_) | copy-start | bytes 1032196
  82.2 6.4 %copy-start.12 = (bf16[16,128]{1,0:T(8,128)(2,1)S(1)}, bf16[16,128]{1,0:T(8,128)(2,1)}, u32[]{:S(2)}) copy-start(bf16[16,128]{1,0:T(8,128)(2,1)} %get-tuple-element.48.refs_0_.refs_4_.refs_7_) | copy-start | bytes 12292
  84.3 31.0 %collective-permute-start.8 = (bf16[96,3584]{1,0:T(8,128)(2,1)}, bf16[96,3584]{1,0:T(8,128)(2,1)}, u32[]{:S(2)}, u32[]{:S(2)}) collective-permute-start(bf16[96,3584]{1,0:T(8,128)(2,1)} %hold.2.refs_8_), channel_id=1, source_target_pairs={{0,2},{1,3},{2,0},{3,1},{4,6},{5,7},{6,4},{7,5},{8,10},{9,11},{10,... | collective-permute-start | bytes 2064392 | tf_op jit(solution)/shard_map/ppermute | solution.py:349
  88.6 1.1 copy-start.5
  89.7 1.0 copy-start.8
  90.7 1.0 copy-start.10
  95.6 11.9 %copy-start.13 = (bf16[8,16,128]{2,1,0:T(8,128)(2,1)}, bf16[8,16,128]{2,1,0:T(8,128)(2,1)S(1)}, u32[]{:S(2)}) copy-start(bf16[8,16,128]{2,1,0:T(8,128)(2,1)S(1)} %get-tuple-element.58.refs_4_.refs_2_) | copy-start | bytes 98308
  95.6 19.8 %collective-permute-start.11 = (bf16[384,1792]{1,0:T(8,128)(2,1)}, bf16[384,1792]{1,0:T(8,128)(2,1)}, u32[]{:S(2)}, u32[]{:S(2)}) collective-permute-start(bf16[384,1792]{1,0:T(8,128)(2,1)} %get-tuple-element.66.refs_1_), channel_id=1, source_target_pairs={{0,8},{8,0},{16,24},{24,16},{1,9},{9,1},{17,25},{25,17},{2,10},{10... | collective-permute-start | bytes 4128776 | tf_op jit(solution)/shard_map/ppermute | solution.py:352
  95.6 37.3 %collective-permute-start.12 = (bf16[384,1792]{1,0:T(8,128)(2,1)}, bf16[384,1792]{1,0:T(8,128)(2,1)}, u32[]{:S(2)}, u32[]{:S(2)}) collective-permute-start(bf16[384,1792]{1,0:T(8,128)(2,1)} %get-tuple-element.69), channel_id=1, source_target_pairs={{0,16},{8,24},{16,0},{24,8},{1,17},{9,25},{17,1},{25,9},{2,18},{10... | collective-permute-start | bytes 4128776 | tf_op jit(solution)/shard_map/ppermute | solution.py:352
  107.4 1.1 copy-start.2
  108.6 1.1 copy-start.3
  108.6 1.4 copy-start.4
  126.6 14.4 %collective-permute-start.14 = (bf16[2,384,1024]{2,1,0:T(8,128)(2,1)}, bf16[2,384,1024]{2,1,0:T(8,128)(2,1)}, u32[]{:S(2)}, u32[]{:S(2)}) collective-permute-start(bf16[2,384,1024]{2,1,0:T(8,128)(2,1)} %get-tuple-element.67.refs_1_.refs_3_), channel_id=1, source_target_pairs={{0,8},{8,0},{16,24},{24,16},{1,9},{9,1},{17,25},{25,17},{2,10},{10... | collective-permute-start | bytes 4718600 | tf_op jit(solution)/shard_map/ppermute | solution.py:352
  126.7 37.1 %collective-permute-start.19 = (bf16[2,384,1024]{2,1,0:T(8,128)(2,1)}, bf16[2,384,1024]{2,1,0:T(8,128)(2,1)}, u32[]{:S(2)}, u32[]{:S(2)}) collective-permute-start(bf16[2,384,1024]{2,1,0:T(8,128)(2,1)} %get-tuple-element.67.refs_1_.refs_3_), channel_id=1, source_target_pairs={{0,16},{8,24},{16,0},{24,8},{1,17},{9,25},{17,1},{25,9},{2,18},{10... | collective-permute-start | bytes 4718600 | tf_op jit(solution)/shard_map/ppermute | solution.py:352
  130.0 37.4 %collective-permute-start.18 = (bf16[464,384]{1,0:T(8,128)(2,1)}, bf16[464,384]{1,0:T(8,128)(2,1)}, u32[]{:S(2)}, u32[]{:S(2)}) collective-permute-start(bf16[464,384]{1,0:T(8,128)(2,1)} %hold.3.refs_6_), channel_id=1, source_target_pairs={{0,7},{1,6},{2,5},{3,4},{4,3},{5,2},{6,1},{7,0},{8,15},{9,14},{10,... | collective-permute-start | bytes 1069064 | tf_op jit(solution)/shard_map/ppermute | solution.py:349
  132.9 8.1 %copy-start.17 = (bf16[2,384,1024]{2,1,0:T(8,128)(2,1)S(1)}, bf16[2,384,1024]{2,1,0:T(8,128)(2,1)}, u32[]{:S(2)}) copy-start(bf16[2,384,1024]{2,1,0:T(8,128)(2,1)} %get-tuple-element.67.refs_1_.refs_3_) | copy-start | bytes 4718596
  139.8 27.7 %collective-permute-start.17 = (bf16[928,384]{1,0:T(8,128)(2,1)}, bf16[928,384]{1,0:T(8,128)(2,1)}, u32[]{:S(2)}, u32[]{:S(2)}) collective-permute-start(bf16[928,384]{1,0:T(8,128)(2,1)} %get-tuple-element.75), channel_id=1, source_target_pairs={{0,2},{1,3},{2,0},{3,1},{4,6},{5,7},{6,4},{7,5},{8,10},{9,11},{10,... | collective-permute-start | bytes 2138120 | tf_op jit(solution)/shard_map/ppermute | solution.py:349
  140.1 30.9 %collective-permute-start.21 = (bf16[464,384]{1,0:T(8,128)(2,1)}, bf16[464,384]{1,0:T(8,128)(2,1)}, u32[]{:S(2)}, u32[]{:S(2)}) collective-permute-start(bf16[464,384]{1,0:T(8,128)(2,1)} %get-tuple-element.71.refs_5_), channel_id=1, source_target_pairs={{0,6},{1,7},{2,4},{3,5},{4,2},{5,3},{6,0},{7,1},{8,14},{9,15},{10,... | collective-permute-start | bytes 1069064 | tf_op jit(solution)/shard_map/ppermute | solution.py:349
  141.0 9.1 %collective-permute-start.13 = (bf16[384,1792]{1,0:T(8,128)(2,1)}, bf16[384,1792]{1,0:T(8,128)(2,1)}, u32[]{:S(2)}, u32[]{:S(2)}) collective-permute-start(bf16[384,1792]{1,0:T(8,128)(2,1)} %collective-permute-done.12.refs_5_.refs_1_), channel_id=1, source_target_pairs={{0,8},{8,0},{16,24},{24,16},{1,9},{9,1},{17,25},{25,17},{2,10},{10... | collective-permute-start | bytes 4128776 | tf_op jit(solution)/shard_map/ppermute | solution.py:352
  141.0 1.0 copy-start.18
  158.3 39.6 %collective-permute-start.15 = (bf16[464,384]{1,0:T(8,128)(2,1)}, bf16[464,384]{1,0:T(8,128)(2,1)}, u32[]{:S(2)}, u32[]{:S(2)}) collective-permute-start(bf16[464,384]{1,0:T(8,128)(2,1)} %get-tuple-element.73), channel_id=1, source_target_pairs={{0,5},{1,4},{2,7},{3,6},{4,1},{5,0},{6,3},{7,2},{8,13},{9,12},{10,... | collective-permute-start | bytes 1069064 | tf_op jit(solution)/shard_map/ppermute | solution.py:349
  163.8 34.1 %collective-permute-start.16 = (bf16[464,384]{1,0:T(8,128)(2,1)}, bf16[464,384]{1,0:T(8,128)(2,1)}, u32[]{:S(2)}, u32[]{:S(2)}) collective-permute-start(bf16[464,384]{1,0:T(8,128)(2,1)} %get-tuple-element.74), channel_id=1, source_target_pairs={{0,4},{1,5},{2,6},{3,7},{4,0},{5,1},{6,2},{7,3},{8,12},{9,13},{10,... | collective-permute-start | bytes 1069064 | tf_op jit(solution)/shard_map/ppermute | solution.py:349
  166.5 1.0 copy-start.21
  167.5 1.0 copy-start.23
  168.4 2.6 %copy-start.14 = (bf16[8,16,128]{2,1,0:T(8,128)(2,1)S(1)}, bf16[8,16,128]{2,1,0:T(8,128)(2,1)}, u32[]{:S(2)}) copy-start(bf16[8,16,128]{2,1,0:T(8,128)(2,1)} %copy-done.13) | copy-start | bytes 98308
  168.4 2.6 %copy-start.19 = (s32[128,2]{0,1:T(2,128)S(1)}, s32[128,2]{0,1:T(2,128)}, u32[]{:S(2)}) copy-start(s32[128,2]{0,1:T(2,128)} %param.10) | copy-start | bytes 3076
  168.4 2.6 %copy-start.22 = (bf16[464,384]{1,0:T(8,128)(2,1)S(1)}, bf16[464,384]{1,0:T(8,128)(2,1)}, u32[]{:S(2)}) copy-start(bf16[464,384]{1,0:T(8,128)(2,1)} %get-tuple-element.77.refs_1_.refs_3_) | copy-start | bytes 1069060
  170.5 25.1 %collective-permute-start.20 = (bf16[928,384]{1,0:T(8,128)(2,1)}, bf16[928,384]{1,0:T(8,128)(2,1)}, u32[]{:S(2)}, u32[]{:S(2)}) collective-permute-start(bf16[928,384]{1,0:T(8,128)(2,1)} %second_back.1.refs_7_), channel_id=1, source_target_pairs={{0,1},{1,0},{2,3},{3,2},{4,5},{5,4},{6,7},{7,6},{8,9},{9,8},{10,11... | collective-permute-start | bytes 2138120 | tf_op jit(solution)/shard_map/ppermute | solution.py:349
  171.0 3.8 %collective-permute-start.22 = (bf16[2,384,1024]{2,1,0:T(8,128)(2,1)}, bf16[2,384,1024]{2,1,0:T(8,128)(2,1)}, u32[]{:S(2)}, u32[]{:S(2)}) collective-permute-start(bf16[2,384,1024]{2,1,0:T(8,128)(2,1)} %collective-permute-done.19.refs_0_.refs_3_), channel_id=1, source_target_pairs={{0,8},{8,0},{16,24},{24,16},{1,9},{9,1},{17,25},{25,17},{2,10},{10... | collective-permute-start | bytes 4718600 | tf_op jit(solution)/shard_map/ppermute | solution.py:352
  174.8 20.8 %copy-start.15 = (bf16[8,16,128]{2,1,0:T(8,128)(2,1)S(1)}, bf16[8,16,128]{2,1,0:T(8,128)(2,1)}, u32[]{:S(2)}) copy-start(bf16[8,16,128]{2,1,0:T(8,128)(2,1)} %copy-done.13) | copy-start | bytes 98308
  174.8 20.8 %copy-start.20 = (s32[128,2]{0,1:T(2,128)S(1)}, s32[128,2]{0,1:T(2,128)}, u32[]{:S(2)}) copy-start(s32[128,2]{0,1:T(2,128)} %param.10) | copy-start | bytes 3076
  (3 other events, 1.8 us)

commit v5 on v4

--- a/solution.py
+++ b/solution.py
@@ -117,16 +117,6 @@
     return found + [(ref, 0) for ref in far_refs]
 
 
-def hold_kernel(in_ref, out_ref):
-    out_ref[...] = in_ref[...]
-
-
-def copy_kernel(*refs):
-    count = len(refs) // 2
-    for src, out in zip(refs[:count], refs[count:]):
-        out[...] = src[...]
-
-
 def fence_kernel(out_ref):
     out_ref[...] = jnp.zeros_like(out_ref)
 
@@ -246,7 +236,7 @@
     toks = metas_ref.shape[2]
     metas = [metas_ref[j].astype(F32) for j in range(n)]
     if more:
-        total = refs[-4][...]
+        total = refs[-4][...].astype(F32)
         gg = [refs[-3][0], refs[-3][1]]
     else:
         total = jnp.zeros((feats, n * toks), F32)
@@ -266,7 +256,7 @@
         score = jnp.dot(got, pick[:, 0:toks], preferred_element_type=F32)
         gg = [gg[c] + jnp.where(ids_ref[c : c + 1, :] == (me ^ k), score, 0.0) for c in (0, 1)]
     if not last:
-        out_ref[...] = total
+        out_ref[...] = total.astype(BF16)
         gates_ref[0] = gg[0]
         gates_ref[1] = gg[1]
         return
@@ -356,7 +346,7 @@
 
     previous = []
 
-    def run(body, name, outs, args, in_specs, out_specs, after=(), grid=(), scalars=0, scratch=(), weight=LONG, mib=48):
+    def run(body, name, outs, args, in_specs, out_specs, after=(), grid=(), scalars=0, scratch=(), weight=LONG, mib=48, alias=None):
         waits = [*after, *previous]
         first = len(args)
 
@@ -374,6 +364,7 @@
             ),
             out_shape=outs,
             compiler_params=params(mib),
+            input_output_aliases=alias or {},
             cost_estimate=pl.CostEstimate(flops=weight, bytes_accessed=1, transcendentals=0),
             name=name,
         )(*args, *waits)
@@ -385,6 +376,13 @@
     def call(body, name, outs, args, after=(), scalars=0, **kinds):
         in_specs = [smem()] * scalars + vmem(len(args) - scalars)
         return run(body, name, outs, args, in_specs, vmem(len(outs)), after, **kinds)
+
+    def hold(values, after=(), weight=LONG):
+        outs = [jax.ShapeDtypeStruct(v.shape, v.dtype) for v in values]
+        count = len(values)
+        alias = {i: i for i in range(count)}
+        spaces = [any_space] * count
+        return run(lambda *_: None, "hold", outs, values, spaces, spaces, after, weight=weight, alias=alias)
 
     def fence(after):
         call(fence_kernel, "fence", [shape(8, 128, dtype=F32)], [], after)
@@ -425,15 +423,14 @@
         [shape((nz - 1) * cap, wide)] * (nx - 1) + [shape(cap, wide)] * (1 + nx),
         [x_all, meta_all, x_near, *x_side],
         mib=59,
-        weight=1,
     )
     x_side = [swap(v, xo) for xo, v in enumerate(made[: nx - 1], 1)]
     x_mid, x_passed = made[nx - 1], made[nx:]
     x_far = [swap(v, nx + xo) for xo, v in enumerate(x_passed)]
-    y_z = [swap(y_sent[zk], zk * nx) for zk in range(2, nz)]
+    y_mid = swap(y_sent[2], 2 * nx)
     got_x = [x_own, x_near, x_mid, *x_side, *x_far]
-    y_near = call(hold_kernel, "hold", [shape(nx * cap, d)], [y_sent[1]], x_far, mib=59)[0]
-    y_near = swap(y_near, nx)
+    y_near = swap(y_sent[1], nx)
+    y_far = swap(hold([y_sent[3]], [*x_far, y_mid])[0], 3 * nx)
 
     tile = 256
     steps = h // tile
@@ -445,6 +442,7 @@
         + [shape(rows, d), shape(rows, 128, dtype=F32), shape(n, 2 * n, toks)],
         [my_y, *got_x, meta],
         scalars=1,
+        mib=59,
         weight=1,
     )
     x_own_came = swap_dp(x_parts[0], 1)
@@ -460,8 +458,8 @@
         grid=(steps,),
         weight=1,
     )
-    fence(y_z)
-    got_y = [y_sent[0], y_near, *y_z]
+    fence([y_near])
+    got_y = [y_sent[0], y_near, y_mid, y_far]
     first_sent = list(range(n - nx + 1, n))
     held = lambda i: jnp.minimum(i, steps - 1)
     column_b = pl.BlockSpec((rows, tile), lambda i, _: (0, held(i)))
@@ -527,9 +525,7 @@
         for k, v in zip(ks, values):
             straight[k] = swap(v, k)
 
-    sent = call(
-        copy_kernel, "hold", [shape(size, rows)] * (nx - 1), sent, weight=1, mib=59
-    )
+    sent = hold(sent, weight=1)
     send(first_sent, sent)
     near, sent = rowgrads(
         [(nx + xo, 0, xo * size) for xo in range(nx)] + [(far[0], 1, 0)],
@@ -576,7 +572,7 @@
     )
     columns = [swap(v, xo) for xo, v in enumerate(sent, 1)]
 
-    sum_shapes = [shape(feats, n * toks, dtype=F32), shape(2, 16, toks, dtype=F32)]
+    sum_shapes = [shape(feats, n * toks), shape(2, 16, toks, dtype=F32)]
 
     def combine(parts, refs, carried, outs, final):
         return call(

time: 202 us -> 200 us (0.990)
  Pallas kernels: 82.1 us -> 78.5 us
  starting transfers between devices: 28 us -> 31.3 us
    pallas_call x18, Pallas kernels: 82.1 us -> 78.5 us  [run(): pl.pallas_call(trimmed, grid_spec=pltpu.PrefetchScalarGridSpec(num_scalar...]
    ppermute x17, starting transfers between devices: 24.8 us -> 28.1 us  [swap(): return lax.ppermute(v, 'expert', [(i, i ^ k) for i in range(n)])]
    unnamed x56 -> x50, local copies, waits for them, and re-layouts: 12.2 us -> 10.5 us
  transfers between devices with their start and end apart: 23 -> 23, of which waited for: 9 -> 8; matrix products, arithmetic and copies ran while one was open for 0% -> 0% of each run, Pallas kernels for 37% -> 38%
where the time goes in v5:
time: 200 us; the launch traced here: 199 us
  Pallas kernels  78.5 us (39%)
  waiting for transfers between devices  78.4 us (39%)
  starting transfers between devices  31.3 us (16%)
  local copies, waits for them, and re-layouts  10.5 us (5%)
    pallas_call x18, Pallas kernels, run(): pl.pallas_call(trimmed, grid_spec=pltpu.PrefetchScalarGridSpec(num_scalar...  78.5 us
    ppermute x17, waiting for transfers between devices, swap(): return lax.ppermute(v, 'expert', [(i, i ^ k) for i in range(n)])  75.1 us
    ppermute x17, starting transfers between devices, swap(): return lax.ppermute(v, 'expert', [(i, i ^ k) for i in range(n)])  28.1 us
    unnamed x50, local copies, waits for them, and re-layouts  10.5 us
  transfers between devices with their start and end apart: 23, of which 8 were waited for; matrix products, arithmetic and copies ran while one was open for 0% of the time, Pallas kernels for 38%

profile of v5, /device:TPU:0, one launch (start us, length us, event | category | flops | bytes accessed | tf_op | source)
XLA Modules:
  0.0 199.5 jit_solution(4655873235103304550)
XLA Ops:
  0.6 4.1 %collective-permute-start.1 = (bf16[128,3584]{1,0:T(8,128)(2,1)}, bf16[128,3584]{1,0:T(8,128)(2,1)}, u32[]{:S(2)}, u32[]{:S(2)}) collective-permute-start(bf16[128,3584]{1,0:T(8,128)(2,1)} %refs_3_.4), channel_id=1, source_target_pairs={{0,4},{1,5},{2,6},{3,7},{4,0},{5,1},{6,2},{7,3},{8,12},{9,13},{10,... | collective-permute-start | bytes 2752520 | tf_op jit(solution)/shard_map/ppermute | solution.py:339
  4.7 3.4 %prep.1 = (bf16[16,128]{1,0:T(8,128)(2,1)}, bf16[96,3712]{1,0:T(8,128)(2,1)}, bf16[48,3584]{1,0:T(8,128)(2,1)}, bf16[48,3712]{1,0:T(8,128)(2,1)}, bf16[96,3584]{1,0:T(8,128)(2,1)}, /*index=5*/bf16[96,3584]{1,0:T(8,128)(2,1)}) custom-call(s32[1]{0:T(128)} %bitcast.refs_0_, s32[2,128]{1,0:T(2,128)} %bitcast.7, bf16[2,128]{1,0:T(2,128)(2,1)} %bitcast.11, ...), custom_call_target="tpu_custom_call" | custom-call | flops 1099511627776 | bytes 1 | tf_op jit(solution)/shard_map/prep/pallas_call | solution.py:356
  8.2 1.6 collective-permute-start
  9.8 1.5 collective-permute-start.3
  11.3 0.5 collective-permute-start.4
  12.2 16.2 %collective-permute-done.3.refs_2_ = bf16[96,3584]{1,0:T(8,128)(2,1)S(1)} collective-permute-done((bf16[96,3584]{1,0:T(8,128)(2,1)}, bf16[96,3584]{1,0:T(8,128)(2,1)S(1)}, u32[]{:S(2)}, u32[]{:S(2)}) %collective-permute-start.3) | collective-permute-done | bytes 688160 | tf_op jit(solution)/shard_map/ppermute | solution.py:339
  28.4 13.0 %collective-permute-done.4.refs_3_ = bf16[96,3584]{1,0:T(8,128)(2,1)S(1)} collective-permute-done((bf16[96,3584]{1,0:T(8,128)(2,1)}, bf16[96,3584]{1,0:T(8,128)(2,1)S(1)}, u32[]{:S(2)}, u32[]{:S(2)}) %collective-permute-start.4) | collective-permute-done | bytes 688160 | tf_op jit(solution)/shard_map/ppermute | solution.py:339
  41.4 0.8 copy-done.23
  42.2 3.7 %second.1 = (bf16[96,3584]{1,0:T(8,128)(2,1)}, bf16[96,3584]{1,0:T(8,128)(2,1)}, bf16[96,3584]{1,0:T(8,128)(2,1)}, bf16[96,3584]{1,0:T(8,128)(2,1)}) custom-call(bf16[16,128]{1,0:T(8,128)(2,1)} %get-tuple-element.48.refs_0_.refs_4_.refs_7_, bf16[128,3584]{1,0:T(8,128)(2,1)} %refs_1_.1, bf16[96,3584]{1,0:T(8,128)(2,1)} %copy-done.22, ...), custom_call_target="tpu_custom_call" | custom-call | flops 1 | bytes 1 | tf_op jit(solution)/shard_map/second/pallas_call | solution.py:356
  46.3 0.6 copy-done.24
  47.1 3.4 %third.1 = (bf16[144,3712]{1,0:T(8,128)(2,1)}, bf16[48,3712]{1,0:T(8,128)(2,1)}, bf16[48,3712]{1,0:T(8,128)(2,1)}, bf16[48,3712]{1,0:T(8,128)(2,1)}) custom-call(bf16[128,3584]{1,0:T(8,128)(2,1)} %collective-permute-done.1.refs_0_, bf16[16,128]{1,0:T(8,128)(2,1)} %copy-done.24, bf16[96,3712]{1,0:T(8,128)(2,1)} %copy-done.21, ...), custom_call_target="tpu_custom_call" | custom-call | flops 1099511627776 | bytes 1 | tf_op jit(solution)/shard_map/third/pallas_call | solution.py:356
  51.0 2.5 %collective-permute-start.7 = (bf16[48,3712]{1,0:T(8,128)(2,1)}, bf16[48,3712]{1,0:T(8,128)(2,1)S(1)}, u32[]{:S(2)}, u32[]{:S(2)}) collective-permute-start(bf16[48,3712]{1,0:T(8,128)(2,1)} %get-tuple-element.56), channel_id=1, source_target_pairs={{0,3},{1,2},{2,1},{3,0},{4,7},{5,6},{6,5},{7,4},{8,11},{9,10},{10,... | collective-permute-start | bytes 1069064 | tf_op jit(solution)/shard_map/ppermute | solution.py:339
  53.9 0.5 collective-permute-start.5
  54.5 15.7 %collective-permute-done.6.refs_1_.refs_5_ = bf16[48,3712]{1,0:T(8,128)(2,1)S(1)} collective-permute-done((bf16[48,3712]{1,0:T(8,128)(2,1)}, bf16[48,3712]{1,0:T(8,128)(2,1)S(1)}, u32[]{:S(2)}, u32[]{:S(2)}) %collective-permute-start.6) | collective-permute-done | bytes 356384 | tf_op jit(solution)/shard_map/ppermute | solution.py:339
  70.1 15.1 %collective-permute-done.7.refs_2_.refs_6_ = bf16[48,3712]{1,0:T(8,128)(2,1)S(1)} collective-permute-done((bf16[48,3712]{1,0:T(8,128)(2,1)}, bf16[48,3712]{1,0:T(8,128)(2,1)S(1)}, u32[]{:S(2)}, u32[]{:S(2)}) %collective-permute-start.7) | collective-permute-done | bytes 356384 | tf_op jit(solution)/shard_map/ppermute | solution.py:339
  85.3 1.1 copy-done.3
  86.4 1.8 collective-permute-start.10
  88.2 4.6 %gather.1 = (bf16[384,1792]{1,0:T(8,128)(2,1)}, bf16[384,1792]{1,0:T(8,128)(2,1)}, bf16[384,3584]{1,0:T(8,128)(2,1)}, f32[384,128]{1,0:T(8,128)}, bf16[8,16,128]{2,1,0:T(8,128)(2,1)}) custom-call(s32[1]{0:T(128)} %bitcast.2.refs_0_, bf16[48,3584]{1,0:T(8,128)(2,1)} %get-tuple-element.46.refs_1_, bf16[96,3712]{1,0:T(8,128)(2,1)} %copy-done.21, ...), custom_call_target="tpu_custom_call" | custom-call | flops 1 | bytes 1 | tf_op jit(solution)/shard_map/gather/pallas_call | solution.py:356
  92.8 1.6 collective-permute-start.12
  94.4 0.9 copy-done.6
  95.3 0.8 copy-done.7
  96.1 10.3 %forward.1 = (bf16[384,1024]{1,0:T(8,128)(2,1)S(1)}, f32[384,1024]{1,0:T(8,128)S(1)}, f32[384,1024]{1,0:T(8,128)S(1)}) custom-call(bf16[384,3584]{1,0:T(8,128)(2,1)} %get-tuple-element.61.refs_0_, f32[384,128]{1,0:T(8,128)S(1)} %copy-done.6, bf16[1,3584,1024]{2,1,0:T(8,128)(2,1)} %refs_3_.7, bf16[1,3584,1024]{2,1,0:T(8,128)(2,1)} %refs_4_.5, ...), custom_call_target="tpu_custom_call" | custom-call | flops 1 | bytes 1 | tf_op jit(solution)/shard_map/forward/pallas_call | solution.py:356
  106.4 1.1 copy-done
  107.6 3.6 %collective-permute-done.9.refs_0_.refs_2_ = bf16[96,3584]{1,0:T(8,128)(2,1)} collective-permute-done((bf16[96,3584]{1,0:T(8,128)(2,1)}, bf16[96,3584]{1,0:T(8,128)(2,1)}, u32[]{:S(2)}, u32[]{:S(2)}) %collective-permute-start.9) | collective-permute-done | bytes 688160 | tf_op jit(solution)/shard_map/ppermute | solution.py:339
  111.2 0.6 copy-done.11
  111.7 11.3 %back.1 = (bf16[2,384,1024]{2,1,0:T(8,128)(2,1)}, bf16[16,384]{1,0:T(8,128)(2,1)}, bf16[464,384]{1,0:T(8,128)(2,1)}) custom-call(s32[1]{0:T(128)} %bitcast.refs_0_, bf16[96,3584]{1,0:T(8,128)(2,1)} %get-tuple-element.52.refs_4_.refs_1_, bf16[96,3584]{1,0:T(8,128)(2,1)} %collective-permute-done.9.refs_0_.refs_2_, ...), custom_call_target="tpu_custom_call" | custom-call | flops 1 | bytes 1 | tf_op jit(solution)/shard_map/back/pallas_call | solution.py:356
  123.1 1.5 collective-permute-start.19
  124.6 0.7 copy-done.10
  125.3 4.7 %collective-permute-start.18 = (bf16[464,384]{1,0:T(8,128)(2,1)}, bf16[464,384]{1,0:T(8,128)(2,1)}, u32[]{:S(2)}, u32[]{:S(2)}) collective-permute-start(bf16[464,384]{1,0:T(8,128)(2,1)} %hold.3.refs_6_), channel_id=1, source_target_pairs={{0,7},{1,6},{2,5},{3,4},{4,3},{5,2},{6,1},{7,0},{8,15},{9,14},{10,... | collective-permute-start | bytes 1069064 | tf_op jit(solution)/shard_map/ppermute | solution.py:339
  130.0 6.9 %rowgrad.2 = (bf16[928,384]{1,0:T(8,128)(2,1)}, bf16[464,384]{1,0:T(8,128)(2,1)}) custom-call(s32[1]{0:T(128)} %bitcast.refs_0_, bf16[2,384,1024]{2,1,0:T(8,128)(2,1)} %get-tuple-element.67.refs_1_.refs_3_, bf16[16,384]{1,0:T(8,128)(2,1)} %get-tuple-element.68.refs_1_.refs_2_, bf16[1,3584,1024]{2,1,0:T(8,128)(2,1)} %refs_3_.7, ...), custom_call_target="tpu_custom_call" | custom-call | flops 1099511627776 | bytes 1 | tf_op jit(solution)/shard_map/rowgrad/pallas_call | solution.py:356
  136.9 1.2 collective-permute-start.17
  138.1 1.2 collective-permute-start.21
  139.4 1.0 copy-done.14
  140.4 7.0 %weights.1 = (bf16[2,896,1024]{2,1,0:T(8,128)(2,1)}, f32[8,128]{1,0:T(8,128)S(1)}) custom-call(s32[1]{0:T(128)} %bitcast.4.refs_0_, bf16[384,1792]{1,0:T(8,128)(2,1)S(1)} %copy-done.13, bf16[384,1792]{1,0:T(8,128)(2,1)} %collective-permute-done.11.refs_11_.refs_2_, bf16[2,384,1024]{2,1,0:T(8,128)(2,1)S(1)} %copy-done.12, ...), custom_call_target="tpu_custom_call" | custom-call | flops 1099511627776 | bytes 1 | tf_op jit(solution)/shard_map/weights/pallas_call | solution.py:356
  147.4 0.6 copy-done.20
  148.0 8.2 %rowgrad.3 = (bf16[464,384]{1,0:T(8,128)(2,1)}, bf16[464,384]{1,0:T(8,128)(2,1)}, bf16[464,384]{1,0:T(8,128)(2,1)}, bf16[464,384]{1,0:T(8,128)(2,1)}) custom-call(s32[1]{0:T(128)} %bitcast.refs_0_, bf16[2,384,1024]{2,1,0:T(8,128)(2,1)} %get-tuple-element.67.refs_1_.refs_3_, bf16[16,384]{1,0:T(8,128)(2,1)} %get-tuple-element.68.refs_1_.refs_2_, ...), custom_call_target="tpu_custom_call" | custom-call | flops 1099511627776 | bytes 1 | tf_op jit(solution)/shard_map/rowgrad/pallas_call | solution.py:356
  156.2 1.0 collective-permute-start.15
  157.2 3.0 %collective-permute-done.19.refs_0_.refs_3_ = bf16[2,384,1024]{2,1,0:T(8,128)(2,1)} collective-permute-done((bf16[2,384,1024]{2,1,0:T(8,128)(2,1)}, bf16[2,384,1024]{2,1,0:T(8,128)(2,1)}, u32[]{:S(2)}, u32[]{:S(2)}) %collective-permute-start.19) | collective-permute-done | bytes 1572896 | tf_op jit(solution)/shard_map/ppermute | solution.py:342
  160.2 4.4 %collective-permute-start.16 = (bf16[464,384]{1,0:T(8,128)(2,1)}, bf16[464,384]{1,0:T(8,128)(2,1)}, u32[]{:S(2)}, u32[]{:S(2)}) collective-permute-start(bf16[464,384]{1,0:T(8,128)(2,1)} %get-tuple-element.74), channel_id=1, source_target_pairs={{0,4},{1,5},{2,6},{3,7},{4,0},{5,1},{6,2},{7,3},{8,12},{9,13},{10,... | collective-permute-start | bytes 1069064 | tf_op jit(solution)/shard_map/ppermute | solution.py:339
  164.6 1.0 copy-done.17
  165.6 1.0 copy-done.19
  166.6 2.1 %second_back.1.refs_7_ = bf16[928,384]{1,0:T(8,128)(2,1)} custom-call(bf16[928,384]{1,0:T(8,128)(2,1)} %collective-permute-done.17.refs_0_.refs_4_, bf16[464,384]{1,0:T(8,128)(2,1)S(1)} %copy-done.19, bf16[464,384]{1,0:T(8,128)(2,1)} %collective-permute-done.18.refs_2_.refs_6_, f32[8,128]{1,0:T(8,128)S(1)} %fence.3.refs_3_), custom_call_target="tpu_custom_call" | custom-call | flops 1099511627776 | bytes 1 | tf_op jit(solution)/shard_map/second_back/pallas_call | solution.py:356
  168.6 1.5 collective-permute-start.20
  170.1 3.5 %combine.3 = (bf16[448,1024]{1,0:T(8,128)(2,1)S(1)}, f32[2,16,128]{2,1,0:T(8,128)S(1)}) custom-call(s32[1]{0:T(128)} %bitcast.refs_0_, s32[2,128]{1,0:T(2,128)S(1)} %bitcast.8, bf16[8,16,128]{2,1,0:T(8,128)(2,1)S(1)} %copy-done.8, bf16[464,384]{1,0:T(8,128)(2,1)S(1)} %copy-done.18, bf16[928,384]{1,0:T(8,128)(2,1)} %collective-permute-done.17.refs_0_.refs_4_, ...), custom_call_target="tpu_custom_call" | custom-call | flops 1099511627776 | bytes 1 | tf_op jit(solution)/shard_map/combine/pallas_call | solution.py:356
  173.9 8.4 %weights_rest.1 = (bf16[1,896,1024]{2,1,0:T(8,128)(2,1)}, bf16[1,896,1024]{2,1,0:T(8,128)(2,1)}, f32[8,128]{1,0:T(8,128)S(1)}) custom-call(s32[1]{0:T(128)} %bitcast.4.refs_0_, bf16[384,1792]{1,0:T(8,128)(2,1)} %collective-permute-done.12.refs_5_.refs_1_, bf16[384,1792]{1,0:T(8,128)(2,1)} %collective-permute-done.13.refs_5_.refs_2_, ...), custom_call_target="tpu_custom_call" | custom-call | flops 1099511627776 | bytes 1 | tf_op jit(solution)/shard_map/weights_rest/pallas_call | solution.py:356
  182.2 11.5 %collective-permute-done.20.refs_3_ = bf16[928,384]{1,0:T(8,128)(2,1)} collective-permute-done((bf16[928,384]{1,0:T(8,128)(2,1)}, bf16[928,384]{1,0:T(8,128)(2,1)}, u32[]{:S(2)}, u32[]{:S(2)}) %collective-permute-start.20) | collective-permute-done | bytes 712736 | tf_op jit(solution)/shard_map/ppermute | solution.py:339
  193.7 2.3 %combine.4 = (bf16[448,1024]{1,0:T(8,128)(2,1)S(1)}, f32[2,16,128]{2,1,0:T(8,128)S(1)}) custom-call(s32[1]{0:T(128)} %bitcast.refs_0_, s32[2,128]{1,0:T(2,128)S(1)} %bitcast.9, bf16[8,16,128]{2,1,0:T(8,128)(2,1)S(1)} %copy-done.9, bf16[928,384]{1,0:T(8,128)(2,1)} %collective-permute-done.20.refs_3_, bf16[448,1024]{1,0:T(8,128)(2,1)S(1)} %get-tuple-element.78.refs_4_, ...), custom_call_target="tpu_custom_call" | custom-call | flops 1099511627776 | bytes 1 | tf_op jit(solution)/shard_map/combine/pallas_call | solution.py:356
  196.1 3.4 %combine.5 = (bf16[448,1024]{1,0:T(8,128)(2,1)}, bf16[2,128]{1,0:T(2,128)(2,1)}) custom-call(s32[1]{0:T(128)} %bitcast.refs_0_, s32[2,128]{1,0:T(2,128)S(1)} %bitcast.10, bf16[8,16,128]{2,1,0:T(8,128)(2,1)S(1)} %copy-done.9, bf16[464,384]{1,0:T(8,128)(2,1)} %collective-permute-done.15.refs_3_, bf16[464,384]{1,0:T(8,128)(2,1)} %collective-permute-done.16.refs_4_, ...), custom_call_target="tpu_custom_call" | custom-call | flops 1099511627776 | bytes 1 | tf_op jit(solution)/shard_map/combine/pallas_call | solution.py:356
  (66 shorter events, 2.2 us)
Async XLA Ops:
  0.6 45.7 %collective-permute-start.1 = (bf16[128,3584]{1,0:T(8,128)(2,1)}, bf16[128,3584]{1,0:T(8,128)(2,1)}, u32[]{:S(2)}, u32[]{:S(2)}) collective-permute-start(bf16[128,3584]{1,0:T(8,128)(2,1)} %refs_3_.4), channel_id=1, source_target_pairs={{0,4},{1,5},{2,6},{3,7},{4,0},{5,1},{6,2},{7,3},{8,12},{9,13},{10,... | collective-permute-start | bytes 2752520 | tf_op jit(solution)/shard_map/ppermute | solution.py:339
  8.2 38.1 %collective-permute-start = (bf16[96,3712]{1,0:T(8,128)(2,1)}, bf16[96,3712]{1,0:T(8,128)(2,1)S(1)}, u32[]{:S(2)}, u32[]{:S(2)}) collective-permute-start(bf16[96,3712]{1,0:T(8,128)(2,1)} %get-tuple-element.47), channel_id=1, source_target_pairs={{0,2},{1,3},{2,0},{3,1},{4,6},{5,7},{6,4},{7,5},{8,10},{9,11},{10,... | collective-permute-start | bytes 2138120 | tf_op jit(solution)/shard_map/ppermute | solution.py:339
  9.8 18.6 %collective-permute-start.3 = (bf16[96,3584]{1,0:T(8,128)(2,1)}, bf16[96,3584]{1,0:T(8,128)(2,1)S(1)}, u32[]{:S(2)}, u32[]{:S(2)}) collective-permute-start(bf16[96,3584]{1,0:T(8,128)(2,1)} %get-tuple-element.50), channel_id=1, source_target_pairs={{0,1},{1,0},{2,3},{3,2},{4,5},{5,4},{6,7},{7,6},{8,9},{9,8},{10,11... | collective-permute-start | bytes 2064392 | tf_op jit(solution)/shard_map/ppermute | solution.py:339
  11.3 30.1 %collective-permute-start.4 = (bf16[96,3584]{1,0:T(8,128)(2,1)}, bf16[96,3584]{1,0:T(8,128)(2,1)S(1)}, u32[]{:S(2)}, u32[]{:S(2)}) collective-permute-start(bf16[96,3584]{1,0:T(8,128)(2,1)} %get-tuple-element.51), channel_id=1, source_target_pairs={{0,1},{1,0},{2,3},{3,2},{4,5},{5,4},{6,7},{7,6},{8,9},{9,8},{10,11... | collective-permute-start | bytes 2064392 | tf_op jit(solution)/shard_map/ppermute | solution.py:339
  11.8 34.4 %collective-permute-start.2 = (bf16[16,128]{1,0:T(8,128)(2,1)}, bf16[16,128]{1,0:T(8,128)(2,1)S(1)}, u32[]{:S(2)}, u32[]{:S(2)}) collective-permute-start(bf16[16,128]{1,0:T(8,128)(2,1)} %get-tuple-element.48.refs_0_.refs_4_.refs_7_), channel_id=1, source_target_pairs={{0,4},{1,5},{2,6},{3,7},{4,0},{5,1},{6,2},{7,3},{8,12},{9,13},{10,... | collective-permute-start | bytes 12296 | tf_op jit(solution)/shard_map/ppermute | solution.py:339
  28.4 13.0 %copy-start.22 = (bf16[96,3584]{1,0:T(8,128)(2,1)}, bf16[96,3584]{1,0:T(8,128)(2,1)S(1)}, u32[]{:S(2)}) copy-start(bf16[96,3584]{1,0:T(8,128)(2,1)S(1)} %collective-permute-done.3.refs_2_) | copy-start | bytes 2064388
  41.4 0.8 copy-start.23
  45.9 39.3 %collective-permute-start.8 = (bf16[96,3584]{1,0:T(8,128)(2,1)}, bf16[96,3584]{1,0:T(8,128)(2,1)}, u32[]{:S(2)}, u32[]{:S(2)}) collective-permute-start(bf16[96,3584]{1,0:T(8,128)(2,1)} %get-tuple-element.58), channel_id=1, source_target_pairs={{0,4},{1,5},{2,6},{3,7},{4,0},{5,1},{6,2},{7,3},{8,12},{9,13},{10,... | collective-permute-start | bytes 2064392 | tf_op jit(solution)/shard_map/ppermute | solution.py:339
  46.3 0.6 copy-start.24
  46.3 0.9 copy-start.21
  50.5 19.6 %collective-permute-start.6 = (bf16[48,3712]{1,0:T(8,128)(2,1)}, bf16[48,3712]{1,0:T(8,128)(2,1)S(1)}, u32[]{:S(2)}, u32[]{:S(2)}) collective-permute-start(bf16[48,3712]{1,0:T(8,128)(2,1)} %get-tuple-element.55), channel_id=1, source_target_pairs={{0,2},{1,3},{2,0},{3,1},{4,6},{5,7},{6,4},{7,5},{8,10},{9,11},{10,... | collective-permute-start | bytes 1069064 | tf_op jit(solution)/shard_map/ppermute | solution.py:339
  51.0 34.3 %collective-permute-start.7 = (bf16[48,3712]{1,0:T(8,128)(2,1)}, bf16[48,3712]{1,0:T(8,128)(2,1)S(1)}, u32[]{:S(2)}, u32[]{:S(2)}) collective-permute-start(bf16[48,3712]{1,0:T(8,128)(2,1)} %get-tuple-element.56), channel_id=1, source_target_pairs={{0,3},{1,2},{2,1},{3,0},{4,7},{5,6},{6,5},{7,4},{8,11},{9,10},{10,... | collective-permute-start | bytes 1069064 | tf_op jit(solution)/shard_map/ppermute | solution.py:339
  53.5 57.6 %collective-permute-start.9 = (bf16[96,3584]{1,0:T(8,128)(2,1)}, bf16[96,3584]{1,0:T(8,128)(2,1)}, u32[]{:S(2)}, u32[]{:S(2)}) collective-permute-start(bf16[96,3584]{1,0:T(8,128)(2,1)} %get-tuple-element.60), channel_id=1, source_target_pairs={{0,2},{1,3},{2,0},{3,1},{4,6},{5,7},{6,4},{7,5},{8,10},{9,11},{10,... | collective-permute-start | bytes 2064392 | tf_op jit(solution)/shard_map/ppermute | solution.py:339
  53.9 34.3 %collective-permute-start.5 = (bf16[144,3712]{1,0:T(8,128)(2,1)}, bf16[144,3712]{1,0:T(8,128)(2,1)}, u32[]{:S(2)}, u32[]{:S(2)}) collective-permute-start(bf16[144,3712]{1,0:T(8,128)(2,1)} %get-tuple-element.54), channel_id=1, source_target_pairs={{0,1},{1,0},{2,3},{3,2},{4,5},{5,4},{6,7},{7,6},{8,9},{9,8},{10,11... | collective-permute-start | bytes 3207176 | tf_op jit(solution)/shard_map/ppermute | solution.py:339
  70.1 16.3 %copy-start.4 = (bf16[48,3712]{1,0:T(8,128)(2,1)}, bf16[48,3712]{1,0:T(8,128)(2,1)S(1)}, u32[]{:S(2)}) copy-start(bf16[48,3712]{1,0:T(8,128)(2,1)S(1)} %collective-permute-done.6.refs_1_.refs_5_) | copy-start | bytes 1069060
  85.3 1.1 copy-start.5
  85.3 1.1 copy-start.3
  86.4 25.3 %collective-permute-start.10 = (bf16[96,3584]{1,0:T(8,128)(2,1)}, bf16[96,3584]{1,0:T(8,128)(2,1)}, u32[]{:S(2)}, u32[]{:S(2)}) collective-permute-start(bf16[96,3584]{1,0:T(8,128)(2,1)} %hold.2.refs_8_), channel_id=1, source_target_pairs={{0,6},{1,7},{2,4},{3,5},{4,2},{5,3},{6,0},{7,1},{8,14},{9,15},{10,... | collective-permute-start | bytes 2064392 | tf_op jit(solution)/shard_map/ppermute | solution.py:339
  92.8 18.9 %collective-permute-start.11 = (bf16[384,1792]{1,0:T(8,128)(2,1)}, bf16[384,1792]{1,0:T(8,128)(2,1)}, u32[]{:S(2)}, u32[]{:S(2)}) collective-permute-start(bf16[384,1792]{1,0:T(8,128)(2,1)} %get-tuple-element.66.refs_1_), channel_id=1, source_target_pairs={{0,8},{8,0},{16,24},{24,16},{1,9},{9,1},{17,25},{25,17},{2,10},{10... | collective-permute-start | bytes 4128776 | tf_op jit(solution)/shard_map/ppermute | solution.py:342
  92.8 37.2 %collective-permute-start.12 = (bf16[384,1792]{1,0:T(8,128)(2,1)}, bf16[384,1792]{1,0:T(8,128)(2,1)}, u32[]{:S(2)}, u32[]{:S(2)}) collective-permute-start(bf16[384,1792]{1,0:T(8,128)(2,1)} %get-tuple-element.69), channel_id=1, source_target_pairs={{0,16},{8,24},{16,0},{24,8},{1,17},{9,25},{17,1},{25,9},{2,18},{10... | collective-permute-start | bytes 4128776 | tf_op jit(solution)/shard_map/ppermute | solution.py:342
  94.4 0.9 copy-start.6
  95.3 0.8 copy-start.7
  106.4 1.1 copy-start
  107.6 3.6 %copy-start.1 = (f32[384,1024]{1,0:T(8,128)}, f32[384,1024]{1,0:T(8,128)S(1)}, u32[]{:S(2)}) copy-start(f32[384,1024]{1,0:T(8,128)S(1)} %get-tuple-element.65.refs_7_) | copy-start | bytes 4718596
  107.6 3.6 %copy-start.2 = (bf16[384,1024]{1,0:T(8,128)(2,1)}, bf16[384,1024]{1,0:T(8,128)(2,1)S(1)}, u32[]{:S(2)}) copy-start(bf16[384,1024]{1,0:T(8,128)(2,1)S(1)} %get-tuple-element.63.refs_1_.refs_5_) | copy-start | bytes 2359300
  111.2 0.6 copy-start.11
  123.0 16.3 %collective-permute-start.14 = (bf16[2,384,1024]{2,1,0:T(8,128)(2,1)}, bf16[2,384,1024]{2,1,0:T(8,128)(2,1)}, u32[]{:S(2)}, u32[]{:S(2)}) collective-permute-start(bf16[2,384,1024]{2,1,0:T(8,128)(2,1)} %get-tuple-element.67.refs_1_.refs_3_), channel_id=1, source_target_pairs={{0,8},{8,0},{16,24},{24,16},{1,9},{9,1},{17,25},{25,17},{2,10},{10... | collective-permute-start | bytes 4718600 | tf_op jit(solution)/shard_map/ppermute | solution.py:342
  123.1 37.1 %collective-permute-start.19 = (bf16[2,384,1024]{2,1,0:T(8,128)(2,1)}, bf16[2,384,1024]{2,1,0:T(8,128)(2,1)}, u32[]{:S(2)}, u32[]{:S(2)}) collective-permute-start(bf16[2,384,1024]{2,1,0:T(8,128)(2,1)} %get-tuple-element.67.refs_1_.refs_3_), channel_id=1, source_target_pairs={{0,16},{8,24},{16,0},{24,8},{1,17},{9,25},{17,1},{25,9},{2,18},{10... | collective-permute-start | bytes 4718600 | tf_op jit(solution)/shard_map/ppermute | solution.py:342
  124.6 0.7 copy-start.10
  125.3 40.3 %collective-permute-start.18 = (bf16[464,384]{1,0:T(8,128)(2,1)}, bf16[464,384]{1,0:T(8,128)(2,1)}, u32[]{:S(2)}, u32[]{:S(2)}) collective-permute-start(bf16[464,384]{1,0:T(8,128)(2,1)} %hold.3.refs_6_), channel_id=1, source_target_pairs={{0,7},{1,6},{2,5},{3,4},{4,3},{5,2},{6,1},{7,0},{8,15},{9,14},{10,... | collective-permute-start | bytes 1069064 | tf_op jit(solution)/shard_map/ppermute | solution.py:339
  130.0 9.3 %copy-start.12 = (bf16[2,384,1024]{2,1,0:T(8,128)(2,1)S(1)}, bf16[2,384,1024]{2,1,0:T(8,128)(2,1)}, u32[]{:S(2)}) copy-start(bf16[2,384,1024]{2,1,0:T(8,128)(2,1)} %get-tuple-element.67.refs_1_.refs_3_) | copy-start | bytes 4718596
  130.0 9.3 %copy-start.13 = (bf16[384,1792]{1,0:T(8,128)(2,1)S(1)}, bf16[384,1792]{1,0:T(8,128)(2,1)}, u32[]{:S(2)}) copy-start(bf16[384,1792]{1,0:T(8,128)(2,1)} %get-tuple-element.66.refs_1_) | copy-start | bytes 4128772
  136.9 28.7 %collective-permute-start.17 = (bf16[928,384]{1,0:T(8,128)(2,1)}, bf16[928,384]{1,0:T(8,128)(2,1)}, u32[]{:S(2)}, u32[]{:S(2)}) collective-permute-start(bf16[928,384]{1,0:T(8,128)(2,1)} %get-tuple-element.75), channel_id=1, source_target_pairs={{0,2},{1,3},{2,0},{3,1},{4,6},{5,7},{6,4},{7,5},{8,10},{9,11},{10,... | collective-permute-start | bytes 2138120 | tf_op jit(solution)/shard_map/ppermute | solution.py:339
  138.1 32.0 %collective-permute-start.21 = (bf16[464,384]{1,0:T(8,128)(2,1)}, bf16[464,384]{1,0:T(8,128)(2,1)}, u32[]{:S(2)}, u32[]{:S(2)}) collective-permute-start(bf16[464,384]{1,0:T(8,128)(2,1)} %get-tuple-element.71.refs_5_), channel_id=1, source_target_pairs={{0,6},{1,7},{2,4},{3,5},{4,2},{5,3},{6,0},{7,1},{8,14},{9,15},{10,... | collective-permute-start | bytes 1069064 | tf_op jit(solution)/shard_map/ppermute | solution.py:339
  139.3 8.6 %collective-permute-start.13 = (bf16[384,1792]{1,0:T(8,128)(2,1)}, bf16[384,1792]{1,0:T(8,128)(2,1)}, u32[]{:S(2)}, u32[]{:S(2)}) collective-permute-start(bf16[384,1792]{1,0:T(8,128)(2,1)} %collective-permute-done.12.refs_5_.refs_1_), channel_id=1, source_target_pairs={{0,8},{8,0},{16,24},{24,16},{1,9},{9,1},{17,25},{25,17},{2,10},{10... | collective-permute-start | bytes 4128776 | tf_op jit(solution)/shard_map/ppermute | solution.py:342
  139.4 1.0 copy-start.14
  147.4 0.6 copy-start.20
  156.2 39.9 %collective-permute-start.15 = (bf16[464,384]{1,0:T(8,128)(2,1)}, bf16[464,384]{1,0:T(8,128)(2,1)}, u32[]{:S(2)}, u32[]{:S(2)}) collective-permute-start(bf16[464,384]{1,0:T(8,128)(2,1)} %get-tuple-element.73), channel_id=1, source_target_pairs={{0,5},{1,4},{2,7},{3,6},{4,1},{5,0},{6,3},{7,2},{8,13},{9,12},{10,... | collective-permute-start | bytes 1069064 | tf_op jit(solution)/shard_map/ppermute | solution.py:339
  160.2 35.8 %collective-permute-start.16 = (bf16[464,384]{1,0:T(8,128)(2,1)}, bf16[464,384]{1,0:T(8,128)(2,1)}, u32[]{:S(2)}, u32[]{:S(2)}) collective-permute-start(bf16[464,384]{1,0:T(8,128)(2,1)} %get-tuple-element.74), channel_id=1, source_target_pairs={{0,4},{1,5},{2,6},{3,7},{4,0},{5,1},{6,2},{7,3},{8,12},{9,13},{10,... | collective-permute-start | bytes 1069064 | tf_op jit(solution)/shard_map/ppermute | solution.py:339
  164.6 1.0 copy-start.17
  165.6 1.0 copy-start.19
  166.6 3.5 %copy-start.8 = (bf16[8,16,128]{2,1,0:T(8,128)(2,1)S(1)}, bf16[8,16,128]{2,1,0:T(8,128)(2,1)}, u32[]{:S(2)}) copy-start(bf16[8,16,128]{2,1,0:T(8,128)(2,1)} %get-tuple-element.59.refs_4_.refs_2_) | copy-start | bytes 98308
  166.6 3.6 %copy-start.15 = (s32[128,2]{0,1:T(2,128)S(1)}, s32[128,2]{0,1:T(2,128)}, u32[]{:S(2)}) copy-start(s32[128,2]{0,1:T(2,128)} %param.10) | copy-start | bytes 3076
  166.6 3.6 %copy-start.18 = (bf16[464,384]{1,0:T(8,128)(2,1)S(1)}, bf16[464,384]{1,0:T(8,128)(2,1)}, u32[]{:S(2)}) copy-start(bf16[464,384]{1,0:T(8,128)(2,1)} %get-tuple-element.77.refs_1_.refs_3_) | copy-start | bytes 1069060
  168.6 25.1 %collective-permute-start.20 = (bf16[928,384]{1,0:T(8,128)(2,1)}, bf16[928,384]{1,0:T(8,128)(2,1)}, u32[]{:S(2)}, u32[]{:S(2)}) collective-permute-start(bf16[928,384]{1,0:T(8,128)(2,1)} %second_back.1.refs_7_), channel_id=1, source_target_pairs={{0,1},{1,0},{2,3},{3,2},{4,5},{5,4},{6,7},{7,6},{8,9},{9,8},{10,11... | collective-permute-start | bytes 2138120 | tf_op jit(solution)/shard_map/ppermute | solution.py:339
  170.1 3.8 %collective-permute-start.22 = (bf16[2,384,1024]{2,1,0:T(8,128)(2,1)}, bf16[2,384,1024]{2,1,0:T(8,128)(2,1)}, u32[]{:S(2)}, u32[]{:S(2)}) collective-permute-start(bf16[2,384,1024]{2,1,0:T(8,128)(2,1)} %collective-permute-done.19.refs_0_.refs_3_), channel_id=1, source_target_pairs={{0,8},{8,0},{16,24},{24,16},{1,9},{9,1},{17,25},{25,17},{2,10},{10... | collective-permute-start | bytes 4718600 | tf_op jit(solution)/shard_map/ppermute | solution.py:342
  173.9 19.9 %copy-start.9 = (bf16[8,16,128]{2,1,0:T(8,128)(2,1)S(1)}, bf16[8,16,128]{2,1,0:T(8,128)(2,1)}, u32[]{:S(2)}) copy-start(bf16[8,16,128]{2,1,0:T(8,128)(2,1)} %get-tuple-element.59.refs_4_.refs_2_) | copy-start | bytes 98308
  173.9 19.9 %copy-start.16 = (s32[128,2]{0,1:T(2,128)S(1)}, s32[128,2]{0,1:T(2,128)}, u32[]{:S(2)}) copy-start(s32[128,2]{0,1:T(2,128)} %param.10) | copy-start | bytes 3076

commit v6 on v5

--- a/solution.py
+++ b/solution.py
@@ -554,7 +554,7 @@
     own, *sent = rowgrads(
         [(k, i, 0) for i, k in enumerate([0, *range(1, nx), *last])],
         [1] * (nx + len(last)),
-        x_came,
+        [*x_came, *[straight[k] for k in first_sent]],
         weight=LONG,
     )
     by_column, sent = sent[: nx - 1], sent[nx - 1 :]
@@ -568,7 +568,6 @@
         "second_back",
         [shape(2 * size, rows)] * (nx - 1),
         [near, *by_column],
-        [straight[k] for k in far[1:]],
     )
     columns = [swap(v, xo) for xo, v in enumerate(sent, 1)]
 

time: 200 us -> 198 us (0.990)
  starting transfers between devices: 31.3 us -> 28.7 us
    ppermute x17, starting transfers between devices: 28.1 us -> 25.6 us  [swap(): return lax.ppermute(v, 'expert', [(i, i ^ k) for i in range(n)])]
  transfers between devices with their start and end apart: 23 -> 23, of which waited for: 8 -> 9; matrix products, arithmetic and copies ran while one was open for 0% -> 0% of each run, Pallas kernels for 38% -> 38%
where the time goes in v6:
time: 198 us; the launch traced here: 197 us
  Pallas kernels  78.5 us (40%)
  waiting for transfers between devices  78.5 us (40%)
  starting transfers between devices  28.7 us (14%)
  local copies, waits for them, and re-layouts  10.5 us (5%)
    pallas_call x18, Pallas kernels, run(): pl.pallas_call(trimmed, grid_spec=pltpu.PrefetchScalarGridSpec(num_scalar...  78.5 us
    ppermute x17, waiting for transfers between devices, swap(): return lax.ppermute(v, 'expert', [(i, i ^ k) for i in range(n)])  77.1 us
    ppermute x17, starting transfers between devices, swap(): return lax.ppermute(v, 'expert', [(i, i ^ k) for i in range(n)])  25.6 us
    unnamed x50, local copies, waits for them, and re-layouts  10.5 us
  transfers between devices with their start and end apart: 23, of which 9 were waited for; matrix products, arithmetic and copies ran while one was open for 0% of the time, Pallas kernels for 38%

profile of v6, /device:TPU:0, one launch (start us, length us, event | category | flops | bytes accessed | tf_op | source)
XLA Modules:
  0.0 197.0 jit_solution(2375435979857206940)
XLA Ops:
  0.6 4.1 %collective-permute-start.1 = (bf16[128,3584]{1,0:T(8,128)(2,1)}, bf16[128,3584]{1,0:T(8,128)(2,1)}, u32[]{:S(2)}, u32[]{:S(2)}) collective-permute-start(bf16[128,3584]{1,0:T(8,128)(2,1)} %refs_3_.4), channel_id=1, source_target_pairs={{0,4},{1,5},{2,6},{3,7},{4,0},{5,1},{6,2},{7,3},{8,12},{9,13},{10,... | collective-permute-start | bytes 2752520 | tf_op jit(solution)/shard_map/ppermute | solution.py:339
  4.7 3.4 %prep.1 = (bf16[16,128]{1,0:T(8,128)(2,1)}, bf16[96,3712]{1,0:T(8,128)(2,1)}, bf16[48,3584]{1,0:T(8,128)(2,1)}, bf16[48,3712]{1,0:T(8,128)(2,1)}, bf16[96,3584]{1,0:T(8,128)(2,1)}, /*index=5*/bf16[96,3584]{1,0:T(8,128)(2,1)}) custom-call(s32[1]{0:T(128)} %bitcast.refs_0_, s32[2,128]{1,0:T(2,128)} %bitcast.7, bf16[2,128]{1,0:T(2,128)(2,1)} %bitcast.11, ...), custom_call_target="tpu_custom_call" | custom-call | flops 1099511627776 | bytes 1 | tf_op jit(solution)/shard_map/prep/pallas_call | solution.py:356
  8.2 1.6 collective-permute-start
  9.8 1.5 collective-permute-start.3
  11.3 0.5 collective-permute-start.4
  12.2 16.2 %collective-permute-done.3.refs_2_ = bf16[96,3584]{1,0:T(8,128)(2,1)S(1)} collective-permute-done((bf16[96,3584]{1,0:T(8,128)(2,1)}, bf16[96,3584]{1,0:T(8,128)(2,1)S(1)}, u32[]{:S(2)}, u32[]{:S(2)}) %collective-permute-start.3) | collective-permute-done | bytes 688160 | tf_op jit(solution)/shard_map/ppermute | solution.py:339
  28.4 13.0 %collective-permute-done.4.refs_3_ = bf16[96,3584]{1,0:T(8,128)(2,1)S(1)} collective-permute-done((bf16[96,3584]{1,0:T(8,128)(2,1)}, bf16[96,3584]{1,0:T(8,128)(2,1)S(1)}, u32[]{:S(2)}, u32[]{:S(2)}) %collective-permute-start.4) | collective-permute-done | bytes 688160 | tf_op jit(solution)/shard_map/ppermute | solution.py:339
  41.4 0.8 copy-done.23
  42.2 3.7 %second.1 = (bf16[96,3584]{1,0:T(8,128)(2,1)}, bf16[96,3584]{1,0:T(8,128)(2,1)}, bf16[96,3584]{1,0:T(8,128)(2,1)}, bf16[96,3584]{1,0:T(8,128)(2,1)}) custom-call(bf16[16,128]{1,0:T(8,128)(2,1)} %get-tuple-element.48.refs_0_.refs_4_.refs_7_, bf16[128,3584]{1,0:T(8,128)(2,1)} %refs_1_.1, bf16[96,3584]{1,0:T(8,128)(2,1)} %copy-done.22, ...), custom_call_target="tpu_custom_call" | custom-call | flops 1 | bytes 1 | tf_op jit(solution)/shard_map/second/pallas_call | solution.py:356
  46.3 0.6 copy-done.24
  47.1 3.4 %third.1 = (bf16[144,3712]{1,0:T(8,128)(2,1)}, bf16[48,3712]{1,0:T(8,128)(2,1)}, bf16[48,3712]{1,0:T(8,128)(2,1)}, bf16[48,3712]{1,0:T(8,128)(2,1)}) custom-call(bf16[128,3584]{1,0:T(8,128)(2,1)} %collective-permute-done.1.refs_0_, bf16[16,128]{1,0:T(8,128)(2,1)} %copy-done.24, bf16[96,3712]{1,0:T(8,128)(2,1)} %copy-done.21, ...), custom_call_target="tpu_custom_call" | custom-call | flops 1099511627776 | bytes 1 | tf_op jit(solution)/shard_map/third/pallas_call | solution.py:356
  51.0 2.5 %collective-permute-start.7 = (bf16[48,3712]{1,0:T(8,128)(2,1)}, bf16[48,3712]{1,0:T(8,128)(2,1)S(1)}, u32[]{:S(2)}, u32[]{:S(2)}) collective-permute-start(bf16[48,3712]{1,0:T(8,128)(2,1)} %get-tuple-element.56), channel_id=1, source_target_pairs={{0,3},{1,2},{2,1},{3,0},{4,7},{5,6},{6,5},{7,4},{8,11},{9,10},{10,... | collective-permute-start | bytes 1069064 | tf_op jit(solution)/shard_map/ppermute | solution.py:339
  54.5 15.7 %collective-permute-done.6.refs_1_.refs_5_ = bf16[48,3712]{1,0:T(8,128)(2,1)S(1)} collective-permute-done((bf16[48,3712]{1,0:T(8,128)(2,1)}, bf16[48,3712]{1,0:T(8,128)(2,1)S(1)}, u32[]{:S(2)}, u32[]{:S(2)}) %collective-permute-start.6) | collective-permute-done | bytes 356384 | tf_op jit(solution)/shard_map/ppermute | solution.py:339
  70.1 15.1 %collective-permute-done.7.refs_2_.refs_6_ = bf16[48,3712]{1,0:T(8,128)(2,1)S(1)} collective-permute-done((bf16[48,3712]{1,0:T(8,128)(2,1)}, bf16[48,3712]{1,0:T(8,128)(2,1)S(1)}, u32[]{:S(2)}, u32[]{:S(2)}) %collective-permute-start.7) | collective-permute-done | bytes 356384 | tf_op jit(solution)/shard_map/ppermute | solution.py:339
  85.3 1.1 copy-done.3
  86.4 1.8 collective-permute-start.10
  88.2 4.6 %gather.1 = (bf16[384,1792]{1,0:T(8,128)(2,1)}, bf16[384,1792]{1,0:T(8,128)(2,1)}, bf16[384,3584]{1,0:T(8,128)(2,1)}, f32[384,128]{1,0:T(8,128)}, bf16[8,16,128]{2,1,0:T(8,128)(2,1)}) custom-call(s32[1]{0:T(128)} %bitcast.2.refs_0_, bf16[48,3584]{1,0:T(8,128)(2,1)} %get-tuple-element.46.refs_1_, bf16[96,3712]{1,0:T(8,128)(2,1)} %copy-done.21, ...), custom_call_target="tpu_custom_call" | custom-call | flops 1 | bytes 1 | tf_op jit(solution)/shard_map/gather/pallas_call | solution.py:356
  92.8 1.6 collective-permute-start.12
  94.4 0.9 copy-done.6
  95.3 0.8 copy-done.7
  96.1 10.3 %forward.1 = (bf16[384,1024]{1,0:T(8,128)(2,1)S(1)}, f32[384,1024]{1,0:T(8,128)S(1)}, f32[384,1024]{1,0:T(8,128)S(1)}) custom-call(bf16[384,3584]{1,0:T(8,128)(2,1)} %get-tuple-element.61.refs_0_, f32[384,128]{1,0:T(8,128)S(1)} %copy-done.6, bf16[1,3584,1024]{2,1,0:T(8,128)(2,1)} %refs_3_.7, bf16[1,3584,1024]{2,1,0:T(8,128)(2,1)} %refs_4_.5, ...), custom_call_target="tpu_custom_call" | custom-call | flops 1 | bytes 1 | tf_op jit(solution)/shard_map/forward/pallas_call | solution.py:356
  106.4 1.1 copy-done
  107.6 3.6 %collective-permute-done.9.refs_0_.refs_2_ = bf16[96,3584]{1,0:T(8,128)(2,1)} collective-permute-done((bf16[96,3584]{1,0:T(8,128)(2,1)}, bf16[96,3584]{1,0:T(8,128)(2,1)}, u32[]{:S(2)}, u32[]{:S(2)}) %collective-permute-start.9) | collective-permute-done | bytes 688160 | tf_op jit(solution)/shard_map/ppermute | solution.py:339
  111.2 0.6 copy-done.11
  111.7 11.3 %back.1 = (bf16[2,384,1024]{2,1,0:T(8,128)(2,1)}, bf16[16,384]{1,0:T(8,128)(2,1)}, bf16[464,384]{1,0:T(8,128)(2,1)}) custom-call(s32[1]{0:T(128)} %bitcast.refs_0_, bf16[96,3584]{1,0:T(8,128)(2,1)} %get-tuple-element.52.refs_4_.refs_1_, bf16[96,3584]{1,0:T(8,128)(2,1)} %collective-permute-done.9.refs_0_.refs_2_, ...), custom_call_target="tpu_custom_call" | custom-call | flops 1 | bytes 1 | tf_op jit(solution)/shard_map/back/pallas_call | solution.py:356
  123.1 1.5 collective-permute-start.19
  124.6 0.7 copy-done.10
  125.3 4.7 %collective-permute-start.14 = (bf16[464,384]{1,0:T(8,128)(2,1)}, bf16[464,384]{1,0:T(8,128)(2,1)}, u32[]{:S(2)}, u32[]{:S(2)}) collective-permute-start(bf16[464,384]{1,0:T(8,128)(2,1)} %hold.3.refs_6_), channel_id=1, source_target_pairs={{0,7},{1,6},{2,5},{3,4},{4,3},{5,2},{6,1},{7,0},{8,15},{9,14},{10,... | collective-permute-start | bytes 1069064 | tf_op jit(solution)/shard_map/ppermute | solution.py:339
  130.0 6.9 %rowgrad.2 = (bf16[928,384]{1,0:T(8,128)(2,1)}, bf16[464,384]{1,0:T(8,128)(2,1)}) custom-call(s32[1]{0:T(128)} %bitcast.refs_0_, bf16[2,384,1024]{2,1,0:T(8,128)(2,1)} %get-tuple-element.67.refs_1_.refs_3_, bf16[16,384]{1,0:T(8,128)(2,1)} %get-tuple-element.68.refs_1_.refs_2_, bf16[1,3584,1024]{2,1,0:T(8,128)(2,1)} %refs_3_.7, ...), custom_call_target="tpu_custom_call" | custom-call | flops 1099511627776 | bytes 1 | tf_op jit(solution)/shard_map/rowgrad/pallas_call | solution.py:356
  136.9 1.2 collective-permute-start.18
  138.1 1.2 collective-permute-start.21
  139.4 1.0 copy-done.14
  140.4 7.0 %weights.1 = (bf16[2,896,1024]{2,1,0:T(8,128)(2,1)}, f32[8,128]{1,0:T(8,128)S(1)}) custom-call(s32[1]{0:T(128)} %bitcast.4.refs_0_, bf16[384,1792]{1,0:T(8,128)(2,1)S(1)} %copy-done.13, bf16[384,1792]{1,0:T(8,128)(2,1)} %collective-permute-done.11.refs_11_.refs_2_, bf16[2,384,1024]{2,1,0:T(8,128)(2,1)S(1)} %copy-done.12, ...), custom_call_target="tpu_custom_call" | custom-call | flops 1099511627776 | bytes 1 | tf_op jit(solution)/shard_map/weights/pallas_call | solution.py:356
  147.4 0.6 copy-done.20
  148.0 8.2 %rowgrad.3 = (bf16[464,384]{1,0:T(8,128)(2,1)}, bf16[464,384]{1,0:T(8,128)(2,1)}, bf16[464,384]{1,0:T(8,128)(2,1)}, bf16[464,384]{1,0:T(8,128)(2,1)}) custom-call(s32[1]{0:T(128)} %bitcast.refs_0_, bf16[2,384,1024]{2,1,0:T(8,128)(2,1)} %get-tuple-element.67.refs_1_.refs_3_, bf16[16,384]{1,0:T(8,128)(2,1)} %get-tuple-element.68.refs_1_.refs_2_, ...), custom_call_target="tpu_custom_call" | custom-call | flops 1099511627776 | bytes 1 | tf_op jit(solution)/shard_map/rowgrad/pallas_call | solution.py:356
  156.2 2.3 %collective-permute-start.16 = (bf16[464,384]{1,0:T(8,128)(2,1)}, bf16[464,384]{1,0:T(8,128)(2,1)}, u32[]{:S(2)}, u32[]{:S(2)}) collective-permute-start(bf16[464,384]{1,0:T(8,128)(2,1)} %get-tuple-element.73), channel_id=1, source_target_pairs={{0,5},{1,4},{2,7},{3,6},{4,1},{5,0},{6,3},{7,2},{8,13},{9,12},{10,... | collective-permute-start | bytes 1069064 | tf_op jit(solution)/shard_map/ppermute | solution.py:339
  158.5 0.6 collective-permute-start.17
  159.1 1.2 collective-permute-done.19.refs_0_.refs_3_
  160.2 1.0 copy-done.17
  161.2 1.0 copy-done.19
  162.2 2.1 %second_back.1.refs_7_ = bf16[928,384]{1,0:T(8,128)(2,1)} custom-call(bf16[928,384]{1,0:T(8,128)(2,1)} %collective-permute-done.18.refs_0_.refs_4_, bf16[464,384]{1,0:T(8,128)(2,1)S(1)} %copy-done.19, f32[8,128]{1,0:T(8,128)S(1)} %fence.3.refs_2_), custom_call_target="tpu_custom_call" | custom-call | flops 1099511627776 | bytes 1 | tf_op jit(solution)/shard_map/second_back/pallas_call | solution.py:356
  164.3 1.4 collective-permute-start.20
  165.7 3.5 %combine.3 = (bf16[448,1024]{1,0:T(8,128)(2,1)S(1)}, f32[2,16,128]{2,1,0:T(8,128)S(1)}) custom-call(s32[1]{0:T(128)} %bitcast.refs_0_, s32[2,128]{1,0:T(2,128)S(1)} %bitcast.8, bf16[8,16,128]{2,1,0:T(8,128)(2,1)S(1)} %copy-done.8, bf16[464,384]{1,0:T(8,128)(2,1)S(1)} %copy-done.18, bf16[928,384]{1,0:T(8,128)(2,1)} %collective-permute-done.18.refs_0_.refs_4_, ...), custom_call_target="tpu_custom_call" | custom-call | flops 1099511627776 | bytes 1 | tf_op jit(solution)/shard_map/combine/pallas_call | solution.py:356
  169.5 8.4 %weights_rest.1 = (bf16[1,896,1024]{2,1,0:T(8,128)(2,1)}, bf16[1,896,1024]{2,1,0:T(8,128)(2,1)}, f32[8,128]{1,0:T(8,128)S(1)}) custom-call(s32[1]{0:T(128)} %bitcast.4.refs_0_, bf16[384,1792]{1,0:T(8,128)(2,1)} %collective-permute-done.12.refs_5_.refs_1_, bf16[384,1792]{1,0:T(8,128)(2,1)} %collective-permute-done.13.refs_5_.refs_2_, ...), custom_call_target="tpu_custom_call" | custom-call | flops 1099511627776 | bytes 1 | tf_op jit(solution)/shard_map/weights_rest/pallas_call | solution.py:356
  177.8 11.8 %collective-permute-done.20.refs_3_ = bf16[928,384]{1,0:T(8,128)(2,1)} collective-permute-done((bf16[928,384]{1,0:T(8,128)(2,1)}, bf16[928,384]{1,0:T(8,128)(2,1)}, u32[]{:S(2)}, u32[]{:S(2)}) %collective-permute-start.20) | collective-permute-done | bytes 712736 | tf_op jit(solution)/shard_map/ppermute | solution.py:339
  189.7 2.3 %combine.4 = (bf16[448,1024]{1,0:T(8,128)(2,1)S(1)}, f32[2,16,128]{2,1,0:T(8,128)S(1)}) custom-call(s32[1]{0:T(128)} %bitcast.refs_0_, s32[2,128]{1,0:T(2,128)S(1)} %bitcast.9, bf16[8,16,128]{2,1,0:T(8,128)(2,1)S(1)} %copy-done.9, bf16[928,384]{1,0:T(8,128)(2,1)} %collective-permute-done.20.refs_3_, bf16[448,1024]{1,0:T(8,128)(2,1)S(1)} %get-tuple-element.78.refs_4_, ...), custom_call_target="tpu_custom_call" | custom-call | flops 1099511627776 | bytes 1 | tf_op jit(solution)/shard_map/combine/pallas_call | solution.py:356
  192.0 1.6 collective-permute-done.17.refs_4_
  193.6 3.4 %combine.5 = (bf16[448,1024]{1,0:T(8,128)(2,1)}, bf16[2,128]{1,0:T(2,128)(2,1)}) custom-call(s32[1]{0:T(128)} %bitcast.refs_0_, s32[2,128]{1,0:T(2,128)S(1)} %bitcast.10, bf16[8,16,128]{2,1,0:T(8,128)(2,1)S(1)} %copy-done.9, bf16[464,384]{1,0:T(8,128)(2,1)} %collective-permute-done.16.refs_3_, bf16[464,384]{1,0:T(8,128)(2,1)} %collective-permute-done.17.refs_4_, ...), custom_call_target="tpu_custom_call" | custom-call | flops 1099511627776 | bytes 1 | tf_op jit(solution)/shard_map/combine/pallas_call | solution.py:356
  (66 shorter events, 2.8 us)
Async XLA Ops:
  0.6 45.7 %collective-permute-start.1 = (bf16[128,3584]{1,0:T(8,128)(2,1)}, bf16[128,3584]{1,0:T(8,128)(2,1)}, u32[]{:S(2)}, u32[]{:S(2)}) collective-permute-start(bf16[128,3584]{1,0:T(8,128)(2,1)} %refs_3_.4), channel_id=1, source_target_pairs={{0,4},{1,5},{2,6},{3,7},{4,0},{5,1},{6,2},{7,3},{8,12},{9,13},{10,... | collective-permute-start | bytes 2752520 | tf_op jit(solution)/shard_map/ppermute | solution.py:339
  8.2 38.1 %collective-permute-start = (bf16[96,3712]{1,0:T(8,128)(2,1)}, bf16[96,3712]{1,0:T(8,128)(2,1)S(1)}, u32[]{:S(2)}, u32[]{:S(2)}) collective-permute-start(bf16[96,3712]{1,0:T(8,128)(2,1)} %get-tuple-element.47), channel_id=1, source_target_pairs={{0,2},{1,3},{2,0},{3,1},{4,6},{5,7},{6,4},{7,5},{8,10},{9,11},{10,... | collective-permute-start | bytes 2138120 | tf_op jit(solution)/shard_map/ppermute | solution.py:339
  9.8 18.6 %collective-permute-start.3 = (bf16[96,3584]{1,0:T(8,128)(2,1)}, bf16[96,3584]{1,0:T(8,128)(2,1)S(1)}, u32[]{:S(2)}, u32[]{:S(2)}) collective-permute-start(bf16[96,3584]{1,0:T(8,128)(2,1)} %get-tuple-element.50), channel_id=1, source_target_pairs={{0,1},{1,0},{2,3},{3,2},{4,5},{5,4},{6,7},{7,6},{8,9},{9,8},{10,11... | collective-permute-start | bytes 2064392 | tf_op jit(solution)/shard_map/ppermute | solution.py:339
  11.3 30.1 %collective-permute-start.4 = (bf16[96,3584]{1,0:T(8,128)(2,1)}, bf16[96,3584]{1,0:T(8,128)(2,1)S(1)}, u32[]{:S(2)}, u32[]{:S(2)}) collective-permute-start(bf16[96,3584]{1,0:T(8,128)(2,1)} %get-tuple-element.51), channel_id=1, source_target_pairs={{0,1},{1,0},{2,3},{3,2},{4,5},{5,4},{6,7},{7,6},{8,9},{9,8},{10,11... | collective-permute-start | bytes 2064392 | tf_op jit(solution)/shard_map/ppermute | solution.py:339
  11.8 34.4 %collective-permute-start.2 = (bf16[16,128]{1,0:T(8,128)(2,1)}, bf16[16,128]{1,0:T(8,128)(2,1)S(1)}, u32[]{:S(2)}, u32[]{:S(2)}) collective-permute-start(bf16[16,128]{1,0:T(8,128)(2,1)} %get-tuple-element.48.refs_0_.refs_4_.refs_7_), channel_id=1, source_target_pairs={{0,4},{1,5},{2,6},{3,7},{4,0},{5,1},{6,2},{7,3},{8,12},{9,13},{10,... | collective-permute-start | bytes 12296 | tf_op jit(solution)/shard_map/ppermute | solution.py:339
  28.4 13.0 %copy-start.22 = (bf16[96,3584]{1,0:T(8,128)(2,1)}, bf16[96,3584]{1,0:T(8,128)(2,1)S(1)}, u32[]{:S(2)}) copy-start(bf16[96,3584]{1,0:T(8,128)(2,1)S(1)} %collective-permute-done.3.refs_2_) | copy-start | bytes 2064388
  41.4 0.8 copy-start.23
  45.9 39.3 %collective-permute-start.8 = (bf16[96,3584]{1,0:T(8,128)(2,1)}, bf16[96,3584]{1,0:T(8,128)(2,1)}, u32[]{:S(2)}, u32[]{:S(2)}) collective-permute-start(bf16[96,3584]{1,0:T(8,128)(2,1)} %get-tuple-element.58), channel_id=1, source_target_pairs={{0,4},{1,5},{2,6},{3,7},{4,0},{5,1},{6,2},{7,3},{8,12},{9,13},{10,... | collective-permute-start | bytes 2064392 | tf_op jit(solution)/shard_map/ppermute | solution.py:339
  46.3 0.6 copy-start.24
  46.3 0.9 copy-start.21
  50.5 19.6 %collective-permute-start.6 = (bf16[48,3712]{1,0:T(8,128)(2,1)}, bf16[48,3712]{1,0:T(8,128)(2,1)S(1)}, u32[]{:S(2)}, u32[]{:S(2)}) collective-permute-start(bf16[48,3712]{1,0:T(8,128)(2,1)} %get-tuple-element.55), channel_id=1, source_target_pairs={{0,2},{1,3},{2,0},{3,1},{4,6},{5,7},{6,4},{7,5},{8,10},{9,11},{10,... | collective-permute-start | bytes 1069064 | tf_op jit(solution)/shard_map/ppermute | solution.py:339
  51.0 34.3 %collective-permute-start.7 = (bf16[48,3712]{1,0:T(8,128)(2,1)}, bf16[48,3712]{1,0:T(8,128)(2,1)S(1)}, u32[]{:S(2)}, u32[]{:S(2)}) collective-permute-start(bf16[48,3712]{1,0:T(8,128)(2,1)} %get-tuple-element.56), channel_id=1, source_target_pairs={{0,3},{1,2},{2,1},{3,0},{4,7},{5,6},{6,5},{7,4},{8,11},{9,10},{10,... | collective-permute-start | bytes 1069064 | tf_op jit(solution)/shard_map/ppermute | solution.py:339
  53.5 57.6 %collective-permute-start.9 = (bf16[96,3584]{1,0:T(8,128)(2,1)}, bf16[96,3584]{1,0:T(8,128)(2,1)}, u32[]{:S(2)}, u32[]{:S(2)}) collective-permute-start(bf16[96,3584]{1,0:T(8,128)(2,1)} %get-tuple-element.60), channel_id=1, source_target_pairs={{0,2},{1,3},{2,0},{3,1},{4,6},{5,7},{6,4},{7,5},{8,10},{9,11},{10,... | collective-permute-start | bytes 2064392 | tf_op jit(solution)/shard_map/ppermute | solution.py:339
  53.9 34.3 %collective-permute-start.5 = (bf16[144,3712]{1,0:T(8,128)(2,1)}, bf16[144,3712]{1,0:T(8,128)(2,1)}, u32[]{:S(2)}, u32[]{:S(2)}) collective-permute-start(bf16[144,3712]{1,0:T(8,128)(2,1)} %get-tuple-element.54), channel_id=1, source_target_pairs={{0,1},{1,0},{2,3},{3,2},{4,5},{5,4},{6,7},{7,6},{8,9},{9,8},{10,11... | collective-permute-start | bytes 3207176 | tf_op jit(solution)/shard_map/ppermute | solution.py:339
  70.1 16.3 %copy-start.4 = (bf16[48,3712]{1,0:T(8,128)(2,1)}, bf16[48,3712]{1,0:T(8,128)(2,1)S(1)}, u32[]{:S(2)}) copy-start(bf16[48,3712]{1,0:T(8,128)(2,1)S(1)} %collective-permute-done.6.refs_1_.refs_5_) | copy-start | bytes 1069060
  85.3 1.1 copy-start.5
  85.3 1.1 copy-start.3
  86.4 25.3 %collective-permute-start.10 = (bf16[96,3584]{1,0:T(8,128)(2,1)}, bf16[96,3584]{1,0:T(8,128)(2,1)}, u32[]{:S(2)}, u32[]{:S(2)}) collective-permute-start(bf16[96,3584]{1,0:T(8,128)(2,1)} %hold.2.refs_8_), channel_id=1, source_target_pairs={{0,6},{1,7},{2,4},{3,5},{4,2},{5,3},{6,0},{7,1},{8,14},{9,15},{10,... | collective-permute-start | bytes 2064392 | tf_op jit(solution)/shard_map/ppermute | solution.py:339
  92.8 18.9 %collective-permute-start.11 = (bf16[384,1792]{1,0:T(8,128)(2,1)}, bf16[384,1792]{1,0:T(8,128)(2,1)}, u32[]{:S(2)}, u32[]{:S(2)}) collective-permute-start(bf16[384,1792]{1,0:T(8,128)(2,1)} %get-tuple-element.66.refs_1_), channel_id=1, source_target_pairs={{0,8},{8,0},{16,24},{24,16},{1,9},{9,1},{17,25},{25,17},{2,10},{10... | collective-permute-start | bytes 4128776 | tf_op jit(solution)/shard_map/ppermute | solution.py:342
  92.8 37.2 %collective-permute-start.12 = (bf16[384,1792]{1,0:T(8,128)(2,1)}, bf16[384,1792]{1,0:T(8,128)(2,1)}, u32[]{:S(2)}, u32[]{:S(2)}) collective-permute-start(bf16[384,1792]{1,0:T(8,128)(2,1)} %get-tuple-element.69), channel_id=1, source_target_pairs={{0,16},{8,24},{16,0},{24,8},{1,17},{9,25},{17,1},{25,9},{2,18},{10... | collective-permute-start | bytes 4128776 | tf_op jit(solution)/shard_map/ppermute | solution.py:342
  94.4 0.9 copy-start.6
  95.3 0.8 copy-start.7
  106.4 1.1 copy-start
  107.6 3.6 %copy-start.1 = (f32[384,1024]{1,0:T(8,128)}, f32[384,1024]{1,0:T(8,128)S(1)}, u32[]{:S(2)}) copy-start(f32[384,1024]{1,0:T(8,128)S(1)} %get-tuple-element.65.refs_7_) | copy-start | bytes 4718596
  107.6 3.6 %copy-start.2 = (bf16[384,1024]{1,0:T(8,128)(2,1)}, bf16[384,1024]{1,0:T(8,128)(2,1)S(1)}, u32[]{:S(2)}) copy-start(bf16[384,1024]{1,0:T(8,128)(2,1)S(1)} %get-tuple-element.63.refs_1_.refs_5_) | copy-start | bytes 2359300
  111.2 0.6 copy-start.11
  123.0 16.3 %collective-permute-start.15 = (bf16[2,384,1024]{2,1,0:T(8,128)(2,1)}, bf16[2,384,1024]{2,1,0:T(8,128)(2,1)}, u32[]{:S(2)}, u32[]{:S(2)}) collective-permute-start(bf16[2,384,1024]{2,1,0:T(8,128)(2,1)} %get-tuple-element.67.refs_1_.refs_3_), channel_id=1, source_target_pairs={{0,8},{8,0},{16,24},{24,16},{1,9},{9,1},{17,25},{25,17},{2,10},{10... | collective-permute-start | bytes 4718600 | tf_op jit(solution)/shard_map/ppermute | solution.py:342
  123.1 37.1 %collective-permute-start.19 = (bf16[2,384,1024]{2,1,0:T(8,128)(2,1)}, bf16[2,384,1024]{2,1,0:T(8,128)(2,1)}, u32[]{:S(2)}, u32[]{:S(2)}) collective-permute-start(bf16[2,384,1024]{2,1,0:T(8,128)(2,1)} %get-tuple-element.67.refs_1_.refs_3_), channel_id=1, source_target_pairs={{0,16},{8,24},{16,0},{24,8},{1,17},{9,25},{17,1},{25,9},{2,18},{10... | collective-permute-start | bytes 4718600 | tf_op jit(solution)/shard_map/ppermute | solution.py:342
  124.6 0.7 copy-start.10
  125.3 22.7 %collective-permute-start.14 = (bf16[464,384]{1,0:T(8,128)(2,1)}, bf16[464,384]{1,0:T(8,128)(2,1)}, u32[]{:S(2)}, u32[]{:S(2)}) collective-permute-start(bf16[464,384]{1,0:T(8,128)(2,1)} %hold.3.refs_6_), channel_id=1, source_target_pairs={{0,7},{1,6},{2,5},{3,4},{4,3},{5,2},{6,1},{7,0},{8,15},{9,14},{10,... | collective-permute-start | bytes 1069064 | tf_op jit(solution)/shard_map/ppermute | solution.py:339
  130.0 9.3 %copy-start.12 = (bf16[2,384,1024]{2,1,0:T(8,128)(2,1)S(1)}, bf16[2,384,1024]{2,1,0:T(8,128)(2,1)}, u32[]{:S(2)}) copy-start(bf16[2,384,1024]{2,1,0:T(8,128)(2,1)} %get-tuple-element.67.refs_1_.refs_3_) | copy-start | bytes 4718596
  130.0 9.3 %copy-start.13 = (bf16[384,1792]{1,0:T(8,128)(2,1)S(1)}, bf16[384,1792]{1,0:T(8,128)(2,1)}, u32[]{:S(2)}) copy-start(bf16[384,1792]{1,0:T(8,128)(2,1)} %get-tuple-element.66.refs_1_) | copy-start | bytes 4128772
  136.9 24.3 %collective-permute-start.18 = (bf16[928,384]{1,0:T(8,128)(2,1)}, bf16[928,384]{1,0:T(8,128)(2,1)}, u32[]{:S(2)}, u32[]{:S(2)}) collective-permute-start(bf16[928,384]{1,0:T(8,128)(2,1)} %get-tuple-element.75), channel_id=1, source_target_pairs={{0,2},{1,3},{2,0},{3,1},{4,6},{5,7},{6,4},{7,5},{8,10},{9,11},{10,... | collective-permute-start | bytes 2138120 | tf_op jit(solution)/shard_map/ppermute | solution.py:339
  138.1 27.6 %collective-permute-start.21 = (bf16[464,384]{1,0:T(8,128)(2,1)}, bf16[464,384]{1,0:T(8,128)(2,1)}, u32[]{:S(2)}, u32[]{:S(2)}) collective-permute-start(bf16[464,384]{1,0:T(8,128)(2,1)} %get-tuple-element.71.refs_5_), channel_id=1, source_target_pairs={{0,6},{1,7},{2,4},{3,5},{4,2},{5,3},{6,0},{7,1},{8,14},{9,15},{10,... | collective-permute-start | bytes 1069064 | tf_op jit(solution)/shard_map/ppermute | solution.py:339
  139.3 8.6 %collective-permute-start.13 = (bf16[384,1792]{1,0:T(8,128)(2,1)}, bf16[384,1792]{1,0:T(8,128)(2,1)}, u32[]{:S(2)}, u32[]{:S(2)}) collective-permute-start(bf16[384,1792]{1,0:T(8,128)(2,1)} %collective-permute-done.12.refs_5_.refs_1_), channel_id=1, source_target_pairs={{0,8},{8,0},{16,24},{24,16},{1,9},{9,1},{17,25},{25,17},{2,10},{10... | collective-permute-start | bytes 4128776 | tf_op jit(solution)/shard_map/ppermute | solution.py:342
  139.4 1.0 copy-start.14
  147.4 0.6 copy-start.20
  156.2 35.8 %collective-permute-start.16 = (bf16[464,384]{1,0:T(8,128)(2,1)}, bf16[464,384]{1,0:T(8,128)(2,1)}, u32[]{:S(2)}, u32[]{:S(2)}) collective-permute-start(bf16[464,384]{1,0:T(8,128)(2,1)} %get-tuple-element.73), channel_id=1, source_target_pairs={{0,5},{1,4},{2,7},{3,6},{4,1},{5,0},{6,3},{7,2},{8,13},{9,12},{10,... | collective-permute-start | bytes 1069064 | tf_op jit(solution)/shard_map/ppermute | solution.py:339
  158.5 35.1 %collective-permute-start.17 = (bf16[464,384]{1,0:T(8,128)(2,1)}, bf16[464,384]{1,0:T(8,128)(2,1)}, u32[]{:S(2)}, u32[]{:S(2)}) collective-permute-start(bf16[464,384]{1,0:T(8,128)(2,1)} %get-tuple-element.74), channel_id=1, source_target_pairs={{0,4},{1,5},{2,6},{3,7},{4,0},{5,1},{6,2},{7,3},{8,12},{9,13},{10,... | collective-permute-start | bytes 1069064 | tf_op jit(solution)/shard_map/ppermute | solution.py:339
  160.2 1.0 copy-start.17
  161.2 1.0 copy-start.19
  162.2 3.5 %copy-start.8 = (bf16[8,16,128]{2,1,0:T(8,128)(2,1)S(1)}, bf16[8,16,128]{2,1,0:T(8,128)(2,1)}, u32[]{:S(2)}) copy-start(bf16[8,16,128]{2,1,0:T(8,128)(2,1)} %get-tuple-element.59.refs_4_.refs_2_) | copy-start | bytes 98308
  162.2 3.5 %copy-start.15 = (s32[128,2]{0,1:T(2,128)S(1)}, s32[128,2]{0,1:T(2,128)}, u32[]{:S(2)}) copy-start(s32[128,2]{0,1:T(2,128)} %param.10) | copy-start | bytes 3076
  162.2 3.5 %copy-start.18 = (bf16[464,384]{1,0:T(8,128)(2,1)S(1)}, bf16[464,384]{1,0:T(8,128)(2,1)}, u32[]{:S(2)}) copy-start(bf16[464,384]{1,0:T(8,128)(2,1)} %get-tuple-element.77.refs_1_.refs_3_) | copy-start | bytes 1069060
  164.3 25.4 %collective-permute-start.20 = (bf16[928,384]{1,0:T(8,128)(2,1)}, bf16[928,384]{1,0:T(8,128)(2,1)}, u32[]{:S(2)}, u32[]{:S(2)}) collective-permute-start(bf16[928,384]{1,0:T(8,128)(2,1)} %second_back.1.refs_7_), channel_id=1, source_target_pairs={{0,1},{1,0},{2,3},{3,2},{4,5},{5,4},{6,7},{7,6},{8,9},{9,8},{10,11... | collective-permute-start | bytes 2138120 | tf_op jit(solution)/shard_map/ppermute | solution.py:339
  165.7 3.8 %collective-permute-start.22 = (bf16[2,384,1024]{2,1,0:T(8,128)(2,1)}, bf16[2,384,1024]{2,1,0:T(8,128)(2,1)}, u32[]{:S(2)}, u32[]{:S(2)}) collective-permute-start(bf16[2,384,1024]{2,1,0:T(8,128)(2,1)} %collective-permute-done.19.refs_0_.refs_3_), channel_id=1, source_target_pairs={{0,8},{8,0},{16,24},{24,16},{1,9},{9,1},{17,25},{25,17},{2,10},{10... | collective-permute-start | bytes 4718600 | tf_op jit(solution)/shard_map/ppermute | solution.py:342
  169.4 20.2 %copy-start.9 = (bf16[8,16,128]{2,1,0:T(8,128)(2,1)S(1)}, bf16[8,16,128]{2,1,0:T(8,128)(2,1)}, u32[]{:S(2)}) copy-start(bf16[8,16,128]{2,1,0:T(8,128)(2,1)} %get-tuple-element.59.refs_4_.refs_2_) | copy-start | bytes 98308
  169.4 20.2 %copy-start.16 = (s32[128,2]{0,1:T(2,128)S(1)}, s32[128,2]{0,1:T(2,128)}, u32[]{:S(2)}) copy-start(s32[128,2]{0,1:T(2,128)} %param.10) | copy-start | bytes 3076
